TPU v7x, 32 devices: a whole 2x2x4 slice. The times are simulated.
32 devices in a mesh: dp: 4 (over y, x), seq: 8 (over z, core).
Axes of the slice: x: 2, y: 2, z: 4, core: 2. Of those that a mesh axis runs over, the one named last changes fastest.
Arguments:
- conv_input: bfloat16 [4096, 5376], P(('dp', 'seq')), may hold values from -6 to 6
- doc_start: int32 [4096], P(('dp', 'seq')), may hold values 0 or 1
- conv_weight: float32 [4, 5376], replicated, may hold values from -3 to 3
- conv_bias: float32 [5376], replicated, may hold values from -0.5 to 0.5
- dt_raw: float32 [4096, 80], P(('dp', 'seq')), may hold values from -3 to 3
- dt_bias: float32 [80], replicated, may hold values from -5.5 to -4.2
- a_log: float32 [80], replicated, may hold values from -9 to 2, as said below
- skip_gain: float32 [80], replicated, may hold values from 0.5 to 1.5
- cotangent: bfloat16 [4096, 5120], P(('dp', 'seq')), may hold values from -6 to 6
Outputs:
- ssm_output: bfloat16 [4096, 5120], P(('dp', 'seq'))
- grad_input: bfloat16 [4096, 5376], P(('dp', 'seq'))
- grad_conv_weight: float32 [4, 5376], replicated
- grad_conv_bias: float32 [5376], replicated
- grad_dt_bias: float32 [80], replicated
- grad_a_log: float32 [80], replicated
- grad_skip_gain: float32 [80], replicated
Inputs may be any that keep to these rules, and one draw needn't show every extreme that they name: `doc_start`: 1 marks the first token of a document; documents may cross shard boundaries. One value per head; exp(a_log) lies between 25 / 1024 and 4.2, so that the per-token decay rates exp(a_log) * steps_dt run from under 1 / 1024 to about 1.1.
All inputs are finite; a program needn't handle non-finite values.
Results may differ from a plain program's by a relative error of at most 0.00115.
Values may be sent and summed in bfloat16 or wider, within the bound.
No kernel may reach another device: no remote copies, remote signals or barrier semaphores. Data moves between devices by JAX's collectives and lax.ppermute only.
A program may use at most 320 MiB of HBM per device.

v0:
```python
import functools

import jax
import jax.numpy as jnp
from jax import lax
from jax.experimental import pallas as pl
from jax.experimental.pallas import tpu as pltpu
from jax.sharding import PartitionSpec as P

HEADS = 80
HEAD_DIM = 64
STATE = 128
CONV = 4
INNER = 5120
CH = 5376

STREAMS = 2
TURNS = 2
PIECES = STREAMS * TURNS
PIECE_HEADS = HEADS // PIECES
WIDTH = PIECE_HEADS * HEAD_DIM
SPAN = STREAMS * WIDTH
PAIR = 2 * HEAD_DIM
CHUNK = 256
BC = 2 * STATE
BC_AT = INNER // BC
FAR = -1e30
CODE = 32766.0
PER = CHUNK // HEAD_DIM

F32 = jnp.float32
BF16 = jnp.bfloat16
I16 = jnp.int16
EXACT = lax.Precision.HIGHEST
ACROSS = ((1,), (1,))
ANY = pl.BlockSpec(memory_space=pl.ANY)
HBM = pl.BlockSpec(memory_space=pltpu.HBM)
SMEM = pl.BlockSpec(memory_space=pltpu.SMEM)
VMEM_LIMIT = 24 * 1024 * 1024

MASK, ENTRY, LEAVE, PULL, RATE, DECAY, RUN, FAR_AT, ROW, SMASK = range(0, 1280, 128)
SKIP = ROW + HEADS
TABLE = SMASK + 136


def iota(shape, dim):
    return lax.broadcasted_iota(jnp.int32, shape, dim)


def mm(a, b, contract=((1,), (0,))):
    return lax.dot_general(a, b, (contract, ((), ())), preferred_element_type=F32)


def halves(value):
    high = value.astype(BF16)
    return high, (value - high.astype(F32)).astype(BF16)


def lanes(*parts):
    return jnp.concatenate(parts, axis=1)


def rows(*parts):
    return jnp.concatenate(parts, axis=0)


def by_head(table, first, count):
    out = []
    for head in range(first, first + count, 2):
        shape = (table.shape[0], PAIR)
        left = jnp.broadcast_to(table[:, head : head + 1], shape)
        right = jnp.broadcast_to(table[:, head + 1 : head + 2], shape)
        out.append(jnp.where(iota(shape, 1) < HEAD_DIM, left, right))
    return lanes(*out)


def taps_of(ext_ref, cols, count, mask):
    taps = []
    for tap in range(CONV):
        back = CONV - 1 - tap
        value = ext_ref[8 - back : 8 - back + count, cols]
        taps.append(value if back == 0 else value * mask[back])
    return taps


def columns(table, width):
    shape = (table.shape[0], width)
    return [jnp.broadcast_to(table[:, i : i + 1], shape) for i in range(CONV)]


def activate(taps, cols, w_ref, b_ref):
    v = b_ref[:, cols] + w_ref[CONV - 1 : CONV, cols] * taps[CONV - 1]
    for tap in range(CONV - 2, -1, -1):
        v = v + w_ref[tap : tap + 1, cols] * taps[tap]
    gate = 1.0 / (1.0 + jnp.exp(-v))
    return v * gate, gate * (1.0 + v * (1.0 - gate))


class Flow:
    def __init__(self, sems):
        self.sems = sems
        self.used = 0

    def copy(self, source, target):
        made = pltpu.make_async_copy(source, target, self.sems.at[self.used])
        self.used += 1
        return made


def at(first, width=CHUNK):
    return slice(first, first + width)


def tail_kernel(x_ref, doc_ref, out_ref):
    count = doc_ref.shape[1]
    edge = x_ref.shape[0] - CONV + 1
    cut = jnp.zeros((1, 1), F32)
    for back in range(CONV - 1):
        row = edge + CONV - 2 - back
        if back:
            cut = cut + doc_ref[:, count - back : count - back + 1].astype(F32)
        keep = (cut == 0.0).astype(F32)
        value = x_ref[row : row + 1, :].astype(F32) * keep
        out_ref[CONV - 2 - back : CONV - 1 - back, :] = value.astype(BF16)


def edge_kernel(gin_ref, misc_ref, back_ref, doc_ref, out_ref):
    count = doc_ref.shape[1]
    size = gin_ref.shape[0]
    cut = jnp.zeros((1, 1), F32)
    keeps = []
    for back in range(CONV - 1):
        if back:
            cut = cut + doc_ref[:, count - back : count - back + 1].astype(F32)
        keeps.insert(0, (cut == 0.0).astype(F32))
    place = iota((8, 1), 0)
    value = misc_ref[...]
    for i in range(CONV - 1):
        row = 8 - CONV + 1 + i
        value = value + jnp.where(place == row, back_ref[i : i + 1, :] * keeps[i], 0.0)
    out_ref[...] = gin_ref[...]
    out_ref[size - 8 :, :] = value.astype(BF16)


def prep_kernel(doc_ref, raw_ref, dtb_ref, alog_ref, skip_ref, tab_ref):
    count = raw_ref.shape[0]
    resets = doc_ref[...].astype(F32)
    t, s = iota((count, count), 0), iota((count, count), 1)

    def total(keep, shape):
        return jnp.sum(jnp.where(keep, jnp.broadcast_to(resets, shape), 0.0), axis=1, keepdims=True)

    square = (count, count)
    lane = iota((count, 128), 1)
    table = jnp.ones((count, 128), F32)
    for back in range(1, CONV):
        fits = (total((s <= t) & (s > t - back), square) == 0.0).astype(F32)
        table = jnp.where(lane == back, fits, table)
    tab_ref[MASK : MASK + count, :] = table
    wide = (count + 8, count)
    at, s_wide = iota(wide, 0) - 8, iota(wide, 1)
    lane, place = iota((count + 8, 128), 1), iota((count + 8, 128), 0) - 8
    table = jnp.zeros((count + 8, 128), F32)
    for ahead in range(CONV):
        fits = (total((s_wide > at) & (s_wide <= at + ahead), wide) == 0.0).astype(F32)
        fits = jnp.where((place + ahead >= 0) & (place + ahead < count), fits, 0.0)
        table = jnp.where(lane == ahead, fits, table)
    tab_ref[SMASK : SMASK + count + 8, :] = table
    segment = total(s <= t, square)
    reset_col = total(s == t, square)
    segment_row = jnp.sum(
        jnp.where(t <= s, jnp.broadcast_to(reset_col, square), 0.0), axis=0, keepdims=True
    )
    causal = (s <= t) & (segment == segment_row)
    tab_ref[FAR_AT : FAR_AT + count, :] = jnp.where(causal, 0.0, FAR)
    v = raw_ref[...] + dtb_ref[...]
    dt = jnp.maximum(v, 0.0) + jnp.log1p(jnp.exp(-jnp.abs(v)))
    rate = -jnp.exp(alog_ref[...])
    decay = rate * dt
    run = jnp.dot((s <= t).astype(F32), decay, precision=EXACT, preferred_element_type=F32)
    end = run[count - 1 : count, :]
    last = segment == segment[count - 1 : count, :]
    gate = 1.0 / (1.0 + jnp.exp(-v))
    fill = jnp.zeros((count, 128 - HEADS), F32)

    def put(where, value):
        tab_ref[where : where + count, :] = lanes(value, fill)

    put(ENTRY, jnp.where(segment == 0.0, jnp.exp(run), 0.0))
    put(LEAVE, jnp.where(last, jnp.exp(end - run) * dt, 0.0))
    put(PULL, gate / dt)
    put(RATE, rate * gate)
    put(DECAY, decay)
    put(RUN, run)
    tab_ref[ROW : ROW + 128, :] = lanes(jnp.log(dt) - run, fill).T
    tab_ref[SKIP : SKIP + 1, :] = lanes(skip_ref[...], fill[:1])


def scores_of(act):
    keys, reads = act[:, :STATE], act[:, STATE:]
    return lax.dot_general(
        reads, keys, (ACROSS, ((), ())), precision=EXACT, preferred_element_type=F32
    )


def local_kernel(turn, flag_ref, x_ref, halo_ref, w_ref, b_ref, cot_ref, tab_ref, *refs):
    lead = turn == 0
    refs = list(refs)
    if lead:
        bch_ref, bcw_ref, bcb_ref = refs[:3]
        refs = refs[3:]
    else:
        turned_ref = refs.pop(0)
    act_ref, slope_ref = refs[:2]
    send_refs, mine_refs = refs[2 : 2 + STREAMS], refs[2 + STREAMS : 2 + 2 * STREAMS]
    if lead:
        bca_ref, bcs_ref, turned_ref, scores_ref = refs[2 + 2 * STREAMS : 6 + 2 * STREAMS]
    xb, cb, ab, sb, nb, mb, ext_ref, bx, in_sems, out_sems = refs[-10:]
    count = xb.shape[0]
    come, go = Flow(in_sems), Flow(out_sems)
    if lead:
        first = come.copy(x_ref.at[:, at(INNER, BC)], bx)
        first.start()
    arriving, leaving = [], []
    for stream in range(STREAMS):
        cols, whole_cols = at(stream * WIDTH, WIDTH), at(turn * SPAN + stream * WIDTH, WIDTH)
        pair = (
            come.copy(x_ref.at[:, whole_cols], xb.at[:, cols]),
            come.copy(cot_ref.at[:, whole_cols], cb.at[:, cols]),
        )
        for copy in pair:
            copy.start()
        arriving.append(pair)
    mask = columns(tab_ref[MASK : MASK + count, :], CHUNK)

    def load(cols, source, halo):
        ext_ref[8 : 8 + count, cols] = source.astype(F32)
        ext_ref[8 - CONV + 1 : 8, cols] = halo.astype(F32)
        return taps_of(ext_ref, cols, count, mask)

    if lead:
        first.wait()
        act, slope = activate(load(at(SPAN, BC), bx[...], bch_ref[...]), at(0), bcw_ref, bcb_ref)
        bca_ref[...] = act
        bcs_ref[...] = slope
        turned = rows(act[:, :STATE].T, act[:, STATE:].T)
        turned_ref[...] = turned
        scores_ref[...] = scores_of(act)
    else:
        turned = turned_ref[...]
    keys, reads = halves(turned[:STATE, :]), halves(turned[STATE:, :])
    keys_both, reads_both = lanes(*keys), lanes(*reads)
    entry, leave = tab_ref[ENTRY : ENTRY + count, :], tab_ref[LEAVE : LEAVE + count, :]
    first_core = flag_ref[0] == 0
    for stream in range(STREAMS):
        for copy in arriving[stream]:
            copy.wait()
        for start in range(stream * WIDTH, (stream + 1) * WIDTH, CHUNK):
            cols = at(start)
            head = (turn * SPAN + start) // HEAD_DIM
            taps = load(cols, xb[:, cols], halo_ref[:, cols])
            act, slope = activate(taps, cols, w_ref, b_ref)
            ab[:, cols] = act
            sb[:, cols] = slope
            e = by_head(entry, head, PER)
            lx_high, lx_low = halves(act * by_head(leave, head, PER))
            ey_high, ey_low = halves(cb[:, cols].astype(F32) * e)
            state = mm(keys_both, rows(lx_high, lx_high)) + mm(keys[0], lx_low)
            adjoint = mm(reads_both, rows(ey_high, ey_high)) + mm(reads[0], ey_low)
            nb[:STATE, cols] = jnp.where(first_core, state, adjoint)
            mb[:, cols] = jnp.where(first_core, adjoint, state)
            nb[STATE:, cols] = jnp.broadcast_to(e[count - 1 : count, :], (8, CHUNK))
        cols = at(stream * WIDTH, WIDTH)
        targets = (send_refs[stream], mine_refs[stream], act_ref.at[:, cols], slope_ref.at[:, cols])
        for source, target in zip((nb, mb, ab, sb), targets):
            copy = go.copy(source.at[:, cols], target)
            copy.start()
            leaving.append(copy)
    for copy in leaving:
        copy.wait()


def decode(codes):
    scale = jnp.exp2(codes[STATE : STATE + 1, :].astype(F32) * (1.0 / 256.0)) * (1.0 / CODE)
    return codes[:STATE, :].astype(F32) * scale


def encode(value):
    most = jnp.max(jnp.abs(value), axis=0, keepdims=True)
    power = jnp.ceil(jnp.log2(jnp.maximum(most, 1e-30)) * 256.0)
    scale = jnp.exp2(power * (1.0 / 256.0)) * (1.0 / CODE)
    codes = jnp.floor(value * (1.0 / scale) + 0.5).astype(jnp.int32)
    tail = jnp.broadcast_to(power.astype(jnp.int32), (16, value.shape[1]))
    return rows(codes, tail).astype(I16)


def chip_kernel(lead, mine_ref, met_ref, own_ref, *refs):
    chip_ref = refs[0]
    mb, eb, ob, sem = refs[-4:]
    come = Flow(sem)
    copies = [
        come.copy(mine_ref, mb),
        come.copy(met_ref, eb),
        come.copy(own_ref.at[pl.ds(STATE, 8), :], ob),
    ]
    for copy in copies:
        copy.start()
    for copy in copies:
        copy.wait()
    for start in range(0, WIDTH, CHUNK):
        cols = at(start)
        own = ob[0:1, cols]
        value = mb[:, cols] + own * eb[:STATE, cols]
        chip_ref[:STATE, cols] = value
        chip_ref[STATE:, cols] = own * eb[STATE:, cols]
        if lead:
            refs[1][:, cols] = encode(value)


def hop_kernel(pick_ref, previous_ref, *refs):
    chip_refs, out_ref = refs[:-1], refs[-1]
    for start in range(0, WIDTH, CHUNK):
        cols = at(start)
        chip = chip_refs[0][:, cols]
        for i, ref in enumerate(chip_refs[1:]):
            chip = jnp.where(pick_ref[0] > i, ref[:, cols], chip)
        before = jnp.where(pick_ref[1] == 0, 0.0, decode(previous_ref[:, cols]))
        out_ref[:, cols] = encode(chip[:STATE, :] + chip[STATE : STATE + 1, :] * before)


def within_kernel(piece, act_ref, cot_ref, tab_ref, scores_ref, y_ref, dx_ref, dscores_ref, *refs):
    ab, cb, yb, db, in_sems, out_sems = refs
    count = ab.shape[0]
    come, go = Flow(in_sems), Flow(out_sems)
    base = (piece % STREAMS) * WIDTH
    copies = (
        come.copy(act_ref.at[:, at(base, WIDTH)], ab),
        come.copy(cot_ref.at[:, at(piece * WIDTH, WIDTH)], cb),
    )
    for copy in copies:
        copy.start()
    for copy in copies:
        copy.wait()
    run = tab_ref[RUN : RUN + count, :]
    far, scores = tab_ref[FAR_AT : FAR_AT + count, :], scores_ref[...]
    left = iota((count, PAIR), 1) < HEAD_DIM
    total = jnp.zeros((count, count), F32)
    zero = jnp.zeros((count, PAIR), BF16)
    for pair in range(PIECE_HEADS // 2):
        cols = at(pair * PAIR, PAIR)
        x_high, x_low = halves(ab[:, cols])
        upstream = cb[:, cols]
        upstream_turned = upstream.astype(F32).T.astype(BF16)
        spread, weights = [], []
        for side in range(2):
            head = piece * PIECE_HEADS + 2 * pair + side
            row = tab_ref[ROW + head : ROW + head + 1, :]
            within = jnp.exp(run[:, head : head + 1] + row + far)
            spread.append(within)
            weights.append(lanes(*halves(within * scores)))
        out = mm(rows(*weights), rows(lanes(x_high, x_low), lanes(x_high, zero)))
        out = out[:, :PAIR] + out[:, PAIR:]
        yb[:, cols] = jnp.where(left, out[:count], out[count:])
        parts = []
        for side in range(2):
            mine = upstream_turned[side * HEAD_DIM : (side + 1) * HEAD_DIM, :]
            pushed = rows(weights[side][:, :count], weights[side][:, count:])
            parts.append(mm(lanes(mine, mine), pushed))
        db[:, cols] = rows(*parts).T
        up_left, up_right = jnp.where(left, upstream, zero), jnp.where(left, zero, upstream)
        lhs = rows(lanes(up_left, up_left), lanes(up_right, up_right))
        products = mm(lhs, lanes(x_high, x_low), ACROSS)
        total = total + spread[0] * products[:count] + spread[1] * products[count:]
    copies = (go.copy(yb, y_ref), go.copy(db, dx_ref))
    for copy in copies:
        copy.start()
    dscores_ref[...] = total
    for copy in copies:
        copy.wait()


def conv_back(dconv, taps, w, z_ref, z_cols, smask):
    count, width = dconv.shape
    z_ref[8 : 8 + count, z_cols] = dconv
    grad = jnp.zeros((count + 8, width), F32)
    for ahead in range(CONV):
        tap = CONV - 1 - ahead
        shifted = z_ref[ahead : ahead + count + 8, z_cols]
        grad = grad + w[tap : tap + 1, :] * (shifted * smask[ahead])
    sums = [jnp.sum(dconv * tap, axis=0, keepdims=True) for tap in taps]
    sums.append(jnp.sum(dconv, axis=0, keepdims=True))
    sums.append(jnp.zeros((3, width), F32))
    return grad[8:].astype(BF16), rows(grad[:8], grad[count:], *sums)


def clear_edges(z_ref, count):
    z_ref[0:8, :] = jnp.zeros((8, z_ref.shape[1]), F32)
    z_ref[8 + count : 16 + count, :] = jnp.zeros((8, z_ref.shape[1]), F32)


def finish_kernel(piece, hops, flag_ref, *refs):
    incs, exchs = refs[:hops], refs[hops : 2 * hops]
    refs = refs[2 * hops :]
    met_ref, act_ref, slope_ref, y_ref, dx_ref, cot_ref, x_ref, halo_ref, w_ref, tab_ref, bc_ref = refs[:11]
    out_ref, gin_ref, misc_ref, dreads_ref, dkeys_ref, scal_ref = refs[-22:-16]
    ib, hb, eb, ab, sb, yb, db, cb, xb, ob, gb, nb, ext_ref, z_ref, in_sems, out_sems = refs[-16:]
    count = xb.shape[0]
    come, go = Flow(in_sems), Flow(out_sems)
    within, base = (piece % STREAMS) * WIDTH, piece * WIDTH
    place = flag_ref[1]
    choices = []
    for here, sources, buffer in ((place, incs, ib), (hops - place, exchs, hb)):
        sem = come.used
        come.used += 1
        for i, source in enumerate(sources):
            choices.append((here == i + 1, pltpu.make_async_copy(source, buffer, come.sems.at[sem])))

        @pl.when(here == 0)
        def _():
            buffer[...] = jnp.zeros(buffer.shape, I16)

    for chosen, copy in choices:
        pl.when(chosen)(copy.start)
    arriving, leaving = [], []
    for start, width in ((0, CHUNK), (CHUNK, WIDTH - CHUNK)):
        cols = at(start, width)
        stream_cols, whole_cols = at(within + start, width), at(base + start, width)
        group = [
            come.copy(met_ref.at[:, cols], eb.at[:, cols]),
            come.copy(act_ref.at[:, stream_cols], ab.at[:, cols]),
            come.copy(slope_ref.at[:, stream_cols], sb.at[:, cols]),
            come.copy(y_ref.at[:, cols], yb.at[:, cols]),
            come.copy(dx_ref.at[:, cols], db.at[:, cols]),
            come.copy(cot_ref.at[:, whole_cols], cb.at[:, cols]),
            come.copy(x_ref.at[:, whole_cols], xb.at[:, cols]),
        ]
        for copy in group:
            copy.start()
        arriving.append(group)
    clear_edges(z_ref, count)
    keys, reads = halves(bc_ref[:, :STATE]), halves(bc_ref[:, STATE:])
    keys_both, reads_both = lanes(*keys), lanes(*reads)
    entry, leave = tab_ref[ENTRY : ENTRY + count, :], tab_ref[LEAVE : LEAVE + count, :]
    skip = tab_ref[SKIP : SKIP + 1, :]
    first_core = flag_ref[0] == 0
    mask = columns(tab_ref[MASK : MASK + count, :], CHUNK)
    smask = columns(tab_ref[SMASK : SMASK + count + 8, :], CHUNK)
    dreads = jnp.zeros((count, STATE), F32)
    dkeys = jnp.zeros((count, STATE), F32)
    sums = jnp.zeros((4 * count + 16, 128), F32)
    for chosen, copy in choices:
        pl.when(chosen)(copy.wait)
    for start in range(0, WIDTH, CHUNK):
        cols, whole_cols = at(start), at(base + start)
        head = (base + start) // HEAD_DIM
        if start <= CHUNK:
            for copy in arriving[start // CHUNK]:
                copy.wait()
        inc, exch = decode(ib[:, cols]), decode(hb[:, cols])
        mine = eb[STATE : STATE + 1, cols] * inc + eb[:STATE, cols]
        state = jnp.where(first_core, exch, mine)
        adjoint = jnp.where(first_core, mine, exch)
        s_high, s_low = halves(state)
        a_high, a_low = halves(adjoint)
        e, leaves = by_head(entry, head, PER), by_head(leave, head, PER)
        act, up = ab[:, cols], cb[:, cols].astype(F32)
        carried = mm(reads_both, rows(s_high, s_high)) + mm(reads[0], s_low)
        y = yb[:, cols] + e * carried
        back = mm(keys_both, rows(a_high, a_high)) + mm(keys[0], a_low)
        back = leaves * back
        dx = db[:, cols] + back
        gain = by_head(skip, head, PER)
        ob[:, cols] = (y + gain * act).astype(BF16)
        ey_high, ey_low = halves(up * e)
        lx_high, lx_low = halves(act * leaves)
        dreads = dreads + mm(lanes(ey_high, ey_high, ey_low), lanes(s_high, s_low, s_high), ACROSS)
        dkeys = dkeys + mm(lanes(lx_high, lx_high, lx_low), lanes(a_high, a_low, a_high), ACROSS)
        through = e[count - 1 : count, :]
        end = jnp.sum(act * back, axis=0, keepdims=True)
        end = end + through * jnp.sum(state * adjoint, axis=0, keepdims=True)
        direct = jnp.sum(up * act, axis=0, keepdims=True)
        received = act * dx
        small = halves(rows(end, direct, jnp.zeros((6, CHUNK), F32)))
        stack = halves(up * y - received) + halves(received)
        pick = (iota((CHUNK, 128), 1) == head + iota((CHUNK, 128), 0) // HEAD_DIM).astype(BF16)
        sums = sums + mm(rows(*stack, rows(*small)), pick)
        dconv = (dx + gain * up) * sb[:, cols]
        ext_ref[8 : 8 + count, cols] = xb[:, cols].astype(F32)
        ext_ref[8 - CONV + 1 : 8, cols] = halo_ref[:, whole_cols].astype(F32)
        taps = taps_of(ext_ref, cols, count, mask)
        gb[:, cols], nb[:, cols] = conv_back(dconv, taps, w_ref[:, whole_cols], z_ref, cols, smask)
    for source, target in ((ob, out_ref), (gb, gin_ref), (nb, misc_ref)):
        copy = go.copy(source, target.at[:, at(base, WIDTH)])
        copy.start()
        leaving.append(copy)
    dreads_ref[...] = dreads
    dkeys_ref[...] = dkeys
    drun = sums[:count] + sums[count : 2 * count]
    received = sums[2 * count : 3 * count] + sums[3 * count : 4 * count]
    small = sums[4 * count : 4 * count + 8] + sums[4 * count + 8 :]
    drun = drun + jnp.where(iota((count, 128), 0) == count - 1, small[0:1, :], 0.0)
    later = (iota((count, count), 1) >= iota((count, count), 0)).astype(F32)
    ddecay = jnp.dot(later, drun, precision=EXACT, preferred_element_type=F32)
    pull, rate = tab_ref[PULL : PULL + count, :], tab_ref[RATE : RATE + count, :]
    ddtb = jnp.sum(received * pull + ddecay * rate, axis=0, keepdims=True)
    dalog = jnp.sum(ddecay * tab_ref[DECAY : DECAY + count, :], axis=0, keepdims=True)
    scal_ref[...] = rows(ddtb, dalog, small[1:2, :], jnp.zeros((5, 128), F32))
    for copy in leaving:
        copy.wait()


def final_kernel(x_ref, halo_ref, w_ref, tab_ref, bc_ref, slope_ref, *refs):
    gin_ref, misc_ref, ext_ref, z_ref = refs[-4:]
    parts = refs[: 4 * PIECES]
    count = x_ref.shape[0]
    ext_ref[8 : 8 + count, :] = x_ref[...].astype(F32)
    ext_ref[8 - CONV + 1 : 8, :] = halo_ref[...].astype(F32)
    clear_edges(z_ref, count)
    total = []
    for kind in range(4):
        value = parts[kind * PIECES][...]
        for piece in range(1, PIECES):
            value = value + parts[kind * PIECES + piece][...]
        total.append(value)
    dreads, dkeys, dscores, scal = total
    keys, reads = bc_ref[:, :STATE], bc_ref[:, STATE:]
    dreads = dreads + jnp.dot(dscores, keys, precision=EXACT, preferred_element_type=F32)
    dkeys = dkeys + jnp.dot(dscores.T, reads, precision=EXACT, preferred_element_type=F32)
    cols = slice(0, BC)
    dconv = lanes(dkeys, dreads) * slope_ref[...]
    taps = taps_of(ext_ref, cols, count, columns(tab_ref[MASK : MASK + count, :], BC))
    smask = columns(tab_ref[SMASK : SMASK + count + 8, :], BC)
    gin_ref[...], misc = conv_back(dconv, taps, w_ref[...], z_ref, cols, smask)
    misc_ref[...] = misc
    misc_ref[16 + CONV + 1 : 24, :128] = scal[:3, :]


def cost(us):
    return pl.CostEstimate(flops=int(us * 1.1e9), bytes_accessed=1000, transcendentals=0)


def whole(shape):
    return pl.BlockSpec(shape, lambda *_: (0,) * len(shape))


def part(shape, *index):
    return pl.BlockSpec(shape, lambda *_: index)


def full(*arrays):
    return [whole(a.shape) for a in arrays]


def call(kernel, ins, specs, outs, out_specs, scratch=(), aliases=None, us=1.0):
    return pl.pallas_call(
        kernel,
        grid=(1,),
        in_specs=specs,
        out_specs=out_specs,
        out_shape=[jax.ShapeDtypeStruct(shape, dtype) for shape, dtype in outs],
        scratch_shapes=list(scratch),
        input_output_aliases=aliases or {},
        compiler_params=pltpu.CompilerParams(vmem_limit_bytes=VMEM_LIMIT),
        cost_estimate=cost(us),
    )(*ins)


def vmem(rows_, cols, dtype=F32):
    return pltpu.VMEM((rows_, cols), dtype)


def sems(count):
    return pltpu.SemaphoreType.DMA((count,))


def permute(value, axis, target):
    size = lax.axis_size(axis)
    return lax.ppermute(value, axis, [(i, target(i)) for i in range(size)])


def other_core(value):
    return permute(value, "seq", lambda i: i ^ 1)


def along(size):
    def target(i):
        if i % 2 == 1:
            return i + 2 if i + 2 < size else i - 1
        return i - 2 if i >= 2 else i + 1

    return target


def xor_sum(value, axis, low):
    size = lax.axis_size(axis)
    bit = low
    while bit < size:
        if 2 * bit < size:
            one = permute(value, axis, lambda i: i ^ bit)
            two = permute(value, axis, lambda i: i ^ (2 * bit))
            three = permute(value, axis, lambda i: i ^ (3 * bit))
            value = (value + one) + (two + three)
            bit *= 4
        else:
            value = value + permute(value, axis, lambda i: i ^ bit)
            bit *= 2
    return value


def chip_of(lead, mine, met, own):
    state = (STATE + 8, WIDTH)
    payload = (STATE + 16, WIDTH)
    outs = [(state, F32)] + [(payload, I16)] * lead
    return call(
        functools.partial(chip_kernel, lead),
        (mine, met, own),
        [HBM] * 3,
        outs,
        [whole(s) for s, _ in outs],
        [vmem(STATE, WIDTH), vmem(*state), vmem(8, WIDTH), sems(3)],
        us=1.5,
    )


def hop(pick, previous, chips):
    payload = (STATE + 16, WIDTH)
    return call(
        hop_kernel,
        (pick, previous, *chips),
        [SMEM, *full(previous, *chips)],
        [(payload, I16)],
        [whole(payload)],
        us=0.8,
    )[0]


def on_device(
    conv_input, doc_start, conv_weight, conv_bias, dt_raw, dt_bias, a_log, skip_gain, cotangent
):
    count = conv_input.shape[0]
    size = lax.axis_size("seq")
    index = lax.axis_index("seq")
    core = lax.rem(index, 2)
    chip = lax.div(index, 2)
    hops = size // 2 - 1
    place = jnp.where(core == 1, chip, hops - chip)
    flag = jnp.stack([core, place]).astype(jnp.int32)
    docs = doc_start[None, :]
    edge = part((16, CH), count // 16 - 1, 0)

    tail_out = call(
        tail_kernel, (conv_input, docs), [edge, whole(docs.shape)],
        [((CONV - 1, CH), BF16)], [whole((CONV - 1, CH))],
    )[0]
    halo = lax.ppermute(tail_out, "seq", [(i, i + 1) for i in range(size - 1)])

    bias = conv_bias[None, :]
    prep_in = (docs, dt_raw, dt_bias[None, :], a_log[None, :], skip_gain[None, :])
    table = (TABLE, 128)
    tab = call(prep_kernel, prep_in, full(*prep_in), [(table, F32)], [whole(table)])[0]

    square = (count, count)
    payload = (STATE + 16, WIDTH)
    shape = (count, WIDTH)
    acts, slopes, chips, sent = [], [], [], []
    mets = []
    given = tab
    for turn in range(TURNS):
        lead = turn == 0
        here = [part((height, SPAN), 0, turn) for height in (CONV - 1, CONV, 1)]
        ins = [flag, conv_input, halo, conv_weight, bias, cotangent, given]
        specs = [SMEM, HBM, *here, HBM, whole(table)]
        outs = [(count, SPAN)] * 2 + [(STATE + 8, WIDTH)] * STREAMS + [(STATE, WIDTH)] * STREAMS
        out_specs = [HBM] * len(outs)
        if lead:
            ins += [halo, conv_weight, bias]
            specs += [part((height, BC), 0, BC_AT) for height in (CONV - 1, CONV, 1)]
            bc_out = [(count, BC), (count, BC), (BC, count), square]
            outs += bc_out
            out_specs += [whole(s) for s in bc_out]
        else:
            ins.append(turned)
            specs.append(whole(turned.shape))
        got = call(
            functools.partial(local_kernel, turn),
            ins,
            specs,
            [(s, F32) for s in outs],
            out_specs,
            [
                vmem(count, SPAN, BF16), vmem(count, SPAN, BF16), vmem(count, SPAN),
                vmem(count, SPAN), vmem(STATE + 8, SPAN), vmem(STATE, SPAN),
                vmem(count + 8, SPAN + BC), vmem(count, BC, BF16),
                sems(2 * STREAMS + 1), sems(4 * STREAMS),
            ],
            us=5.0,
        )
        act, slope, *got = got
        if lead:
            bc_act, bc_slope, turned, scores = got[2 * STREAMS :]
        acts.append(act)
        slopes.append(slope)
        for stream in range(STREAMS):
            send, mine = got[stream], got[STREAMS + stream]
            met = other_core(send)
            mets.append(met)
            chip, *first = chip_of(lead, mine, met, send)
            chips.append(chip)
            sent += first
        if lead:
            given, *sent = lax.optimization_barrier((given, *sent))

    received = [[] for _ in range(STREAMS)]
    swapped = [[] for _ in range(STREAMS)]
    for turn in range(TURNS + hops - 1):
        if turn:
            piece = jnp.clip(turn - place, 0, TURNS - 1)
            pick = jnp.stack([piece, place]).astype(jnp.int32)
            sent = [
                hop(pick, received[stream][-1], chips[stream::STREAMS]) for stream in range(STREAMS)
            ]
        for stream in range(STREAMS):
            got = permute(sent[stream], "seq", along(size))
            received[stream].append(got)
            swapped[stream].append(other_core(got))

    withins = []
    for j in range(PIECES):
        ins = (acts[j // STREAMS], cotangent, tab, scores)
        withins.append(
            call(
                functools.partial(within_kernel, j),
                ins,
                [HBM, HBM, *full(tab, scores)],
                [(shape, F32), (shape, F32), (square, F32)],
                [HBM, HBM, whole(square)],
                [vmem(*shape), vmem(*shape, BF16), vmem(*shape), vmem(*shape), sems(2), sems(2)],
                us=3.0,
            )
        )

    shared = None
    dreads, dkeys, scals = [None] * PIECES, [None] * PIECES, [None] * PIECES
    shared_out = [((count, INNER), BF16), ((count, CH), BF16), ((24, CH), F32)]
    small_out = [((count, STATE), F32), ((count, STATE), F32), ((8, 128), F32)]
    for j in range(PIECES):
        turn, stream = j // STREAMS, j % STREAMS
        y, dx, _ = withins[j]
        ins = [flag, *received[stream][turn : turn + hops], *swapped[stream][turn : turn + hops]]
        specs = [SMEM] + [ANY] * (2 * hops)
        ins += [mets[j], acts[turn], slopes[turn], y, dx, cotangent, conv_input]
        specs += [HBM] * 7 + full(halo, conv_weight, tab, bc_act)
        ins += [halo, conv_weight, tab, bc_act]
        aliases = None
        if shared is not None:
            aliases = {len(ins) + i: i for i in range(3)}
            ins += shared
            specs += [HBM] * 3
        *shared, dreads[j], dkeys[j], scals[j] = call(
            functools.partial(finish_kernel, j, hops),
            ins,
            specs,
            shared_out + small_out,
            [HBM] * 3 + [whole(s) for s, _ in small_out],
            [
                vmem(*payload, I16), vmem(*payload, I16), vmem(STATE + 8, WIDTH),
                vmem(*shape), vmem(*shape), vmem(*shape), vmem(*shape), vmem(*shape, BF16),
                vmem(*shape, BF16), vmem(*shape, BF16), vmem(*shape, BF16), vmem(24, WIDTH),
                vmem(count + 8, WIDTH), vmem(count + 16, WIDTH), sems(2 + 14), sems(3),
            ],
            aliases,
            us=5.0,
        )
    output, gin, misc = shared

    dscores = [group[2] for group in withins]
    small = (tab, bc_act, bc_slope, *dreads, *dkeys, *dscores, *scals)
    ins = (conv_input, halo, conv_weight) + small + (gin, misc)
    bc_common = [part((count, BC), 0, BC_AT), part((CONV - 1, BC), 0, BC_AT), part((CONV, BC), 0, BC_AT)]
    gin, misc = call(
        final_kernel,
        ins,
        bc_common + full(*small) + [ANY] * 2,
        shared_out[1:],
        [part((count, BC), 0, BC_AT), part((24, BC), 0, BC_AT)],
        [vmem(count + 8, BC), vmem(count + 16, BC)],
        {len(ins) - 2: 0, len(ins) - 1: 1},
    )

    returned = lax.ppermute(
        misc[8 - CONV + 1 : 8], "seq", [(i, i - 1) for i in range(1, size)]
    )
    grad_input = call(
        edge_kernel,
        (gin, misc, returned, docs),
        [edge, part((8, CH), 1, 0), *full(returned, docs)],
        [((count, CH), BF16)],
        [edge],
        aliases={0: 0},
    )[0]

    half = CH // 2
    lower, upper = misc[16:24, :half], misc[16:24, half:]
    first = core == 0
    value = jnp.where(first, lower, upper)
    value = value + other_core(jnp.where(first, upper, lower))
    value = xor_sum(value, "dp", 1)
    value = xor_sum(value, "seq", 2)
    value = value * float(lax.axis_size("dp") * size * count) ** (-0.5)
    other = other_core(value)
    lower = jnp.where(first, value, other)
    upper = jnp.where(first, other, value)
    summed = jnp.concatenate([lower, upper], axis=1)
    scal = summed[CONV + 1 :, INNER : INNER + HEADS]
    return (output, grad_input, summed[:CONV], summed[CONV], scal[0], scal[1], scal[2])


def solution(mesh):
    return jax.shard_map(
        on_device,
        mesh=mesh,
        in_specs=(
            P(("dp", "seq"), None),
            P(("dp", "seq")),
            P(),
            P(),
            P(("dp", "seq"), None),
            P(),
            P(),
            P(),
            P(("dp", "seq"), None),
        ),
        out_specs=(P(("dp", "seq"), None), P(("dp", "seq"), None), P(), P(), P(), P(), P()),
        check_vma=False,
    )
```

profile of v0, /device:TPU:1, one launch (start us, length us, event | category | flops | bytes accessed | tf_op | source)
XLA Modules:
  0.0 115.4 jit_solution(12909556809487388877)
XLA Ops:
  0.6 1.3 %copy-done = bf16[128,5376]{1,0:T(8,128)(2,1)S(1)} copy-done((bf16[128,5376]{1,0:T(8,128)(2,1)S(1)}, bf16[128,5376]{1,0:T(8,128)(2,1)}, u32[]{:S(2)}) %copy-start) | copy-done | bytes 1376280
  2.8 4.6 %collective-permute-start = (bf16[3,5376]{1,0:T(4,128)(2,1)S(1)}, bf16[3,5376]{1,0:T(4,128)(2,1)S(1)}, u32[]{:S(2)}, u32[]{:S(2)}) collective-permute-start(bf16[3,5376]{1,0:T(4,128)(2,1)S(1)} %shard_map.145), channel_id=1, source_target_pairs={{0,1},{1,2},{2,3},{3,4},{4,5},{5,6},{6,7},{8,9},{9,10},{10,11},{11... | collective-permute-start | bytes 96776 | tf_op jit(solution)/shard_map/ppermute | solution.py:655
  9.4 4.3 %shard_map.146 = (f32[128,2560]{1,0:T(8,128)S(1)}, f32[128,2560]{1,0:T(8,128)S(1)}, f32[136,1280]{1,0:T(8,128)S(1)}, f32[136,1280]{1,0:T(8,128)S(1)}, f32[128,12...) custom-call(s32[2]{0:T(128)S(1)} %pad_add_fusion.flag_ref, ...), custom_call_target="tpu_custom_call" | custom-call | flops 5500000256 | bytes 1000 | tf_op jit(solution)/shard_map/pallas_call | solution.py:555
  13.8 1.0 copy-done.27
  14.8 1.1 copy-done.29
  16.4 1.6 %collective-permute-done.1.met_ref.refs_6_ = f32[136,1280]{1,0:T(8,128)S(1)} collective-permute-done((f32[136,1280]{1,0:T(8,128)S(1)}, f32[136,1280]{1,0:T(8,128)S(1)}, u32[]{:S(2)}, u32[]{:S(2)}) %collective-permute-start.1) | collective-permute-done | bytes 696352 | tf_op jit(solution)/shard_map/ppermute | solution.py:578
  22.3 4.5 %shard_map.149 = (f32[128,2560]{1,0:T(8,128)S(1)}, f32[128,2560]{1,0:T(8,128)S(1)}, f32[136,1280]{1,0:T(8,128)}, f32[136,1280]{1,0:T(8,128)}, f32[128,1280]{1,0:T(8,128)S(1)}, /*index=5*/f32[128,1280]{1,0:T(8,128)S(1)}) custom-call(s32[2]{0:T(128)S(1)} %pad_add_fusion.flag_ref, bf16[128,5376]{1,0:T(8,128)(2,1)S(1)} %copy-done.1, ...), custom_call_target="tpu_custom_call" | custom-call | flops 5500000256 | bytes 1000 | tf_op jit(solution)/shard_map/pallas_call | solution.py:555
  26.8 0.9 copy-done.19
  28.6 1.1 copy-done.23
  29.6 1.1 copy-done.25
  31.3 1.3 %collective-permute-start.3 = (s16[144,1280]{1,0:T(8,128)(2,1)}, s16[144,1280]{1,0:T(8,128)(2,1)S(1)}, u32[]{:S(2)}, u32[]{:S(2)}) collective-permute-start(s16[144,1280]{1,0:T(8,128)(2,1)} %copy-done.9), channel_id=1, source_target_pairs={{0,1},{1,3},{2,0},{3,5},{4,2},{5,7},{6,4},{7,6},{8,9},{9,11},{10,8... | collective-permute-start | bytes 1105928 | tf_op jit(solution)/shard_map/ppermute | solution.py:578
  32.8 1.3 %collective-permute-start.11 = (s16[144,1280]{1,0:T(8,128)(2,1)S(1)}, s16[144,1280]{1,0:T(8,128)(2,1)S(1)}, u32[]{:S(2)}, u32[]{:S(2)}) collective-permute-start(s16[144,1280]{1,0:T(8,128)(2,1)S(1)} %get-tuple-element.86), channel_id=1, source_target_pairs={{0,1},{1,3},{2,0},{3,5},{4,2},{5,7},{6,4},{7,6},{8,9},{9,11},{10,8... | collective-permute-start | bytes 1105928 | tf_op jit(solution)/shard_map/ppermute | solution.py:578
  34.1 1.1 copy-done.22
  35.2 1.3 %shard_map.150.refs_1_ = f32[136,1280]{1,0:T(8,128)S(1)} custom-call(f32[128,1280]{1,0:T(8,128)S(1)} %copy-done.22, f32[136,1280]{1,0:T(8,128)S(1)} %collective-permute-done.4.met_ref.refs_6_, f32[136,1280]{1,0:T(8,128)} %get-tuple-element.79.own_ref), custom_call_target="tpu_custom_call" | custom-call | flops 1650000000 | bytes 1000 | tf_op jit(solution)/shard_map/pallas_call | solution.py:555
  36.5 0.9 collective-permute-done.3.previous_ref.refs_0_
  37.4 0.9 shard_map.151
  38.3 2.1 %collective-permute-start.5 = (s16[144,1280]{1,0:T(8,128)(2,1)S(1)}, s16[144,1280]{1,0:T(8,128)(2,1)S(1)}, u32[]{:S(2)}, u32[]{:S(2)}) collective-permute-start(s16[144,1280]{1,0:T(8,128)(2,1)S(1)} %shard_map.151), channel_id=1, source_target_pairs={{0,1},{1,3},{2,0},{3,5},{4,2},{5,7},{6,4},{7,6},{8,9},{9,11},{10,8... | collective-permute-start | bytes 1105928 | tf_op jit(solution)/shard_map/ppermute | solution.py:578
  40.4 1.4 %shard_map.155.refs_1_ = f32[136,1280]{1,0:T(8,128)S(1)} custom-call(f32[128,1280]{1,0:T(8,128)S(1)} %copy-done.20, f32[136,1280]{1,0:T(8,128)} %collective-permute-done.12.met_ref.refs_6_, f32[136,1280]{1,0:T(8,128)} %get-tuple-element.89.own_ref), custom_call_target="tpu_custom_call" | custom-call | flops 1650000000 | bytes 1000 | tf_op jit(solution)/shard_map/pallas_call | solution.py:555
  41.9 0.9 shard_map.156
  42.8 1.6 %collective-permute-start.13 = (s16[144,1280]{1,0:T(8,128)(2,1)S(1)}, s16[144,1280]{1,0:T(8,128)(2,1)S(1)}, u32[]{:S(2)}, u32[]{:S(2)}) collective-permute-start(s16[144,1280]{1,0:T(8,128)(2,1)S(1)} %shard_map.156), channel_id=1, source_target_pairs={{0,1},{1,3},{2,0},{3,5},{4,2},{5,7},{6,4},{7,6},{8,9},{9,11},{10,8... | collective-permute-start | bytes 1105928 | tf_op jit(solution)/shard_map/ppermute | solution.py:578
  44.4 1.9 %shard_map.161 = (f32[128,1280]{1,0:T(8,128)S(1)}, f32[128,1280]{1,0:T(8,128)S(1)}, f32[128,128]{1,0:T(8,128)S(1)}) custom-call(f32[128,2560]{1,0:T(8,128)S(1)} %copy-done.28, bf16[128,5120]{1,0:T(8,128)(2,1)S(1)} %copy-done.4, f32[1288,128]{1,0:T(8,128)S(1)} %shard_map.144.tab_ref.refs_15_, f32[128,128]{1,0:T(8,128)S(1)} %copy-done.32), custom_call_target="tpu_custom_call" | custom-call | flops 3300000000 | bytes 1000 | tf_op jit(solution)/shard_map/pallas_call | solution.py:555
  46.3 0.9 shard_map.152
  47.2 1.3 %collective-permute-start.6 = (s16[144,1280]{1,0:T(8,128)(2,1)S(1)}, s16[144,1280]{1,0:T(8,128)(2,1)S(1)}, u32[]{:S(2)}, u32[]{:S(2)}) collective-permute-start(s16[144,1280]{1,0:T(8,128)(2,1)S(1)} %shard_map.152), channel_id=1, source_target_pairs={{0,1},{1,3},{2,0},{3,5},{4,2},{5,7},{6,4},{7,6},{8,9},{9,11},{10,8... | collective-permute-start | bytes 1105928 | tf_op jit(solution)/shard_map/ppermute | solution.py:578
  49.1 0.9 shard_map.157
  50.1 2.2 %collective-permute-start.14 = (s16[144,1280]{1,0:T(8,128)(2,1)S(1)}, s16[144,1280]{1,0:T(8,128)(2,1)S(1)}, u32[]{:S(2)}, u32[]{:S(2)}) collective-permute-start(s16[144,1280]{1,0:T(8,128)(2,1)S(1)} %shard_map.157), channel_id=1, source_target_pairs={{0,1},{1,3},{2,0},{3,5},{4,2},{5,7},{6,4},{7,6},{8,9},{9,11},{10,8... | collective-permute-start | bytes 1105928 | tf_op jit(solution)/shard_map/ppermute | solution.py:578
  52.3 2.1 %shard_map.160 = (f32[128,1280]{1,0:T(8,128)S(1)}, f32[128,1280]{1,0:T(8,128)S(1)}, f32[128,128]{1,0:T(8,128)S(1)}) custom-call(f32[128,2560]{1,0:T(8,128)S(1)} %copy-done.28, bf16[128,5120]{1,0:T(8,128)(2,1)S(1)} %copy-done.4, f32[1288,128]{1,0:T(8,128)S(1)} %shard_map.144.tab_ref.refs_15_, f32[128,128]{1,0:T(8,128)S(1)} %copy-done.32), custom_call_target="tpu_custom_call" | custom-call | flops 3300000000 | bytes 1000 | tf_op jit(solution)/shard_map/pallas_call | solution.py:555
  54.9 0.9 shard_map.153
  55.9 1.6 %collective-permute-start.7 = (s16[144,1280]{1,0:T(8,128)(2,1)S(1)}, s16[144,1280]{1,0:T(8,128)(2,1)S(1)}, u32[]{:S(2)}, u32[]{:S(2)}) collective-permute-start(s16[144,1280]{1,0:T(8,128)(2,1)S(1)} %shard_map.153), channel_id=1, source_target_pairs={{0,1},{1,3},{2,0},{3,5},{4,2},{5,7},{6,4},{7,6},{8,9},{9,11},{10,8... | collective-permute-start | bytes 1105928 | tf_op jit(solution)/shard_map/ppermute | solution.py:578
  57.4 0.9 shard_map.158
  58.3 1.8 %collective-permute-start.15 = (s16[144,1280]{1,0:T(8,128)(2,1)S(1)}, s16[144,1280]{1,0:T(8,128)(2,1)S(1)}, u32[]{:S(2)}, u32[]{:S(2)}) collective-permute-start(s16[144,1280]{1,0:T(8,128)(2,1)S(1)} %shard_map.158), channel_id=1, source_target_pairs={{0,1},{1,3},{2,0},{3,5},{4,2},{5,7},{6,4},{7,6},{8,9},{9,11},{10,8... | collective-permute-start | bytes 1105928 | tf_op jit(solution)/shard_map/ppermute | solution.py:578
  61.0 1.9 %shard_map.159 = (f32[128,1280]{1,0:T(8,128)S(1)}, f32[128,1280]{1,0:T(8,128)S(1)}, f32[128,128]{1,0:T(8,128)S(1)}) custom-call(f32[128,2560]{1,0:T(8,128)S(1)} %copy-done.24, bf16[128,5120]{1,0:T(8,128)(2,1)S(1)} %copy-done.4, f32[1288,128]{1,0:T(8,128)S(1)} %shard_map.144.tab_ref.refs_15_, f32[128,128]{1,0:T(8,128)S(1)} %copy-done.32), custom_call_target="tpu_custom_call" | custom-call | flops 3300000000 | bytes 1000 | tf_op jit(solution)/shard_map/pallas_call | solution.py:555
  63.0 1.9 %shard_map.154 = (f32[128,1280]{1,0:T(8,128)S(1)}, f32[128,1280]{1,0:T(8,128)S(1)}, f32[128,128]{1,0:T(8,128)S(1)}) custom-call(f32[128,2560]{1,0:T(8,128)S(1)} %copy-done.24, bf16[128,5120]{1,0:T(8,128)(2,1)S(1)} %copy-done.4, f32[1288,128]{1,0:T(8,128)S(1)} %shard_map.144.tab_ref.refs_15_, f32[128,128]{1,0:T(8,128)S(1)} %copy-done.32), custom_call_target="tpu_custom_call" | custom-call | flops 3300000000 | bytes 1000 | tf_op jit(solution)/shard_map/pallas_call | solution.py:555
  65.8 2.6 %collective-permute-start.10 = (s16[144,1280]{1,0:T(8,128)(2,1)S(1)}, s16[144,1280]{1,0:T(8,128)(2,1)S(1)}, u32[]{:S(2)}, u32[]{:S(2)}) collective-permute-start(s16[144,1280]{1,0:T(8,128)(2,1)S(1)} %collective-permute-done.7.refs_2_), channel_id=1, source_target_pairs={{0,1},{1,0},{2,3},{3,2},{4,5},{5,4},{6,7},{7,6},{8,9},{9,8},{10,11... | collective-permute-start | bytes 1105928 | tf_op jit(solution)/shard_map/ppermute | solution.py:578
  68.5 5.2 %shard_map.162 = (bf16[128,5120]{1,0:T(8,128)(2,1)}, bf16[128,5376]{1,0:T(8,128)(2,1)}, f32[24,5376]{1,0:T(8,128)S(1)}, f32[128,128]{1,0:T(8,128)S(1)}, f32[128,128]{1,0:T(8,128)S(1)}, /*index=5*/f32[8,128]{1,0:T(8,128)S(1)}) custom-call(s32[2]{0:T(128)S(1)} %pad_add_fusion.flag_ref, s16[144,1280]{1,0:T(8,128)(2,1)S(1)} %collective-permute-done.11.previous_ref.refs_0_, ...), custom_call_target="tpu_custom_call" | custom-call | flops 5500000256 | bytes 1000 | tf_op jit(solution)/shard_map/pallas_call | solution.py:555
  73.7 5.1 %shard_map.163 = (bf16[128,5120]{1,0:T(8,128)(2,1)}, bf16[128,5376]{1,0:T(8,128)(2,1)}, f32[24,5376]{1,0:T(8,128)S(1)}, f32[128,128]{1,0:T(8,128)S(1)}, f32[128,128]{1,0:T(8,128)S(1)}, /*index=5*/f32[8,128]{1,0:T(8,128)S(1)}) custom-call(s32[2]{0:T(128)S(1)} %pad_add_fusion.flag_ref, ...), custom_call_target="tpu_custom_call", output_to_operand_aliasing={{0}: (18, {}), {1}: (19, {}), {2}: (20, {})} | custom-call | flops 5500000256 | bytes 1000 | tf_op jit(solution)/shard_map/pallas_call | solution.py:555
  78.9 5.7 %shard_map.164 = (bf16[128,5120]{1,0:T(8,128)(2,1)}, bf16[128,5376]{1,0:T(8,128)(2,1)}, f32[24,5376]{1,0:T(8,128)S(1)}, f32[128,128]{1,0:T(8,128)S(1)}, f32[128,128]{1,0:T(8,128)S(1)}, /*index=5*/f32[8,128]{1,0:T(8,128)S(1)}) custom-call(s32[2]{0:T(128)S(1)} %pad_add_fusion.flag_ref, ...), custom_call_target="tpu_custom_call", output_to_operand_aliasing={{0}: (18, {}), {1}: (19, {}), {2}: (20, {})} | custom-call | flops 5500000256 | bytes 1000 | tf_op jit(solution)/shard_map/pallas_call | solution.py:555
  84.6 5.1 %shard_map.165 = (bf16[128,5120]{1,0:T(8,128)(2,1)}, bf16[128,5376]{1,0:T(8,128)(2,1)}, f32[24,5376]{1,0:T(8,128)S(1)}, f32[128,128]{1,0:T(8,128)S(1)}, f32[128,128]{1,0:T(8,128)S(1)}, /*index=5*/f32[8,128]{1,0:T(8,128)S(1)}) custom-call(s32[2]{0:T(128)S(1)} %pad_add_fusion.flag_ref, ...), custom_call_target="tpu_custom_call", output_to_operand_aliasing={{0}: (18, {}), {1}: (19, {}), {2}: (20, {})} | custom-call | flops 5500000256 | bytes 1000 | tf_op jit(solution)/shard_map/pallas_call | solution.py:555
  89.8 1.0 shard_map.166
  91.4 0.9 collective-permute-done.22
  92.3 2.2 %collective-permute-start.25 = (f32[8,2688]{1,0:T(8,128)S(1)}, f32[8,2688]{1,0:T(8,128)S(1)}, u32[]{:S(2)}, u32[]{:S(2)}) collective-permute-start(f32[8,2688]{1,0:T(8,128)S(1)} %select_add_fusion), channel_id=1, source_target_pairs={{0,24},{8,16},{16,8},{24,0},{1,25},{9,17},{17,9},{25,1},{2,26},{10... | collective-permute-start | bytes 258056 | tf_op jit(solution)/shard_map/ppermute | solution.py:578
  95.0 2.0 %collective-permute-done.25 = f32[8,2688]{1,0:T(8,128)S(1)} collective-permute-done((f32[8,2688]{1,0:T(8,128)S(1)}, f32[8,2688]{1,0:T(8,128)S(1)}, u32[]{:S(2)}, u32[]{:S(2)}) %collective-permute-start.25) | collective-permute-done | bytes 86048 | tf_op jit(solution)/shard_map/ppermute | solution.py:578
  97.1 2.1 %collective-permute-done.24 = f32[8,2688]{1,0:T(8,128)S(1)} collective-permute-done((f32[8,2688]{1,0:T(8,128)S(1)}, f32[8,2688]{1,0:T(8,128)S(1)}, u32[]{:S(2)}, u32[]{:S(2)}) %collective-permute-start.24) | collective-permute-done | bytes 86048 | tf_op jit(solution)/shard_map/ppermute | solution.py:578
  99.2 2.1 %collective-permute-start.28 = (f32[8,2688]{1,0:T(8,128)S(1)}, f32[8,2688]{1,0:T(8,128)S(1)}, u32[]{:S(2)}, u32[]{:S(2)}) collective-permute-start(f32[8,2688]{1,0:T(8,128)S(1)} %add_add_fusion), channel_id=1, source_target_pairs={{0,6},{1,7},{2,4},{3,5},{4,2},{5,3},{6,0},{7,1},{8,14},{9,15},{10,... | collective-permute-start | bytes 258056 | tf_op jit(solution)/shard_map/ppermute | solution.py:578
  101.2 1.3 %collective-permute-start.27 = (f32[8,2688]{1,0:T(8,128)S(1)}, f32[8,2688]{1,0:T(8,128)S(1)}, u32[]{:S(2)}, u32[]{:S(2)}) collective-permute-start(f32[8,2688]{1,0:T(8,128)S(1)} %add_add_fusion), channel_id=1, source_target_pairs={{0,4},{1,5},{2,6},{3,7},{4,0},{5,1},{6,2},{7,3},{8,12},{9,13},{10,... | collective-permute-start | bytes 258056 | tf_op jit(solution)/shard_map/ppermute | solution.py:578
  102.8 3.8 %collective-permute-start.21 = (f32[3,5376]{1,0:T(4,128)S(1)}, f32[3,5376]{1,0:T(4,128)S(1)}, u32[]{:S(2)}, u32[]{:S(2)}) collective-permute-start(f32[3,5376]{1,0:T(4,128)S(1)} %slice.28), channel_id=1, source_target_pairs={{1,0},{2,1},{3,2},{4,3},{5,4},{6,5},{7,6},{9,8},{10,9},{11,10},{12... | collective-permute-start | bytes 193544 | tf_op jit(solution)/shard_map/ppermute | solution.py:790
  106.6 3.9 %collective-permute-done.27 = f32[8,2688]{1,0:T(8,128)S(1)} collective-permute-done((f32[8,2688]{1,0:T(8,128)S(1)}, f32[8,2688]{1,0:T(8,128)S(1)}, u32[]{:S(2)}, u32[]{:S(2)}) %collective-permute-start.27) | collective-permute-done | bytes 86048 | tf_op jit(solution)/shard_map/ppermute | solution.py:578
  110.5 1.2 %collective-permute-start.29 = (f32[8,2688]{1,0:T(8,128)S(1)}, f32[8,2688]{1,0:T(8,128)S(1)}, u32[]{:S(2)}, u32[]{:S(2)}) collective-permute-start(f32[8,2688]{1,0:T(8,128)S(1)} %add_multiply_fusion), channel_id=1, source_target_pairs={{0,1},{1,0},{2,3},{3,2},{4,5},{5,4},{6,7},{7,6},{8,9},{9,8},{10,11... | collective-permute-start | bytes 258056 | tf_op jit(solution)/shard_map/ppermute | solution.py:578
  111.7 1.8 %shard_map.167 = bf16[128,5376]{1,0:T(8,128)(2,1)} custom-call(bf16[128,5376]{1,0:T(8,128)(2,1)} %get-tuple-element.127.gin_ref, f32[24,5376]{1,0:T(8,128)S(1)} %get-tuple-element.128.misc_ref, f32[3,5376]{1,0:T(4,128)S(1)} %collective-permute-done.21.back_ref, s32[1,128]{1,0:T(1,128)S(1)} %bitcast.20), custom_call_target="tpu_custom_call", output_to_operand_aliasing={{}: (0, {})} | custom-call | flops 1100000000 | bytes 1000 | tf_op jit(solution)/shard_map/pallas_call | solution.py:555
  (121 shorter events, 15.4 us)
Async XLA Ops:
  2.6 4.8 %copy-start.33 = (f32[128,80]{0,1:T(8,128)S(1)}, f32[128,80]{0,1:T(8,128)}, u32[]{:S(2)}) copy-start(f32[128,80]{0,1:T(8,128)} %param.13) | copy-start | bytes 122884
  2.6 5.0 %copy-start.10 = (f32[80]{0:T(128)S(1)}, f32[80]{0:T(128)}, u32[]{:S(2)}) copy-start(f32[80]{0:T(128)} %param.14) | copy-start | bytes 964
  2.6 5.0 %copy-start.11 = (f32[80]{0:T(128)S(1)}, f32[80]{0:T(128)}, u32[]{:S(2)}) copy-start(f32[80]{0:T(128)} %param.15) | copy-start | bytes 964
  2.6 5.0 %copy-start.12 = (f32[80]{0:T(128)S(1)}, f32[80]{0:T(128)}, u32[]{:S(2)}) copy-start(f32[80]{0:T(128)} %param.16) | copy-start | bytes 964
  2.8 5.7 %collective-permute-start = (bf16[3,5376]{1,0:T(4,128)(2,1)S(1)}, bf16[3,5376]{1,0:T(4,128)(2,1)S(1)}, u32[]{:S(2)}, u32[]{:S(2)}) collective-permute-start(bf16[3,5376]{1,0:T(4,128)(2,1)S(1)} %shard_map.145), channel_id=1, source_target_pairs={{0,1},{1,2},{2,3},{3,4},{4,5},{5,6},{6,7},{8,9},{9,10},{10,11},{11... | collective-permute-start | bytes 96776 | tf_op jit(solution)/shard_map/ppermute | solution.py:655
  7.6 1.7 %copy-start.3 = (bf16[128,5120]{1,0:T(8,128)(2,1)S(1)}, bf16[128,5120]{1,0:T(8,128)(2,1)}, u32[]{:S(2)}) copy-start(bf16[128,5120]{1,0:T(8,128)(2,1)} %refs_11_.7) | copy-start | bytes 3932164
  15.9 2.9 %copy-start.31 = (f32[128,128]{1,0:T(8,128)}, f32[128,128]{1,0:T(8,128)S(1)}, u32[]{:S(2)}) copy-start(f32[128,128]{1,0:T(8,128)S(1)} %get-tuple-element.82.scores_ref) | copy-start | bytes 196612
  15.9 2.2 %collective-permute-start.1 = (f32[136,1280]{1,0:T(8,128)S(1)}, f32[136,1280]{1,0:T(8,128)S(1)}, u32[]{:S(2)}, u32[]{:S(2)}) collective-permute-start(f32[136,1280]{1,0:T(8,128)S(1)} %get-tuple-element.69.own_ref), channel_id=1, source_target_pairs={{0,1},{1,0},{2,3},{3,2},{4,5},{5,4},{6,7},{7,6},{8,9},{9,8},{10,11... | collective-permute-start | bytes 2088968 | tf_op jit(solution)/shard_map/ppermute | solution.py:578
  15.9 3.9 %collective-permute-start.2 = (f32[136,1280]{1,0:T(8,128)S(1)}, f32[136,1280]{1,0:T(8,128)S(1)}, u32[]{:S(2)}, u32[]{:S(2)}) collective-permute-start(f32[136,1280]{1,0:T(8,128)S(1)} %get-tuple-element.72.own_ref), channel_id=1, source_target_pairs={{0,1},{1,0},{2,3},{3,2},{4,5},{5,4},{6,7},{7,6},{8,9},{9,8},{10,11... | collective-permute-start | bytes 2088968 | tf_op jit(solution)/shard_map/ppermute | solution.py:578
  30.7 3.3 %collective-permute-start.4 = (f32[136,1280]{1,0:T(8,128)}, f32[136,1280]{1,0:T(8,128)S(1)}, u32[]{:S(2)}, u32[]{:S(2)}) collective-permute-start(f32[136,1280]{1,0:T(8,128)} %get-tuple-element.79.own_ref), channel_id=1, source_target_pairs={{0,1},{1,0},{2,3},{3,2},{4,5},{5,4},{6,7},{7,6},{8,9},{9,8},{10,11... | collective-permute-start | bytes 2088968 | tf_op jit(solution)/shard_map/ppermute | solution.py:578
  30.9 9.5 %collective-permute-start.12 = (f32[136,1280]{1,0:T(8,128)}, f32[136,1280]{1,0:T(8,128)}, u32[]{:S(2)}, u32[]{:S(2)}) collective-permute-start(f32[136,1280]{1,0:T(8,128)} %get-tuple-element.89.own_ref), channel_id=1, source_target_pairs={{0,1},{1,0},{2,3},{3,2},{4,5},{5,4},{6,7},{7,6},{8,9},{9,8},{10,11... | collective-permute-start | bytes 2088968 | tf_op jit(solution)/shard_map/ppermute | solution.py:578
  31.3 6.1 %collective-permute-start.3 = (s16[144,1280]{1,0:T(8,128)(2,1)}, s16[144,1280]{1,0:T(8,128)(2,1)S(1)}, u32[]{:S(2)}, u32[]{:S(2)}) collective-permute-start(s16[144,1280]{1,0:T(8,128)(2,1)} %copy-done.9), channel_id=1, source_target_pairs={{0,1},{1,3},{2,0},{3,5},{4,2},{5,7},{6,4},{7,6},{8,9},{9,11},{10,8... | collective-permute-start | bytes 1105928 | tf_op jit(solution)/shard_map/ppermute | solution.py:578
  32.8 9.1 %collective-permute-start.11 = (s16[144,1280]{1,0:T(8,128)(2,1)S(1)}, s16[144,1280]{1,0:T(8,128)(2,1)S(1)}, u32[]{:S(2)}, u32[]{:S(2)}) collective-permute-start(s16[144,1280]{1,0:T(8,128)(2,1)S(1)} %get-tuple-element.86), channel_id=1, source_target_pairs={{0,1},{1,3},{2,0},{3,5},{4,2},{5,7},{6,4},{7,6},{8,9},{9,11},{10,8... | collective-permute-start | bytes 1105928 | tf_op jit(solution)/shard_map/ppermute | solution.py:578
  35.2 2.2 %copy-start.18 = (f32[136,1280]{1,0:T(8,128)S(1)}, f32[136,1280]{1,0:T(8,128)}, u32[]{:S(2)}) copy-start(f32[136,1280]{1,0:T(8,128)} %copy-done.17) | copy-start | bytes 2088964
  37.4 3.0 %copy-start.20 = (f32[128,1280]{1,0:T(8,128)S(1)}, f32[128,1280]{1,0:T(8,128)}, u32[]{:S(2)}) copy-start(f32[128,1280]{1,0:T(8,128)} %copy-done.19) | copy-start | bytes 1966084
  38.3 8.0 %collective-permute-start.5 = (s16[144,1280]{1,0:T(8,128)(2,1)S(1)}, s16[144,1280]{1,0:T(8,128)(2,1)S(1)}, u32[]{:S(2)}, u32[]{:S(2)}) collective-permute-start(s16[144,1280]{1,0:T(8,128)(2,1)S(1)} %shard_map.151), channel_id=1, source_target_pairs={{0,1},{1,3},{2,0},{3,5},{4,2},{5,7},{6,4},{7,6},{8,9},{9,11},{10,8... | collective-permute-start | bytes 1105928 | tf_op jit(solution)/shard_map/ppermute | solution.py:578
  40.4 1.5 %copy-start.16 = (f32[136,1280]{1,0:T(8,128)S(1)}, f32[136,1280]{1,0:T(8,128)}, u32[]{:S(2)}) copy-start(f32[136,1280]{1,0:T(8,128)} %copy-done.15) | copy-start | bytes 2088964
  41.9 2.5 %copy-start.4 = (bf16[128,5120]{1,0:T(8,128)(2,1)S(1)}, bf16[128,5120]{1,0:T(8,128)(2,1)}, u32[]{:S(2)}) copy-start(bf16[128,5120]{1,0:T(8,128)(2,1)} %refs_11_.7) | copy-start | bytes 3932164
  41.9 2.5 %copy-start.28 = (f32[128,2560]{1,0:T(8,128)S(1)}, f32[128,2560]{1,0:T(8,128)}, u32[]{:S(2)}) copy-start(f32[128,2560]{1,0:T(8,128)} %copy-done.27) | copy-start | bytes 3932164
  41.9 2.5 %copy-start.32 = (f32[128,128]{1,0:T(8,128)S(1)}, f32[128,128]{1,0:T(8,128)}, u32[]{:S(2)}) copy-start(f32[128,128]{1,0:T(8,128)} %copy-done.31) | copy-start | bytes 196612
  42.8 6.3 %collective-permute-start.13 = (s16[144,1280]{1,0:T(8,128)(2,1)S(1)}, s16[144,1280]{1,0:T(8,128)(2,1)S(1)}, u32[]{:S(2)}, u32[]{:S(2)}) collective-permute-start(s16[144,1280]{1,0:T(8,128)(2,1)S(1)} %shard_map.156), channel_id=1, source_target_pairs={{0,1},{1,3},{2,0},{3,5},{4,2},{5,7},{6,4},{7,6},{8,9},{9,11},{10,8... | collective-permute-start | bytes 1105928 | tf_op jit(solution)/shard_map/ppermute | solution.py:578
  47.2 7.7 %collective-permute-start.6 = (s16[144,1280]{1,0:T(8,128)(2,1)S(1)}, s16[144,1280]{1,0:T(8,128)(2,1)S(1)}, u32[]{:S(2)}, u32[]{:S(2)}) collective-permute-start(s16[144,1280]{1,0:T(8,128)(2,1)S(1)} %shard_map.152), channel_id=1, source_target_pairs={{0,1},{1,3},{2,0},{3,5},{4,2},{5,7},{6,4},{7,6},{8,9},{9,11},{10,8... | collective-permute-start | bytes 1105928 | tf_op jit(solution)/shard_map/ppermute | solution.py:578
  50.1 7.4 %collective-permute-start.14 = (s16[144,1280]{1,0:T(8,128)(2,1)S(1)}, s16[144,1280]{1,0:T(8,128)(2,1)S(1)}, u32[]{:S(2)}, u32[]{:S(2)}) collective-permute-start(s16[144,1280]{1,0:T(8,128)(2,1)S(1)} %shard_map.157), channel_id=1, source_target_pairs={{0,1},{1,3},{2,0},{3,5},{4,2},{5,7},{6,4},{7,6},{8,9},{9,11},{10,8... | collective-permute-start | bytes 1105928 | tf_op jit(solution)/shard_map/ppermute | solution.py:578
  54.3 10.5 %collective-permute-start.20 = (s16[144,1280]{1,0:T(8,128)(2,1)S(1)}, s16[144,1280]{1,0:T(8,128)(2,1)S(1)}, u32[]{:S(2)}, u32[]{:S(2)}) collective-permute-start(s16[144,1280]{1,0:T(8,128)(2,1)S(1)} %collective-permute-done.11.previous_ref.refs_0_), channel_id=1, source_target_pairs={{0,1},{1,0},{2,3},{3,2},{4,5},{5,4},{6,7},{7,6},{8,9},{9,8},{10,11... | collective-permute-start | bytes 1105928 | tf_op jit(solution)/shard_map/ppermute | solution.py:578
  54.7 10.3 %collective-permute-start.16 = (s16[144,1280]{1,0:T(8,128)(2,1)S(1)}, s16[144,1280]{1,0:T(8,128)(2,1)S(1)}, u32[]{:S(2)}, u32[]{:S(2)}) collective-permute-start(s16[144,1280]{1,0:T(8,128)(2,1)S(1)} %collective-permute-done.13.previous_ref.refs_1_.refs_0_), channel_id=1, source_target_pairs={{0,1},{1,0},{2,3},{3,2},{4,5},{5,4},{6,7},{7,6},{8,9},{9,8},{10,11... | collective-permute-start | bytes 1105928 | tf_op jit(solution)/shard_map/ppermute | solution.py:578
  55.8 5.2 %copy-start.24 = (f32[128,2560]{1,0:T(8,128)S(1)}, f32[128,2560]{1,0:T(8,128)}, u32[]{:S(2)}) copy-start(f32[128,2560]{1,0:T(8,128)} %copy-done.23) | copy-start | bytes 3932164
  55.9 9.6 %collective-permute-start.7 = (s16[144,1280]{1,0:T(8,128)(2,1)S(1)}, s16[144,1280]{1,0:T(8,128)(2,1)S(1)}, u32[]{:S(2)}, u32[]{:S(2)}) collective-permute-start(s16[144,1280]{1,0:T(8,128)(2,1)S(1)} %shard_map.153), channel_id=1, source_target_pairs={{0,1},{1,3},{2,0},{3,5},{4,2},{5,7},{6,4},{7,6},{8,9},{9,11},{10,8... | collective-permute-start | bytes 1105928 | tf_op jit(solution)/shard_map/ppermute | solution.py:578
  58.3 7.5 %collective-permute-start.15 = (s16[144,1280]{1,0:T(8,128)(2,1)S(1)}, s16[144,1280]{1,0:T(8,128)(2,1)S(1)}, u32[]{:S(2)}, u32[]{:S(2)}) collective-permute-start(s16[144,1280]{1,0:T(8,128)(2,1)S(1)} %shard_map.158), channel_id=1, source_target_pairs={{0,1},{1,3},{2,0},{3,5},{4,2},{5,7},{6,4},{7,6},{8,9},{9,11},{10,8... | collective-permute-start | bytes 1105928 | tf_op jit(solution)/shard_map/ppermute | solution.py:578
  60.2 8.3 %collective-permute-start.17 = (s16[144,1280]{1,0:T(8,128)(2,1)S(1)}, s16[144,1280]{1,0:T(8,128)(2,1)S(1)}, u32[]{:S(2)}, u32[]{:S(2)}) collective-permute-start(s16[144,1280]{1,0:T(8,128)(2,1)S(1)} %collective-permute-done.14.previous_ref.refs_2_.refs_1_), channel_id=1, source_target_pairs={{0,1},{1,0},{2,3},{3,2},{4,5},{5,4},{6,7},{7,6},{8,9},{9,8},{10,11... | collective-permute-start | bytes 1105928 | tf_op jit(solution)/shard_map/ppermute | solution.py:578
  62.9 5.5 %copy-start.8 = (f32[136,1280]{1,0:T(8,128)S(1)}, f32[136,1280]{1,0:T(8,128)}, u32[]{:S(2)}) copy-start(f32[136,1280]{1,0:T(8,128)} %copy-done.7) | copy-start | bytes 2088964
  63.0 5.5 %copy-start.30 = (f32[128,2560]{1,0:T(8,128)S(1)}, f32[128,2560]{1,0:T(8,128)}, u32[]{:S(2)}) copy-start(f32[128,2560]{1,0:T(8,128)} %copy-done.29) | copy-start | bytes 3932164
  64.9 8.8 %collective-permute-start.19 = (s16[144,1280]{1,0:T(8,128)(2,1)S(1)}, s16[144,1280]{1,0:T(8,128)(2,1)S(1)}, u32[]{:S(2)}, u32[]{:S(2)}) collective-permute-start(s16[144,1280]{1,0:T(8,128)(2,1)S(1)} %collective-permute-done.3.previous_ref.refs_0_), channel_id=1, source_target_pairs={{0,1},{1,0},{2,3},{3,2},{4,5},{5,4},{6,7},{7,6},{8,9},{9,8},{10,11... | collective-permute-start | bytes 1105928 | tf_op jit(solution)/shard_map/ppermute | solution.py:578
  65.0 8.7 %collective-permute-start.8 = (s16[144,1280]{1,0:T(8,128)(2,1)S(1)}, s16[144,1280]{1,0:T(8,128)(2,1)S(1)}, u32[]{:S(2)}, u32[]{:S(2)}) collective-permute-start(s16[144,1280]{1,0:T(8,128)(2,1)S(1)} %collective-permute-done.5.previous_ref.refs_1_.refs_0_), channel_id=1, source_target_pairs={{0,1},{1,0},{2,3},{3,2},{4,5},{5,4},{6,7},{7,6},{8,9},{9,8},{10,11... | collective-permute-start | bytes 1105928 | tf_op jit(solution)/shard_map/ppermute | solution.py:578
  65.5 8.2 %collective-permute-start.9 = (s16[144,1280]{1,0:T(8,128)(2,1)S(1)}, s16[144,1280]{1,0:T(8,128)(2,1)S(1)}, u32[]{:S(2)}, u32[]{:S(2)}) collective-permute-start(s16[144,1280]{1,0:T(8,128)(2,1)S(1)} %collective-permute-done.6.previous_ref.refs_2_.refs_1_), channel_id=1, source_target_pairs={{0,1},{1,0},{2,3},{3,2},{4,5},{5,4},{6,7},{7,6},{8,9},{9,8},{10,11... | collective-permute-start | bytes 1105928 | tf_op jit(solution)/shard_map/ppermute | solution.py:578
  65.8 18.8 %collective-permute-start.10 = (s16[144,1280]{1,0:T(8,128)(2,1)S(1)}, s16[144,1280]{1,0:T(8,128)(2,1)S(1)}, u32[]{:S(2)}, u32[]{:S(2)}) collective-permute-start(s16[144,1280]{1,0:T(8,128)(2,1)S(1)} %collective-permute-done.7.refs_2_), channel_id=1, source_target_pairs={{0,1},{1,0},{2,3},{3,2},{4,5},{5,4},{6,7},{7,6},{8,9},{9,8},{10,11... | collective-permute-start | bytes 1105928 | tf_op jit(solution)/shard_map/ppermute | solution.py:578
  68.5 10.4 %collective-permute-start.18 = (s16[144,1280]{1,0:T(8,128)(2,1)S(1)}, s16[144,1280]{1,0:T(8,128)(2,1)S(1)}, u32[]{:S(2)}, u32[]{:S(2)}) collective-permute-start(s16[144,1280]{1,0:T(8,128)(2,1)S(1)} %collective-permute-done.15.refs_2_), channel_id=1, source_target_pairs={{0,1},{1,0},{2,3},{3,2},{4,5},{5,4},{6,7},{7,6},{8,9},{9,8},{10,11... | collective-permute-start | bytes 1105928 | tf_op jit(solution)/shard_map/ppermute | solution.py:578
  68.5 5.2 %copy-start.6 = (f32[136,1280]{1,0:T(8,128)S(1)}, f32[136,1280]{1,0:T(8,128)}, u32[]{:S(2)}) copy-start(f32[136,1280]{1,0:T(8,128)} %copy-done.5) | copy-start | bytes 2088964
  73.7 5.2 %copy-start.26 = (f32[128,2560]{1,0:T(8,128)S(1)}, f32[128,2560]{1,0:T(8,128)}, u32[]{:S(2)}) copy-start(f32[128,2560]{1,0:T(8,128)} %copy-done.25) | copy-start | bytes 3932164
  90.8 20.9 %copy-start.14 = (s32[128]{0:T(128)S(1)}, s32[128]{0:T(128)}, u32[]{:S(2)}) copy-start(s32[128]{0:T(128)} %param.10) | copy-start | bytes 1540
  90.8 1.5 %collective-permute-start.22 = (f32[8,2688]{1,0:T(8,128)S(1)}, f32[8,2688]{1,0:T(8,128)S(1)}, u32[]{:S(2)}, u32[]{:S(2)}) collective-permute-start(f32[8,2688]{1,0:T(8,128)S(1)} %slice_select_fusion), channel_id=1, source_target_pairs={{0,1},{1,0},{2,3},{3,2},{4,5},{5,4},{6,7},{7,6},{8,9},{9,8},{10,11... | collective-permute-start | bytes 258056 | tf_op jit(solution)/shard_map/ppermute | solution.py:578
  92.3 4.7 %collective-permute-start.25 = (f32[8,2688]{1,0:T(8,128)S(1)}, f32[8,2688]{1,0:T(8,128)S(1)}, u32[]{:S(2)}, u32[]{:S(2)}) collective-permute-start(f32[8,2688]{1,0:T(8,128)S(1)} %select_add_fusion), channel_id=1, source_target_pairs={{0,24},{8,16},{16,8},{24,0},{1,25},{9,17},{17,9},{25,1},{2,26},{10... | collective-permute-start | bytes 258056 | tf_op jit(solution)/shard_map/ppermute | solution.py:578
  94.6 4.6 %collective-permute-start.24 = (f32[8,2688]{1,0:T(8,128)S(1)}, f32[8,2688]{1,0:T(8,128)S(1)}, u32[]{:S(2)}, u32[]{:S(2)}) collective-permute-start(f32[8,2688]{1,0:T(8,128)S(1)} %select_add_fusion), channel_id=1, source_target_pairs={{0,16},{8,24},{16,0},{24,8},{1,17},{9,25},{17,1},{25,9},{2,18},{10... | collective-permute-start | bytes 258056 | tf_op jit(solution)/shard_map/ppermute | solution.py:578
  94.8 4.4 %collective-permute-start.23 = (f32[8,2688]{1,0:T(8,128)S(1)}, f32[8,2688]{1,0:T(8,128)S(1)}, u32[]{:S(2)}, u32[]{:S(2)}) collective-permute-start(f32[8,2688]{1,0:T(8,128)S(1)} %select_add_fusion), channel_id=1, source_target_pairs={{0,8},{8,0},{16,24},{24,16},{1,9},{9,1},{17,25},{25,17},{2,10},{10... | collective-permute-start | bytes 258056 | tf_op jit(solution)/shard_map/ppermute | solution.py:578
  99.2 7.4 %collective-permute-start.28 = (f32[8,2688]{1,0:T(8,128)S(1)}, f32[8,2688]{1,0:T(8,128)S(1)}, u32[]{:S(2)}, u32[]{:S(2)}) collective-permute-start(f32[8,2688]{1,0:T(8,128)S(1)} %add_add_fusion), channel_id=1, source_target_pairs={{0,6},{1,7},{2,4},{3,5},{4,2},{5,3},{6,0},{7,1},{8,14},{9,15},{10,... | collective-permute-start | bytes 258056 | tf_op jit(solution)/shard_map/ppermute | solution.py:578
  101.2 9.2 %collective-permute-start.27 = (f32[8,2688]{1,0:T(8,128)S(1)}, f32[8,2688]{1,0:T(8,128)S(1)}, u32[]{:S(2)}, u32[]{:S(2)}) collective-permute-start(f32[8,2688]{1,0:T(8,128)S(1)} %add_add_fusion), channel_id=1, source_target_pairs={{0,4},{1,5},{2,6},{3,7},{4,0},{5,1},{6,2},{7,3},{8,12},{9,13},{10,... | collective-permute-start | bytes 258056 | tf_op jit(solution)/shard_map/ppermute | solution.py:578
  102.5 8.0 %collective-permute-start.26 = (f32[8,2688]{1,0:T(8,128)S(1)}, f32[8,2688]{1,0:T(8,128)S(1)}, u32[]{:S(2)}, u32[]{:S(2)}) collective-permute-start(f32[8,2688]{1,0:T(8,128)S(1)} %add_add_fusion), channel_id=1, source_target_pairs={{0,2},{1,3},{2,0},{3,1},{4,6},{5,7},{6,4},{7,5},{8,10},{9,11},{10,... | collective-permute-start | bytes 258056 | tf_op jit(solution)/shard_map/ppermute | solution.py:578
  102.8 8.9 %collective-permute-start.21 = (f32[3,5376]{1,0:T(4,128)S(1)}, f32[3,5376]{1,0:T(4,128)S(1)}, u32[]{:S(2)}, u32[]{:S(2)}) collective-permute-start(f32[3,5376]{1,0:T(4,128)S(1)} %slice.28), channel_id=1, source_target_pairs={{1,0},{2,1},{3,2},{4,3},{5,4},{6,5},{7,6},{9,8},{10,9},{11,10},{12... | collective-permute-start | bytes 193544 | tf_op jit(solution)/shard_map/ppermute | solution.py:790
  110.5 3.0 %collective-permute-start.29 = (f32[8,2688]{1,0:T(8,128)S(1)}, f32[8,2688]{1,0:T(8,128)S(1)}, u32[]{:S(2)}, u32[]{:S(2)}) collective-permute-start(f32[8,2688]{1,0:T(8,128)S(1)} %add_multiply_fusion), channel_id=1, source_target_pairs={{0,1},{1,0},{2,3},{3,2},{4,5},{5,4},{6,7},{7,6},{8,9},{9,8},{10,11... | collective-permute-start | bytes 258056 | tf_op jit(solution)/shard_map/ppermute | solution.py:578
  (17 other events, 16.8 us)
where the time goes:
time: 116 us; the launch traced here: 115 us
  Pallas kernels  50.9 us (44%)
  starting transfers between devices  35.4 us (31%)
  local copies, waits for them, and re-layouts  13.7 us (12%)
  waiting for transfers between devices  12.5 us (11%)
  other arithmetic  1.71 us (1%)
    pallas_call x24, Pallas kernels, call(): pl.pallas_call(kernel, grid=(1,), in_specs=specs, out_specs=out_specs, ou...  50.9 us
    ppermute x28, starting transfers between devices, permute(): return lax.ppermute(value, axis, [(i, target(i)) for i in range(size)])  27 us
    unnamed x71, local copies, waits for them, and re-layouts  13.2 us
    ppermute x28, waiting for transfers between devices, permute(): return lax.ppermute(value, axis, [(i, target(i)) for i in range(size)])  12.4 us
    ppermute x1, starting transfers between devices, on_device(): halo = lax.ppermute(tail_out, 'seq', [(i, i + 1) for i in range(size - 1)])  4.59 us
    ppermute x1, starting transfers between devices, on_device(): lax.ppermute(misc[8 - CONV + 1:8], 'seq', [(i, i - 1) for i in range(1, s...  3.77 us
  transfers between devices with their start and end apart: 30, of which 9 were waited for; matrix products, arithmetic and copies ran while one was open for 0% of the time, Pallas kernels for 30%

commit v1 on v0

--- a/solution.py
+++ b/solution.py
@@ -143,7 +143,7 @@
 
 
 def prep_kernel(doc_ref, raw_ref, dtb_ref, alog_ref, skip_ref, tab_ref):
-    count = raw_ref.shape[0]
+    count = raw_ref.shape[1]
     resets = doc_ref[...].astype(F32)
     t, s = iota((count, count), 0), iota((count, count), 1)
 
@@ -173,7 +173,8 @@
     )
     causal = (s <= t) & (segment == segment_row)
     tab_ref[FAR_AT : FAR_AT + count, :] = jnp.where(causal, 0.0, FAR)
-    v = raw_ref[...] + dtb_ref[...]
+    raw = rows(raw_ref[...], jnp.zeros((128 - HEADS, count), F32)).T[:, :HEADS]
+    v = raw + dtb_ref[...]
     dt = jnp.maximum(v, 0.0) + jnp.log1p(jnp.exp(-jnp.abs(v)))
     rate = -jnp.exp(alog_ref[...])
     decay = rate * dt
@@ -211,11 +212,10 @@
         refs = refs[3:]
     else:
         turned_ref = refs.pop(0)
-    act_ref, slope_ref = refs[:2]
-    send_refs, mine_refs = refs[2 : 2 + STREAMS], refs[2 + STREAMS : 2 + 2 * STREAMS]
+    send_refs, mine_refs = refs[:STREAMS], refs[STREAMS : 2 * STREAMS]
     if lead:
-        bca_ref, bcs_ref, turned_ref, scores_ref = refs[2 + 2 * STREAMS : 6 + 2 * STREAMS]
-    xb, cb, ab, sb, nb, mb, ext_ref, bx, in_sems, out_sems = refs[-10:]
+        bca_ref, bcs_ref, turned_ref, scores_ref = refs[2 * STREAMS : 4 + 2 * STREAMS]
+    xb, cb, nb, mb, ext_ref, bx, in_sems, out_sems = refs[-8:]
     count = xb.shape[0]
     come, go = Flow(in_sems), Flow(out_sems)
     if lead:
@@ -259,9 +259,7 @@
             cols = at(start)
             head = (turn * SPAN + start) // HEAD_DIM
             taps = load(cols, xb[:, cols], halo_ref[:, cols])
-            act, slope = activate(taps, cols, w_ref, b_ref)
-            ab[:, cols] = act
-            sb[:, cols] = slope
+            act, _ = activate(taps, cols, w_ref, b_ref)
             e = by_head(entry, head, PER)
             lx_high, lx_low = halves(act * by_head(leave, head, PER))
             ey_high, ey_low = halves(cb[:, cols].astype(F32) * e)
@@ -271,8 +269,7 @@
             mb[:, cols] = jnp.where(first_core, adjoint, state)
             nb[STATE:, cols] = jnp.broadcast_to(e[count - 1 : count, :], (8, CHUNK))
         cols = at(stream * WIDTH, WIDTH)
-        targets = (send_refs[stream], mine_refs[stream], act_ref.at[:, cols], slope_ref.at[:, cols])
-        for source, target in zip((nb, mb, ab, sb), targets):
+        for source, target in ((nb, send_refs[stream]), (mb, mine_refs[stream])):
             copy = go.copy(source.at[:, cols], target)
             copy.start()
             leaving.append(copy)
@@ -328,17 +325,19 @@
         out_ref[:, cols] = encode(chip[:STATE, :] + chip[STATE : STATE + 1, :] * before)
 
 
-def within_kernel(piece, act_ref, cot_ref, tab_ref, scores_ref, y_ref, dx_ref, dscores_ref, *refs):
-    ab, cb, yb, db, in_sems, out_sems = refs
-    count = ab.shape[0]
+def within_kernel(
+    piece, x_ref, cot_ref, halo_ref, w_ref, b_ref, tab_ref, scores_ref, y_ref, dx_ref, dscores_ref, *refs
+):
+    xb, cb, yb, db, ext_ref, in_sems, out_sems = refs
+    count = xb.shape[0]
     come, go = Flow(in_sems), Flow(out_sems)
-    base = (piece % STREAMS) * WIDTH
     copies = (
-        come.copy(act_ref.at[:, at(base, WIDTH)], ab),
+        come.copy(x_ref.at[:, at(piece * WIDTH, WIDTH)], xb),
         come.copy(cot_ref.at[:, at(piece * WIDTH, WIDTH)], cb),
     )
     for copy in copies:
         copy.start()
+    mask = columns(tab_ref[MASK : MASK + count, :], PAIR)
     for copy in copies:
         copy.wait()
     run = tab_ref[RUN : RUN + count, :]
@@ -348,7 +347,10 @@
     zero = jnp.zeros((count, PAIR), BF16)
     for pair in range(PIECE_HEADS // 2):
         cols = at(pair * PAIR, PAIR)
-        x_high, x_low = halves(ab[:, cols])
+        ext_ref[8 : 8 + count, cols] = xb[:, cols].astype(F32)
+        ext_ref[8 - CONV + 1 : 8, cols] = halo_ref[:, cols].astype(F32)
+        act, _ = activate(taps_of(ext_ref, cols, count, mask), cols, w_ref, b_ref)
+        x_high, x_low = halves(act)
         upstream = cb[:, cols]
         upstream_turned = upstream.astype(F32).T.astype(BF16)
         spread, weights = [], []
@@ -401,12 +403,12 @@
 def finish_kernel(piece, hops, flag_ref, *refs):
     incs, exchs = refs[:hops], refs[hops : 2 * hops]
     refs = refs[2 * hops :]
-    met_ref, act_ref, slope_ref, y_ref, dx_ref, cot_ref, x_ref, halo_ref, w_ref, tab_ref, bc_ref = refs[:11]
-    out_ref, gin_ref, misc_ref, dreads_ref, dkeys_ref, scal_ref = refs[-22:-16]
-    ib, hb, eb, ab, sb, yb, db, cb, xb, ob, gb, nb, ext_ref, z_ref, in_sems, out_sems = refs[-16:]
+    met_ref, y_ref, dx_ref, cot_ref, x_ref, halo_ref, w_ref, b_ref, tab_ref, bc_ref = refs[:10]
+    out_ref, gin_ref, misc_ref, dreads_ref, dkeys_ref, scal_ref = refs[-20:-14]
+    ib, hb, eb, yb, db, cb, xb, ob, gb, nb, ext_ref, z_ref, in_sems, out_sems = refs[-14:]
     count = xb.shape[0]
     come, go = Flow(in_sems), Flow(out_sems)
-    within, base = (piece % STREAMS) * WIDTH, piece * WIDTH
+    base = piece * WIDTH
     place = flag_ref[1]
     choices = []
     for here, sources, buffer in ((place, incs, ib), (hops - place, exchs, hb)):
@@ -424,11 +426,9 @@
     arriving, leaving = [], []
     for start, width in ((0, CHUNK), (CHUNK, WIDTH - CHUNK)):
         cols = at(start, width)
-        stream_cols, whole_cols = at(within + start, width), at(base + start, width)
+        whole_cols = at(base + start, width)
         group = [
             come.copy(met_ref.at[:, cols], eb.at[:, cols]),
-            come.copy(act_ref.at[:, stream_cols], ab.at[:, cols]),
-            come.copy(slope_ref.at[:, stream_cols], sb.at[:, cols]),
             come.copy(y_ref.at[:, cols], yb.at[:, cols]),
             come.copy(dx_ref.at[:, cols], db.at[:, cols]),
             come.copy(cot_ref.at[:, whole_cols], cb.at[:, cols]),
@@ -451,7 +451,7 @@
     for chosen, copy in choices:
         pl.when(chosen)(copy.wait)
     for start in range(0, WIDTH, CHUNK):
-        cols, whole_cols = at(start), at(base + start)
+        cols = at(start)
         head = (base + start) // HEAD_DIM
         if start <= CHUNK:
             for copy in arriving[start // CHUNK]:
@@ -463,7 +463,11 @@
         s_high, s_low = halves(state)
         a_high, a_low = halves(adjoint)
         e, leaves = by_head(entry, head, PER), by_head(leave, head, PER)
-        act, up = ab[:, cols], cb[:, cols].astype(F32)
+        ext_ref[8 : 8 + count, cols] = xb[:, cols].astype(F32)
+        ext_ref[8 - CONV + 1 : 8, cols] = halo_ref[:, cols].astype(F32)
+        taps = taps_of(ext_ref, cols, count, mask)
+        act, slope = activate(taps, cols, w_ref, b_ref)
+        up = cb[:, cols].astype(F32)
         carried = mm(reads_both, rows(s_high, s_high)) + mm(reads[0], s_low)
         y = yb[:, cols] + e * carried
         back = mm(keys_both, rows(a_high, a_high)) + mm(keys[0], a_low)
@@ -484,11 +488,8 @@
         stack = halves(up * y - received) + halves(received)
         pick = (iota((CHUNK, 128), 1) == head + iota((CHUNK, 128), 0) // HEAD_DIM).astype(BF16)
         sums = sums + mm(rows(*stack, rows(*small)), pick)
-        dconv = (dx + gain * up) * sb[:, cols]
-        ext_ref[8 : 8 + count, cols] = xb[:, cols].astype(F32)
-        ext_ref[8 - CONV + 1 : 8, cols] = halo_ref[:, whole_cols].astype(F32)
-        taps = taps_of(ext_ref, cols, count, mask)
-        gb[:, cols], nb[:, cols] = conv_back(dconv, taps, w_ref[:, whole_cols], z_ref, cols, smask)
+        dconv = (dx + gain * up) * slope
+        gb[:, cols], nb[:, cols] = conv_back(dconv, taps, w_ref[:, cols], z_ref, cols, smask)
     for source, target in ((ob, out_ref), (gb, gin_ref), (nb, misc_ref)):
         copy = go.copy(source, target.at[:, at(base, WIDTH)])
         copy.start()
@@ -655,22 +656,21 @@
     halo = lax.ppermute(tail_out, "seq", [(i, i + 1) for i in range(size - 1)])
 
     bias = conv_bias[None, :]
-    prep_in = (docs, dt_raw, dt_bias[None, :], a_log[None, :], skip_gain[None, :])
+    prep_in = (docs, dt_raw.T, dt_bias[None, :], a_log[None, :], skip_gain[None, :])
     table = (TABLE, 128)
     tab = call(prep_kernel, prep_in, full(*prep_in), [(table, F32)], [whole(table)])[0]
 
     square = (count, count)
     payload = (STATE + 16, WIDTH)
     shape = (count, WIDTH)
-    acts, slopes, chips, sent = [], [], [], []
-    mets = []
+    chips, sent, mets = [], [], []
     given = tab
     for turn in range(TURNS):
         lead = turn == 0
         here = [part((height, SPAN), 0, turn) for height in (CONV - 1, CONV, 1)]
         ins = [flag, conv_input, halo, conv_weight, bias, cotangent, given]
         specs = [SMEM, HBM, *here, HBM, whole(table)]
-        outs = [(count, SPAN)] * 2 + [(STATE + 8, WIDTH)] * STREAMS + [(STATE, WIDTH)] * STREAMS
+        outs = [(STATE + 8, WIDTH)] * STREAMS + [(STATE, WIDTH)] * STREAMS
         out_specs = [HBM] * len(outs)
         if lead:
             ins += [halo, conv_weight, bias]
@@ -688,18 +688,14 @@
             [(s, F32) for s in outs],
             out_specs,
             [
-                vmem(count, SPAN, BF16), vmem(count, SPAN, BF16), vmem(count, SPAN),
-                vmem(count, SPAN), vmem(STATE + 8, SPAN), vmem(STATE, SPAN),
-                vmem(count + 8, SPAN + BC), vmem(count, BC, BF16),
-                sems(2 * STREAMS + 1), sems(4 * STREAMS),
+                vmem(count, SPAN, BF16), vmem(count, SPAN, BF16), vmem(STATE + 8, SPAN),
+                vmem(STATE, SPAN), vmem(count + 8, SPAN + BC), vmem(count, BC, BF16),
+                sems(2 * STREAMS + 1), sems(2 * STREAMS),
             ],
             us=5.0,
         )
-        act, slope, *got = got
         if lead:
             bc_act, bc_slope, turned, scores = got[2 * STREAMS :]
-        acts.append(act)
-        slopes.append(slope)
         for stream in range(STREAMS):
             send, mine = got[stream], got[STREAMS + stream]
             met = other_core(send)
@@ -707,50 +703,37 @@
             chip, *first = chip_of(lead, mine, met, send)
             chips.append(chip)
             sent += first
-        if lead:
-            given, *sent = lax.optimization_barrier((given, *sent))
-
-    received = [[] for _ in range(STREAMS)]
-    swapped = [[] for _ in range(STREAMS)]
-    for turn in range(TURNS + hops - 1):
-        if turn:
-            piece = jnp.clip(turn - place, 0, TURNS - 1)
-            pick = jnp.stack([piece, place]).astype(jnp.int32)
-            sent = [
-                hop(pick, received[stream][-1], chips[stream::STREAMS]) for stream in range(STREAMS)
-            ]
-        for stream in range(STREAMS):
-            got = permute(sent[stream], "seq", along(size))
-            received[stream].append(got)
-            swapped[stream].append(other_core(got))
 
     withins = []
     for j in range(PIECES):
-        ins = (acts[j // STREAMS], cotangent, tab, scores)
+        here = [part((height, WIDTH), 0, j) for height in (CONV - 1, CONV, 1)]
         withins.append(
             call(
                 functools.partial(within_kernel, j),
-                ins,
-                [HBM, HBM, *full(tab, scores)],
+                (conv_input, cotangent, halo, conv_weight, bias, tab, scores),
+                [HBM, HBM, *here, *full(tab, scores)],
                 [(shape, F32), (shape, F32), (square, F32)],
                 [HBM, HBM, whole(square)],
-                [vmem(*shape), vmem(*shape, BF16), vmem(*shape), vmem(*shape), sems(2), sems(2)],
-                us=3.0,
+                [
+                    vmem(*shape, BF16), vmem(*shape, BF16), vmem(*shape), vmem(*shape),
+                    vmem(count + 8, WIDTH), sems(2), sems(2),
+                ],
+                us=2.0,
             )
         )
 
-    shared = None
     dreads, dkeys, scals = [None] * PIECES, [None] * PIECES, [None] * PIECES
     shared_out = [((count, INNER), BF16), ((count, CH), BF16), ((24, CH), F32)]
     small_out = [((count, STATE), F32), ((count, STATE), F32), ((8, 128), F32)]
-    for j in range(PIECES):
+
+    def finish(j, shared):
         turn, stream = j // STREAMS, j % STREAMS
+        here = [part((height, WIDTH), 0, j) for height in (CONV - 1, CONV, 1)]
         y, dx, _ = withins[j]
         ins = [flag, *received[stream][turn : turn + hops], *swapped[stream][turn : turn + hops]]
         specs = [SMEM] + [ANY] * (2 * hops)
-        ins += [mets[j], acts[turn], slopes[turn], y, dx, cotangent, conv_input]
-        specs += [HBM] * 7 + full(halo, conv_weight, tab, bc_act)
-        ins += [halo, conv_weight, tab, bc_act]
+        ins += [mets[j], y, dx, cotangent, conv_input, halo, conv_weight, bias, tab, bc_act]
+        specs += [HBM] * 5 + here + full(tab, bc_act)
         aliases = None
         if shared is not None:
             aliases = {len(ins) + i: i for i in range(3)}
@@ -764,13 +747,36 @@
             [HBM] * 3 + [whole(s) for s, _ in small_out],
             [
                 vmem(*payload, I16), vmem(*payload, I16), vmem(STATE + 8, WIDTH),
-                vmem(*shape), vmem(*shape), vmem(*shape), vmem(*shape), vmem(*shape, BF16),
-                vmem(*shape, BF16), vmem(*shape, BF16), vmem(*shape, BF16), vmem(24, WIDTH),
-                vmem(count + 8, WIDTH), vmem(count + 16, WIDTH), sems(2 + 14), sems(3),
+                vmem(*shape), vmem(*shape), vmem(*shape, BF16), vmem(*shape, BF16),
+                vmem(*shape, BF16), vmem(*shape, BF16), vmem(24, WIDTH),
+                vmem(count + 8, WIDTH), vmem(count + 16, WIDTH), sems(2 + 10), sems(3),
             ],
             aliases,
             us=5.0,
         )
+        return shared
+
+    received = [[] for _ in range(STREAMS)]
+    swapped = [[] for _ in range(STREAMS)]
+    shared = None
+    turns = TURNS + hops - 1
+    for turn in range(turns):
+        if turn:
+            piece = jnp.clip(turn - place, 0, TURNS - 1)
+            pick = jnp.stack([piece, place]).astype(jnp.int32)
+            sent = [
+                hop(pick, received[stream][-1], chips[stream::STREAMS]) for stream in range(STREAMS)
+            ]
+        arrived = [permute(value, "seq", along(size)) for value in sent]
+        for stream in range(STREAMS):
+            got = arrived[stream]
+            if turn == turns - 1:
+                shared = finish(stream, shared)
+                got, shared = lax.optimization_barrier((got, shared))
+            received[stream].append(got)
+            swapped[stream].append(other_core(got))
+    for j in range(STREAMS, PIECES):
+        shared = finish(j, shared)
     output, gin, misc = shared
 
     dscores = [group[2] for group in withins]

time: 116 us -> 110 us (0.948)
  local copies, waits for them, and re-layouts: 13.7 us -> 8.95 us
  waiting for transfers between devices: 12.5 us -> 7.93 us
  Pallas kernels: 50.9 us -> 54.8 us
    ppermute x28, waiting for transfers between devices: 12.4 us -> 7.55 us  [permute(): return lax.ppermute(value, axis, [(i, target(i)) for i in range(size)])]
    unnamed x71 -> x44, local copies, waits for them, and re-layouts: 13.2 us -> 8.4 us
    pallas_call x24, Pallas kernels: 50.9 us -> 54.8 us  [call(): pl.pallas_call(kernel, grid=(1,), in_specs=specs, out_specs=out_specs, ou...]
  transfers between devices with their start and end apart: 30 -> 30, of which waited for: 9 -> 10; matrix products, arithmetic and copies ran while one was open for 0% -> 0% of each run, Pallas kernels for 30% -> 40%
where the time goes in v1:
time: 110 us; the launch traced here: 109 us
  Pallas kernels  54.8 us (50%)
  starting transfers between devices  34.7 us (32%)
  local copies, waits for them, and re-layouts  8.95 us (8%)
  waiting for transfers between devices  7.93 us (7%)
  other arithmetic  1.71 us (2%)
    pallas_call x24, Pallas kernels, call(): pl.pallas_call(kernel, grid=(1,), in_specs=specs, out_specs=out_specs, ou...  54.8 us
    ppermute x28, starting transfers between devices, permute(): return lax.ppermute(value, axis, [(i, target(i)) for i in range(size)])  26.5 us
    unnamed x44, local copies, waits for them, and re-layouts  8.4 us
    ppermute x28, waiting for transfers between devices, permute(): return lax.ppermute(value, axis, [(i, target(i)) for i in range(size)])  7.55 us
    ppermute x1, starting transfers between devices, on_device(): halo = lax.ppermute(tail_out, 'seq', [(i, i + 1) for i in range(size - 1)])  4.59 us
    ppermute x1, starting transfers between devices, on_device(): lax.ppermute(misc[8 - CONV + 1:8], 'seq', [(i, i - 1) for i in range(1, s...  3.68 us
  transfers between devices with their start and end apart: 30, of which 10 were waited for; matrix products, arithmetic and copies ran while one was open for 0% of the time, Pallas kernels for 40%

profile of v1, /device:TPU:1, one launch (start us, length us, event | category | flops | bytes accessed | tf_op | source)
XLA Modules:
  0.0 109.2 jit_solution(12027416064072593835)
XLA Ops:
  0.6 1.3 %copy-done = bf16[128,5376]{1,0:T(8,128)(2,1)S(1)} copy-done((bf16[128,5376]{1,0:T(8,128)(2,1)S(1)}, bf16[128,5376]{1,0:T(8,128)(2,1)}, u32[]{:S(2)}) %copy-start) | copy-done | bytes 1376280
  2.8 4.6 %collective-permute-start = (bf16[3,5376]{1,0:T(4,128)(2,1)S(1)}, bf16[3,5376]{1,0:T(4,128)(2,1)S(1)}, u32[]{:S(2)}, u32[]{:S(2)}) collective-permute-start(bf16[3,5376]{1,0:T(4,128)(2,1)S(1)} %shard_map.144), channel_id=1, source_target_pairs={{0,1},{1,2},{2,3},{3,4},{4,5},{5,6},{6,7},{8,9},{9,10},{10,11},{11... | collective-permute-start | bytes 96776 | tf_op jit(solution)/shard_map/ppermute | solution.py:656
  9.3 4.6 %shard_map.146 = (f32[136,1280]{1,0:T(8,128)}, f32[136,1280]{1,0:T(8,128)}, f32[128,1280]{1,0:T(8,128)S(1)}, f32[128,1280]{1,0:T(8,128)S(1)}, f32[128,256]{1,0:T...) custom-call(s32[2]{0:T(128)S(1)} %pad_add_fusion.flag_ref, ...), custom_call_target="tpu_custom_call" | custom-call | flops 5500000256 | bytes 1000 | tf_op jit(solution)/shard_map/pallas_call | solution.py:556
  13.9 0.8 copy-done.17
  14.8 0.8 copy-done.19
  16.1 3.4 %shard_map.148 = (f32[136,1280]{1,0:T(8,128)}, f32[136,1280]{1,0:T(8,128)S(1)}, f32[128,1280]{1,0:T(8,128)S(1)}, f32[128,1280]{1,0:T(8,128)S(1)}) custom-call(s32[2]{0:T(128)S(1)} %pad_add_fusion.flag_ref, bf16[128,5376]{1,0:T(8,128)(2,1)S(1)} %copy-done.1, bf16[3,5376]{1,0:T(4,128)(2,1)S(1)} %collective-permute-done.halo_ref.refs_0_.refs_11_, ...), custom_call_target="tpu_custom_call" | custom-call | flops 5500000256 | bytes 1000 | tf_op jit(solution)/shard_map/pallas_call | solution.py:556
  19.6 0.8 copy-done.5
  20.4 0.9 copy-done.13
  22.8 1.1 copy-done.20
  23.9 1.6 %shard_map.154 = (f32[136,1280]{1,0:T(8,128)S(1)}, s16[144,1280]{1,0:T(8,128)(2,1)S(1)}) custom-call(f32[128,1280]{1,0:T(8,128)S(1)} %copy-done.20, f32[136,1280]{1,0:T(8,128)} %collective-permute-done.10.met_ref.refs_6_, f32[136,1280]{1,0:T(8,128)} %get-tuple-element.81.own_ref), custom_call_target="tpu_custom_call" | custom-call | flops 1650000000 | bytes 1000 | tf_op jit(solution)/shard_map/pallas_call | solution.py:556
  25.4 1.3 %collective-permute-start.11 = (s16[144,1280]{1,0:T(8,128)(2,1)S(1)}, s16[144,1280]{1,0:T(8,128)(2,1)S(1)}, u32[]{:S(2)}, u32[]{:S(2)}) collective-permute-start(s16[144,1280]{1,0:T(8,128)(2,1)S(1)} %get-tuple-element.82), channel_id=1, source_target_pairs={{0,1},{1,3},{2,0},{3,5},{4,2},{5,7},{6,4},{7,6},{8,9},{9,11},{10,8... | collective-permute-start | bytes 1105928 | tf_op jit(solution)/shard_map/ppermute | solution.py:579
  26.8 1.6 %shard_map.147 = (f32[136,1280]{1,0:T(8,128)S(1)}, s16[144,1280]{1,0:T(8,128)(2,1)S(1)}) custom-call(f32[128,1280]{1,0:T(8,128)S(1)} %copy-done.18, f32[136,1280]{1,0:T(8,128)} %collective-permute-done.1.met_ref.refs_6_, f32[136,1280]{1,0:T(8,128)} %get-tuple-element.70.own_ref), custom_call_target="tpu_custom_call" | custom-call | flops 1650000000 | bytes 1000 | tf_op jit(solution)/shard_map/pallas_call | solution.py:556
  28.4 1.3 %collective-permute-start.2 = (s16[144,1280]{1,0:T(8,128)(2,1)S(1)}, s16[144,1280]{1,0:T(8,128)(2,1)S(1)}, u32[]{:S(2)}, u32[]{:S(2)}) collective-permute-start(s16[144,1280]{1,0:T(8,128)(2,1)S(1)} %get-tuple-element.71), channel_id=1, source_target_pairs={{0,1},{1,3},{2,0},{3,5},{4,2},{5,7},{6,4},{7,6},{8,9},{9,11},{10,8... | collective-permute-start | bytes 1105928 | tf_op jit(solution)/shard_map/ppermute | solution.py:579
  29.7 1.4 %shard_map.155.refs_1_ = f32[136,1280]{1,0:T(8,128)S(1)} custom-call(f32[128,1280]{1,0:T(8,128)S(1)} %copy-done.16, f32[136,1280]{1,0:T(8,128)} %collective-permute-done.12.met_ref.refs_6_, f32[136,1280]{1,0:T(8,128)} %get-tuple-element.85.own_ref), custom_call_target="tpu_custom_call" | custom-call | flops 1650000000 | bytes 1000 | tf_op jit(solution)/shard_map/pallas_call | solution.py:556
  31.2 0.9 shard_map.156
  32.1 2.2 %collective-permute-start.13 = (s16[144,1280]{1,0:T(8,128)(2,1)S(1)}, s16[144,1280]{1,0:T(8,128)(2,1)S(1)}, u32[]{:S(2)}, u32[]{:S(2)}) collective-permute-start(s16[144,1280]{1,0:T(8,128)(2,1)S(1)} %shard_map.156), channel_id=1, source_target_pairs={{0,1},{1,3},{2,0},{3,5},{4,2},{5,7},{6,4},{7,6},{8,9},{9,11},{10,8... | collective-permute-start | bytes 1105928 | tf_op jit(solution)/shard_map/ppermute | solution.py:579
  35.2 0.9 shard_map.150
  36.1 2.2 %collective-permute-start.4 = (s16[144,1280]{1,0:T(8,128)(2,1)S(1)}, s16[144,1280]{1,0:T(8,128)(2,1)S(1)}, u32[]{:S(2)}, u32[]{:S(2)}) collective-permute-start(s16[144,1280]{1,0:T(8,128)(2,1)S(1)} %shard_map.150), channel_id=1, source_target_pairs={{0,1},{1,3},{2,0},{3,5},{4,2},{5,7},{6,4},{7,6},{8,9},{9,11},{10,8... | collective-permute-start | bytes 1105928 | tf_op jit(solution)/shard_map/ppermute | solution.py:579
  38.3 2.3 %shard_map.153 = (f32[128,1280]{1,0:T(8,128)S(1)}, f32[128,1280]{1,0:T(8,128)S(1)}, f32[128,128]{1,0:T(8,128)S(1)}) custom-call(bf16[128,5376]{1,0:T(8,128)(2,1)S(1)} %copy-done.1, bf16[128,5120]{1,0:T(8,128)(2,1)S(1)} %copy-done.4, bf16[3,5376]{1,0:T(4,128)(2,1)S(1)} %collective-permute-done.halo_ref.refs_0_.refs_11_, f32[4,5376]{1,0:T(4,128)S(1)} %copy-done.2, ...), custom_call_target="tpu_custom_call" | custom-call | flops 2200000000 | bytes 1000 | tf_op jit(solution)/shard_map/pallas_call | solution.py:556
  40.6 0.9 shard_map.157
  41.5 1.3 %collective-permute-start.14 = (s16[144,1280]{1,0:T(8,128)(2,1)S(1)}, s16[144,1280]{1,0:T(8,128)(2,1)S(1)}, u32[]{:S(2)}, u32[]{:S(2)}) collective-permute-start(s16[144,1280]{1,0:T(8,128)(2,1)S(1)} %shard_map.157), channel_id=1, source_target_pairs={{0,1},{1,3},{2,0},{3,5},{4,2},{5,7},{6,4},{7,6},{8,9},{9,11},{10,8... | collective-permute-start | bytes 1105928 | tf_op jit(solution)/shard_map/ppermute | solution.py:579
  42.8 2.3 %shard_map.159 = (f32[128,1280]{1,0:T(8,128)S(1)}, f32[128,1280]{1,0:T(8,128)S(1)}, f32[128,128]{1,0:T(8,128)S(1)}) custom-call(bf16[128,5376]{1,0:T(8,128)(2,1)S(1)} %copy-done.1, bf16[128,5120]{1,0:T(8,128)(2,1)S(1)} %copy-done.4, bf16[3,5376]{1,0:T(4,128)(2,1)S(1)} %collective-permute-done.halo_ref.refs_0_.refs_11_, f32[4,5376]{1,0:T(4,128)S(1)} %copy-done.2, ...), custom_call_target="tpu_custom_call" | custom-call | flops 2200000000 | bytes 1000 | tf_op jit(solution)/shard_map/pallas_call | solution.py:556
  45.2 0.9 shard_map.151
  46.1 0.9 collective-permute-start.5
  47.0 2.5 %shard_map.162 = (f32[128,1280]{1,0:T(8,128)S(1)}, f32[128,1280]{1,0:T(8,128)S(1)}, f32[128,128]{1,0:T(8,128)S(1)}) custom-call(bf16[128,5376]{1,0:T(8,128)(2,1)S(1)} %copy-done.1, bf16[128,5120]{1,0:T(8,128)(2,1)S(1)} %copy-done.4, bf16[3,5376]{1,0:T(4,128)(2,1)S(1)} %collective-permute-done.halo_ref.refs_0_.refs_11_, f32[4,5376]{1,0:T(4,128)S(1)} %copy-done.2, ...), custom_call_target="tpu_custom_call" | custom-call | flops 2200000000 | bytes 1000 | tf_op jit(solution)/shard_map/pallas_call | solution.py:556
  50.2 2.3 %shard_map.163 = (f32[128,1280]{1,0:T(8,128)S(1)}, f32[128,1280]{1,0:T(8,128)S(1)}, f32[128,128]{1,0:T(8,128)S(1)}) custom-call(bf16[128,5376]{1,0:T(8,128)(2,1)S(1)} %copy-done.1, bf16[128,5120]{1,0:T(8,128)(2,1)S(1)} %copy-done.4, bf16[3,5376]{1,0:T(4,128)(2,1)S(1)} %collective-permute-done.halo_ref.refs_0_.refs_11_, f32[4,5376]{1,0:T(4,128)S(1)} %copy-done.2, ...), custom_call_target="tpu_custom_call" | custom-call | flops 2200000000 | bytes 1000 | tf_op jit(solution)/shard_map/pallas_call | solution.py:556
  53.0 0.9 shard_map.158
  54.1 0.9 shard_map.152
  55.0 1.4 %collective-permute-start.6 = (s16[144,1280]{1,0:T(8,128)(2,1)S(1)}, s16[144,1280]{1,0:T(8,128)(2,1)S(1)}, u32[]{:S(2)}, u32[]{:S(2)}) collective-permute-start(s16[144,1280]{1,0:T(8,128)(2,1)S(1)} %shard_map.152), channel_id=1, source_target_pairs={{0,1},{1,3},{2,0},{3,5},{4,2},{5,7},{6,4},{7,6},{8,9},{9,11},{10,8... | collective-permute-start | bytes 1105928 | tf_op jit(solution)/shard_map/ppermute | solution.py:579
  56.4 1.3 %collective-permute-start.15 = (s16[144,1280]{1,0:T(8,128)(2,1)S(1)}, s16[144,1280]{1,0:T(8,128)(2,1)S(1)}, u32[]{:S(2)}, u32[]{:S(2)}) collective-permute-start(s16[144,1280]{1,0:T(8,128)(2,1)S(1)} %shard_map.158), channel_id=1, source_target_pairs={{0,1},{1,3},{2,0},{3,5},{4,2},{5,7},{6,4},{7,6},{8,9},{9,11},{10,8... | collective-permute-start | bytes 1105928 | tf_op jit(solution)/shard_map/ppermute | solution.py:579
  57.7 5.9 %shard_map.160 = (bf16[128,5120]{1,0:T(8,128)(2,1)}, bf16[128,5376]{1,0:T(8,128)(2,1)}, f32[24,5376]{1,0:T(8,128)S(1)}, f32[128,128]{1,0:T(8,128)S(1)}, f32[128,128]{1,0:T(8,128)S(1)}, /*index=5*/f32[8,128]{1,0:T(8,128)S(1)}) custom-call(s32[2]{0:T(128)S(1)} %pad_add_fusion.flag_ref, s16[144,1280]{1,0:T(8,128)(2,1)S(1)} %collective-permute-done.11.previous_ref.refs_0_, ...), custom_call_target="tpu_custom_call" | custom-call | flops 5500000256 | bytes 1000 | tf_op jit(solution)/shard_map/pallas_call | solution.py:556
  63.6 1.2 %collective-permute-done.15.refs_2_ = s16[144,1280]{1,0:T(8,128)(2,1)S(1)} collective-permute-done((s16[144,1280]{1,0:T(8,128)(2,1)S(1)}, s16[144,1280]{1,0:T(8,128)(2,1)S(1)}, u32[]{:S(2)}, u32[]{:S(2)}) %collective-permute-start.15) | collective-permute-done | bytes 368672 | tf_op jit(solution)/shard_map/ppermute | solution.py:579
  64.8 2.1 %collective-permute-start.20 = (s16[144,1280]{1,0:T(8,128)(2,1)S(1)}, s16[144,1280]{1,0:T(8,128)(2,1)S(1)}, u32[]{:S(2)}, u32[]{:S(2)}) collective-permute-start(s16[144,1280]{1,0:T(8,128)(2,1)S(1)} %collective-permute-done.15.refs_2_), channel_id=1, source_target_pairs={{0,1},{1,0},{2,3},{3,2},{4,5},{5,4},{6,7},{7,6},{8,9},{9,8},{10,11... | collective-permute-start | bytes 1105928 | tf_op jit(solution)/shard_map/ppermute | solution.py:579
  66.9 5.9 %shard_map.161 = (bf16[128,5120]{1,0:T(8,128)(2,1)}, bf16[128,5376]{1,0:T(8,128)(2,1)}, f32[24,5376]{1,0:T(8,128)S(1)}, f32[128,128]{1,0:T(8,128)S(1)}, f32[128,128]{1,0:T(8,128)S(1)}, /*index=5*/f32[8,128]{1,0:T(8,128)S(1)}) custom-call(s32[2]{0:T(128)S(1)} %pad_add_fusion.flag_ref, ...), custom_call_target="tpu_custom_call", output_to_operand_aliasing={{0}: (17, {}), {1}: (18, {}), {2}: (19, {})} | custom-call | flops 5500000256 | bytes 1000 | tf_op jit(solution)/shard_map/pallas_call | solution.py:556
  72.9 5.9 %shard_map.164 = (bf16[128,5120]{1,0:T(8,128)(2,1)}, bf16[128,5376]{1,0:T(8,128)(2,1)}, f32[24,5376]{1,0:T(8,128)S(1)}, f32[128,128]{1,0:T(8,128)S(1)}, f32[128,128]{1,0:T(8,128)S(1)}, /*index=5*/f32[8,128]{1,0:T(8,128)S(1)}) custom-call(s32[2]{0:T(128)S(1)} %pad_add_fusion.flag_ref, ...), custom_call_target="tpu_custom_call", output_to_operand_aliasing={{0}: (17, {}), {1}: (18, {}), {2}: (19, {})} | custom-call | flops 5500000256 | bytes 1000 | tf_op jit(solution)/shard_map/pallas_call | solution.py:556
  78.8 5.7 %shard_map.165 = (bf16[128,5120]{1,0:T(8,128)(2,1)}, bf16[128,5376]{1,0:T(8,128)(2,1)}, f32[24,5376]{1,0:T(8,128)S(1)}, f32[128,128]{1,0:T(8,128)S(1)}, f32[128,128]{1,0:T(8,128)S(1)}, /*index=5*/f32[8,128]{1,0:T(8,128)S(1)}) custom-call(s32[2]{0:T(128)S(1)} %pad_add_fusion.flag_ref, ...), custom_call_target="tpu_custom_call", output_to_operand_aliasing={{0}: (17, {}), {1}: (18, {}), {2}: (19, {})} | custom-call | flops 5500000256 | bytes 1000 | tf_op jit(solution)/shard_map/pallas_call | solution.py:556
  84.5 1.1 shard_map.166
  86.1 0.9 collective-permute-done.22
  87.0 1.3 %collective-permute-start.24 = (f32[8,2688]{1,0:T(8,128)S(1)}, f32[8,2688]{1,0:T(8,128)S(1)}, u32[]{:S(2)}, u32[]{:S(2)}) collective-permute-start(f32[8,2688]{1,0:T(8,128)S(1)} %select_add_fusion), channel_id=1, source_target_pairs={{0,16},{8,24},{16,0},{24,8},{1,17},{9,25},{17,1},{25,9},{2,18},{10... | collective-permute-start | bytes 258056 | tf_op jit(solution)/shard_map/ppermute | solution.py:579
  88.3 1.2 %collective-permute-start.25 = (f32[8,2688]{1,0:T(8,128)S(1)}, f32[8,2688]{1,0:T(8,128)S(1)}, u32[]{:S(2)}, u32[]{:S(2)}) collective-permute-start(f32[8,2688]{1,0:T(8,128)S(1)} %select_add_fusion), channel_id=1, source_target_pairs={{0,24},{8,16},{16,8},{24,0},{1,25},{9,17},{17,9},{25,1},{2,26},{10... | collective-permute-start | bytes 258056 | tf_op jit(solution)/shard_map/ppermute | solution.py:579
  89.7 1.1 %collective-permute-done.24 = f32[8,2688]{1,0:T(8,128)S(1)} collective-permute-done((f32[8,2688]{1,0:T(8,128)S(1)}, f32[8,2688]{1,0:T(8,128)S(1)}, u32[]{:S(2)}, u32[]{:S(2)}) %collective-permute-start.24) | collective-permute-done | bytes 86048 | tf_op jit(solution)/shard_map/ppermute | solution.py:579
  90.9 1.7 %collective-permute-done.25 = f32[8,2688]{1,0:T(8,128)S(1)} collective-permute-done((f32[8,2688]{1,0:T(8,128)S(1)}, f32[8,2688]{1,0:T(8,128)S(1)}, u32[]{:S(2)}, u32[]{:S(2)}) %collective-permute-start.25) | collective-permute-done | bytes 86048 | tf_op jit(solution)/shard_map/ppermute | solution.py:579
  92.6 1.5 %collective-permute-done.23 = f32[8,2688]{1,0:T(8,128)S(1)} collective-permute-done((f32[8,2688]{1,0:T(8,128)S(1)}, f32[8,2688]{1,0:T(8,128)S(1)}, u32[]{:S(2)}, u32[]{:S(2)}) %collective-permute-start.23) | collective-permute-done | bytes 86048 | tf_op jit(solution)/shard_map/ppermute | solution.py:579
  94.1 2.5 %collective-permute-start.27 = (f32[8,2688]{1,0:T(8,128)S(1)}, f32[8,2688]{1,0:T(8,128)S(1)}, u32[]{:S(2)}, u32[]{:S(2)}) collective-permute-start(f32[8,2688]{1,0:T(8,128)S(1)} %add_add_fusion), channel_id=1, source_target_pairs={{0,4},{1,5},{2,6},{3,7},{4,0},{5,1},{6,2},{7,3},{8,12},{9,13},{10,... | collective-permute-start | bytes 258056 | tf_op jit(solution)/shard_map/ppermute | solution.py:579
  96.6 1.1 collective-permute-start.28
  97.7 3.7 %collective-permute-start.21 = (f32[3,5376]{1,0:T(4,128)S(1)}, f32[3,5376]{1,0:T(4,128)S(1)}, u32[]{:S(2)}, u32[]{:S(2)}) collective-permute-start(f32[3,5376]{1,0:T(4,128)S(1)} %slice.28), channel_id=1, source_target_pairs={{1,0},{2,1},{3,2},{4,3},{5,4},{6,5},{7,6},{9,8},{10,9},{11,10},{12... | collective-permute-start | bytes 193544 | tf_op jit(solution)/shard_map/ppermute | solution.py:796
  102.2 3.1 %collective-permute-start.29 = (f32[8,2688]{1,0:T(8,128)S(1)}, f32[8,2688]{1,0:T(8,128)S(1)}, u32[]{:S(2)}, u32[]{:S(2)}) collective-permute-start(f32[8,2688]{1,0:T(8,128)S(1)} %add_multiply_fusion), channel_id=1, source_target_pairs={{0,1},{1,0},{2,3},{3,2},{4,5},{5,4},{6,7},{7,6},{8,9},{9,8},{10,11... | collective-permute-start | bytes 258056 | tf_op jit(solution)/shard_map/ppermute | solution.py:579
  105.5 1.8 %shard_map.167 = bf16[128,5376]{1,0:T(8,128)(2,1)} custom-call(bf16[128,5376]{1,0:T(8,128)(2,1)} %get-tuple-element.129.gin_ref, f32[24,5376]{1,0:T(8,128)S(1)} %get-tuple-element.130.misc_ref, f32[3,5376]{1,0:T(4,128)S(1)} %collective-permute-done.21.back_ref, s32[1,128]{1,0:T(1,128)S(1)} %bitcast.22), custom_call_target="tpu_custom_call", output_to_operand_aliasing={{}: (0, {})} | custom-call | flops 1100000000 | bytes 1000 | tf_op jit(solution)/shard_map/pallas_call | solution.py:556
  (94 shorter events, 10.8 us)
Async XLA Ops:
  0.6 1.3 %copy-start = (bf16[128,5376]{1,0:T(8,128)(2,1)S(1)}, bf16[128,5376]{1,0:T(8,128)(2,1)}, u32[]{:S(2)}) copy-start(bf16[128,5376]{1,0:T(8,128)(2,1)} %x_ref.15) | copy-start | bytes 4128772
  2.6 4.9 %copy-start.7 = (f32[128,80]{0,1:T(8,128)S(1)}, f32[128,80]{0,1:T(8,128)}, u32[]{:S(2)}) copy-start(f32[128,80]{0,1:T(8,128)} %param.13) | copy-start | bytes 122884
  2.6 4.9 %copy-start.8 = (f32[80]{0:T(128)S(1)}, f32[80]{0:T(128)}, u32[]{:S(2)}) copy-start(f32[80]{0:T(128)} %param.14) | copy-start | bytes 964
  2.6 4.9 %copy-start.9 = (f32[80]{0:T(128)S(1)}, f32[80]{0:T(128)}, u32[]{:S(2)}) copy-start(f32[80]{0:T(128)} %param.15) | copy-start | bytes 964
  2.6 4.9 %copy-start.10 = (f32[80]{0:T(128)S(1)}, f32[80]{0:T(128)}, u32[]{:S(2)}) copy-start(f32[80]{0:T(128)} %param.16) | copy-start | bytes 964
  2.8 5.7 %collective-permute-start = (bf16[3,5376]{1,0:T(4,128)(2,1)S(1)}, bf16[3,5376]{1,0:T(4,128)(2,1)S(1)}, u32[]{:S(2)}, u32[]{:S(2)}) collective-permute-start(bf16[3,5376]{1,0:T(4,128)(2,1)S(1)} %shard_map.144), channel_id=1, source_target_pairs={{0,1},{1,2},{2,3},{3,4},{4,5},{5,6},{6,7},{8,9},{9,10},{10,11},{11... | collective-permute-start | bytes 96776 | tf_op jit(solution)/shard_map/ppermute | solution.py:656
  7.5 1.3 %copy-start.1 = (bf16[128,5376]{1,0:T(8,128)(2,1)S(1)}, bf16[128,5376]{1,0:T(8,128)(2,1)}, u32[]{:S(2)}) copy-start(bf16[128,5376]{1,0:T(8,128)(2,1)} %x_ref.15) | copy-start | bytes 4128772
  7.5 1.3 %copy-start.2 = (f32[4,5376]{1,0:T(4,128)S(1)}, f32[4,5376]{1,0:T(4,128)}, u32[]{:S(2)}) copy-start(f32[4,5376]{1,0:T(4,128)} %w_ref.13) | copy-start | bytes 258052
  7.5 1.7 %copy-start.3 = (bf16[128,5120]{1,0:T(8,128)(2,1)S(1)}, bf16[128,5120]{1,0:T(8,128)(2,1)}, u32[]{:S(2)}) copy-start(bf16[128,5120]{1,0:T(8,128)(2,1)} %refs_9_.7) | copy-start | bytes 3932164
  13.9 0.9 copy-start.17
  15.6 11.2 %collective-permute-start.1 = (f32[136,1280]{1,0:T(8,128)}, f32[136,1280]{1,0:T(8,128)}, u32[]{:S(2)}, u32[]{:S(2)}) collective-permute-start(f32[136,1280]{1,0:T(8,128)} %get-tuple-element.70.own_ref), channel_id=1, source_target_pairs={{0,1},{1,0},{2,3},{3,2},{4,5},{5,4},{6,7},{7,6},{8,9},{9,8},{10,11... | collective-permute-start | bytes 2088968 | tf_op jit(solution)/shard_map/ppermute | solution.py:579
  15.6 7.2 %collective-permute-start.10 = (f32[136,1280]{1,0:T(8,128)}, f32[136,1280]{1,0:T(8,128)}, u32[]{:S(2)}, u32[]{:S(2)}) collective-permute-start(f32[136,1280]{1,0:T(8,128)} %get-tuple-element.81.own_ref), channel_id=1, source_target_pairs={{0,1},{1,0},{2,3},{3,2},{4,5},{5,4},{6,7},{7,6},{8,9},{9,8},{10,11... | collective-permute-start | bytes 2088968 | tf_op jit(solution)/shard_map/ppermute | solution.py:579
  19.6 0.9 copy-start.5
  20.4 0.9 copy-start.13
  22.1 7.6 %collective-permute-start.12 = (f32[136,1280]{1,0:T(8,128)}, f32[136,1280]{1,0:T(8,128)}, u32[]{:S(2)}, u32[]{:S(2)}) collective-permute-start(f32[136,1280]{1,0:T(8,128)} %get-tuple-element.85.own_ref), channel_id=1, source_target_pairs={{0,1},{1,0},{2,3},{3,2},{4,5},{5,4},{6,7},{7,6},{8,9},{9,8},{10,11... | collective-permute-start | bytes 2088968 | tf_op jit(solution)/shard_map/ppermute | solution.py:579
  22.2 12.1 %collective-permute-start.3 = (f32[136,1280]{1,0:T(8,128)}, f32[136,1280]{1,0:T(8,128)S(1)}, u32[]{:S(2)}, u32[]{:S(2)}) collective-permute-start(f32[136,1280]{1,0:T(8,128)} %copy-done.5), channel_id=1, source_target_pairs={{0,1},{1,0},{2,3},{3,2},{4,5},{5,4},{6,7},{7,6},{8,9},{9,8},{10,11... | collective-permute-start | bytes 2088968 | tf_op jit(solution)/shard_map/ppermute | solution.py:579
  22.8 1.1 copy-start.20
  23.9 3.0 %copy-start.18 = (f32[128,1280]{1,0:T(8,128)S(1)}, f32[128,1280]{1,0:T(8,128)}, u32[]{:S(2)}) copy-start(f32[128,1280]{1,0:T(8,128)} %copy-done.17) | copy-start | bytes 1966084
  25.4 5.8 %collective-permute-start.11 = (s16[144,1280]{1,0:T(8,128)(2,1)S(1)}, s16[144,1280]{1,0:T(8,128)(2,1)S(1)}, u32[]{:S(2)}, u32[]{:S(2)}) collective-permute-start(s16[144,1280]{1,0:T(8,128)(2,1)S(1)} %get-tuple-element.82), channel_id=1, source_target_pairs={{0,1},{1,3},{2,0},{3,5},{4,2},{5,7},{6,4},{7,6},{8,9},{9,11},{10,8... | collective-permute-start | bytes 1105928 | tf_op jit(solution)/shard_map/ppermute | solution.py:579
  26.8 2.9 %copy-start.16 = (f32[128,1280]{1,0:T(8,128)S(1)}, f32[128,1280]{1,0:T(8,128)}, u32[]{:S(2)}) copy-start(f32[128,1280]{1,0:T(8,128)} %copy-done.15) | copy-start | bytes 1966084
  28.4 6.8 %collective-permute-start.2 = (s16[144,1280]{1,0:T(8,128)(2,1)S(1)}, s16[144,1280]{1,0:T(8,128)(2,1)S(1)}, u32[]{:S(2)}, u32[]{:S(2)}) collective-permute-start(s16[144,1280]{1,0:T(8,128)(2,1)S(1)} %get-tuple-element.71), channel_id=1, source_target_pairs={{0,1},{1,3},{2,0},{3,5},{4,2},{5,7},{6,4},{7,6},{8,9},{9,11},{10,8... | collective-permute-start | bytes 1105928 | tf_op jit(solution)/shard_map/ppermute | solution.py:579
  31.2 3.1 %copy-start.6 = (f32[136,1280]{1,0:T(8,128)S(1)}, f32[136,1280]{1,0:T(8,128)}, u32[]{:S(2)}) copy-start(f32[136,1280]{1,0:T(8,128)} %copy-done.5) | copy-start | bytes 2088964
  31.2 3.1 %copy-start.14 = (f32[128,1280]{1,0:T(8,128)S(1)}, f32[128,1280]{1,0:T(8,128)}, u32[]{:S(2)}) copy-start(f32[128,1280]{1,0:T(8,128)} %copy-done.13) | copy-start | bytes 1966084
  32.1 8.5 %collective-permute-start.13 = (s16[144,1280]{1,0:T(8,128)(2,1)S(1)}, s16[144,1280]{1,0:T(8,128)(2,1)S(1)}, u32[]{:S(2)}, u32[]{:S(2)}) collective-permute-start(s16[144,1280]{1,0:T(8,128)(2,1)S(1)} %shard_map.156), channel_id=1, source_target_pairs={{0,1},{1,3},{2,0},{3,5},{4,2},{5,7},{6,4},{7,6},{8,9},{9,11},{10,8... | collective-permute-start | bytes 1105928 | tf_op jit(solution)/shard_map/ppermute | solution.py:579
  35.2 3.1 %copy-start.4 = (bf16[128,5120]{1,0:T(8,128)(2,1)S(1)}, bf16[128,5120]{1,0:T(8,128)(2,1)}, u32[]{:S(2)}) copy-start(bf16[128,5120]{1,0:T(8,128)(2,1)} %refs_9_.7) | copy-start | bytes 3932164
  36.1 9.1 %collective-permute-start.4 = (s16[144,1280]{1,0:T(8,128)(2,1)S(1)}, s16[144,1280]{1,0:T(8,128)(2,1)S(1)}, u32[]{:S(2)}, u32[]{:S(2)}) collective-permute-start(s16[144,1280]{1,0:T(8,128)(2,1)S(1)} %shard_map.150), channel_id=1, source_target_pairs={{0,1},{1,3},{2,0},{3,5},{4,2},{5,7},{6,4},{7,6},{8,9},{9,11},{10,8... | collective-permute-start | bytes 1105928 | tf_op jit(solution)/shard_map/ppermute | solution.py:579
  41.5 8.6 %collective-permute-start.14 = (s16[144,1280]{1,0:T(8,128)(2,1)S(1)}, s16[144,1280]{1,0:T(8,128)(2,1)S(1)}, u32[]{:S(2)}, u32[]{:S(2)}) collective-permute-start(s16[144,1280]{1,0:T(8,128)(2,1)S(1)} %shard_map.157), channel_id=1, source_target_pairs={{0,1},{1,3},{2,0},{3,5},{4,2},{5,7},{6,4},{7,6},{8,9},{9,11},{10,8... | collective-permute-start | bytes 1105928 | tf_op jit(solution)/shard_map/ppermute | solution.py:579
  46.1 7.8 %collective-permute-start.5 = (s16[144,1280]{1,0:T(8,128)(2,1)S(1)}, s16[144,1280]{1,0:T(8,128)(2,1)S(1)}, u32[]{:S(2)}, u32[]{:S(2)}) collective-permute-start(s16[144,1280]{1,0:T(8,128)(2,1)S(1)} %shard_map.151), channel_id=1, source_target_pairs={{0,1},{1,3},{2,0},{3,5},{4,2},{5,7},{6,4},{7,6},{8,9},{9,11},{10,8... | collective-permute-start | bytes 1105928 | tf_op jit(solution)/shard_map/ppermute | solution.py:579
  49.5 5.5 %collective-permute-start.16 = (s16[144,1280]{1,0:T(8,128)(2,1)S(1)}, s16[144,1280]{1,0:T(8,128)(2,1)S(1)}, u32[]{:S(2)}, u32[]{:S(2)}) collective-permute-start(s16[144,1280]{1,0:T(8,128)(2,1)S(1)} %collective-permute-done.11.previous_ref.refs_0_), channel_id=1, source_target_pairs={{0,1},{1,0},{2,3},{3,2},{4,5},{5,4},{6,7},{7,6},{8,9},{9,8},{10,11... | collective-permute-start | bytes 1105928 | tf_op jit(solution)/shard_map/ppermute | solution.py:579
  49.6 6.8 %collective-permute-start.17 = (s16[144,1280]{1,0:T(8,128)(2,1)S(1)}, s16[144,1280]{1,0:T(8,128)(2,1)S(1)}, u32[]{:S(2)}, u32[]{:S(2)}) collective-permute-start(s16[144,1280]{1,0:T(8,128)(2,1)S(1)} %collective-permute-done.13.previous_ref.refs_1_.refs_0_), channel_id=1, source_target_pairs={{0,1},{1,0},{2,3},{3,2},{4,5},{5,4},{6,7},{7,6},{8,9},{9,8},{10,11... | collective-permute-start | bytes 1105928 | tf_op jit(solution)/shard_map/ppermute | solution.py:579
  50.1 7.6 %collective-permute-start.18 = (s16[144,1280]{1,0:T(8,128)(2,1)S(1)}, s16[144,1280]{1,0:T(8,128)(2,1)S(1)}, u32[]{:S(2)}, u32[]{:S(2)}) collective-permute-start(s16[144,1280]{1,0:T(8,128)(2,1)S(1)} %collective-permute-done.14.previous_ref.refs_2_.refs_1_), channel_id=1, source_target_pairs={{0,1},{1,0},{2,3},{3,2},{4,5},{5,4},{6,7},{7,6},{8,9},{9,8},{10,11... | collective-permute-start | bytes 1105928 | tf_op jit(solution)/shard_map/ppermute | solution.py:579
  52.5 14.4 %collective-permute-start.7 = (s16[144,1280]{1,0:T(8,128)(2,1)S(1)}, s16[144,1280]{1,0:T(8,128)(2,1)S(1)}, u32[]{:S(2)}, u32[]{:S(2)}) collective-permute-start(s16[144,1280]{1,0:T(8,128)(2,1)S(1)} %collective-permute-done.2.previous_ref.refs_0_), channel_id=1, source_target_pairs={{0,1},{1,0},{2,3},{3,2},{4,5},{5,4},{6,7},{7,6},{8,9},{9,8},{10,11... | collective-permute-start | bytes 1105928 | tf_op jit(solution)/shard_map/ppermute | solution.py:579
  53.9 13.0 %collective-permute-start.8 = (s16[144,1280]{1,0:T(8,128)(2,1)S(1)}, s16[144,1280]{1,0:T(8,128)(2,1)S(1)}, u32[]{:S(2)}, u32[]{:S(2)}) collective-permute-start(s16[144,1280]{1,0:T(8,128)(2,1)S(1)} %collective-permute-done.4.previous_ref.refs_1_.refs_0_), channel_id=1, source_target_pairs={{0,1},{1,0},{2,3},{3,2},{4,5},{5,4},{6,7},{7,6},{8,9},{9,8},{10,11... | collective-permute-start | bytes 1105928 | tf_op jit(solution)/shard_map/ppermute | solution.py:579
  55.0 17.8 %collective-permute-start.6 = (s16[144,1280]{1,0:T(8,128)(2,1)S(1)}, s16[144,1280]{1,0:T(8,128)(2,1)S(1)}, u32[]{:S(2)}, u32[]{:S(2)}) collective-permute-start(s16[144,1280]{1,0:T(8,128)(2,1)S(1)} %shard_map.152), channel_id=1, source_target_pairs={{0,1},{1,3},{2,0},{3,5},{4,2},{5,7},{6,4},{7,6},{8,9},{9,11},{10,8... | collective-permute-start | bytes 1105928 | tf_op jit(solution)/shard_map/ppermute | solution.py:579
  56.4 8.4 %collective-permute-start.15 = (s16[144,1280]{1,0:T(8,128)(2,1)S(1)}, s16[144,1280]{1,0:T(8,128)(2,1)S(1)}, u32[]{:S(2)}, u32[]{:S(2)}) collective-permute-start(s16[144,1280]{1,0:T(8,128)(2,1)S(1)} %shard_map.158), channel_id=1, source_target_pairs={{0,1},{1,3},{2,0},{3,5},{4,2},{5,7},{6,4},{7,6},{8,9},{9,11},{10,8... | collective-permute-start | bytes 1105928 | tf_op jit(solution)/shard_map/ppermute | solution.py:579
  57.7 9.2 %collective-permute-start.9 = (s16[144,1280]{1,0:T(8,128)(2,1)S(1)}, s16[144,1280]{1,0:T(8,128)(2,1)S(1)}, u32[]{:S(2)}, u32[]{:S(2)}) collective-permute-start(s16[144,1280]{1,0:T(8,128)(2,1)S(1)} %collective-permute-done.5.previous_ref.refs_2_.refs_1_), channel_id=1, source_target_pairs={{0,1},{1,0},{2,3},{3,2},{4,5},{5,4},{6,7},{7,6},{8,9},{9,8},{10,11... | collective-permute-start | bytes 1105928 | tf_op jit(solution)/shard_map/ppermute | solution.py:579
  64.8 8.1 %collective-permute-start.20 = (s16[144,1280]{1,0:T(8,128)(2,1)S(1)}, s16[144,1280]{1,0:T(8,128)(2,1)S(1)}, u32[]{:S(2)}, u32[]{:S(2)}) collective-permute-start(s16[144,1280]{1,0:T(8,128)(2,1)S(1)} %collective-permute-done.15.refs_2_), channel_id=1, source_target_pairs={{0,1},{1,0},{2,3},{3,2},{4,5},{5,4},{6,7},{7,6},{8,9},{9,8},{10,11... | collective-permute-start | bytes 1105928 | tf_op jit(solution)/shard_map/ppermute | solution.py:579
  72.8 6.0 %collective-permute-start.19 = (s16[144,1280]{1,0:T(8,128)(2,1)S(1)}, s16[144,1280]{1,0:T(8,128)(2,1)S(1)}, u32[]{:S(2)}, u32[]{:S(2)}) collective-permute-start(s16[144,1280]{1,0:T(8,128)(2,1)S(1)} %collective-permute-done.6.refs_2_), channel_id=1, source_target_pairs={{0,1},{1,0},{2,3},{3,2},{4,5},{5,4},{6,7},{7,6},{8,9},{9,8},{10,11... | collective-permute-start | bytes 1105928 | tf_op jit(solution)/shard_map/ppermute | solution.py:579
  85.5 20.0 %copy-start.12 = (s32[128]{0:T(128)S(1)}, s32[128]{0:T(128)}, u32[]{:S(2)}) copy-start(s32[128]{0:T(128)} %param.10) | copy-start | bytes 1540
  85.5 1.5 %collective-permute-start.22 = (f32[8,2688]{1,0:T(8,128)S(1)}, f32[8,2688]{1,0:T(8,128)S(1)}, u32[]{:S(2)}, u32[]{:S(2)}) collective-permute-start(f32[8,2688]{1,0:T(8,128)S(1)} %slice_select_fusion), channel_id=1, source_target_pairs={{0,1},{1,0},{2,3},{3,2},{4,5},{5,4},{6,7},{7,6},{8,9},{9,8},{10,11... | collective-permute-start | bytes 258056 | tf_op jit(solution)/shard_map/ppermute | solution.py:579
  87.0 3.8 %collective-permute-start.24 = (f32[8,2688]{1,0:T(8,128)S(1)}, f32[8,2688]{1,0:T(8,128)S(1)}, u32[]{:S(2)}, u32[]{:S(2)}) collective-permute-start(f32[8,2688]{1,0:T(8,128)S(1)} %select_add_fusion), channel_id=1, source_target_pairs={{0,16},{8,24},{16,0},{24,8},{1,17},{9,25},{17,1},{25,9},{2,18},{10... | collective-permute-start | bytes 258056 | tf_op jit(solution)/shard_map/ppermute | solution.py:579
  88.3 4.2 %collective-permute-start.25 = (f32[8,2688]{1,0:T(8,128)S(1)}, f32[8,2688]{1,0:T(8,128)S(1)}, u32[]{:S(2)}, u32[]{:S(2)}) collective-permute-start(f32[8,2688]{1,0:T(8,128)S(1)} %select_add_fusion), channel_id=1, source_target_pairs={{0,24},{8,16},{16,8},{24,0},{1,25},{9,17},{17,9},{25,1},{2,26},{10... | collective-permute-start | bytes 258056 | tf_op jit(solution)/shard_map/ppermute | solution.py:579
  89.5 4.5 %collective-permute-start.23 = (f32[8,2688]{1,0:T(8,128)S(1)}, f32[8,2688]{1,0:T(8,128)S(1)}, u32[]{:S(2)}, u32[]{:S(2)}) collective-permute-start(f32[8,2688]{1,0:T(8,128)S(1)} %select_add_fusion), channel_id=1, source_target_pairs={{0,8},{8,0},{16,24},{24,16},{1,9},{9,1},{17,25},{25,17},{2,10},{10... | collective-permute-start | bytes 258056 | tf_op jit(solution)/shard_map/ppermute | solution.py:579
  94.1 7.3 %collective-permute-start.27 = (f32[8,2688]{1,0:T(8,128)S(1)}, f32[8,2688]{1,0:T(8,128)S(1)}, u32[]{:S(2)}, u32[]{:S(2)}) collective-permute-start(f32[8,2688]{1,0:T(8,128)S(1)} %add_add_fusion), channel_id=1, source_target_pairs={{0,4},{1,5},{2,6},{3,7},{4,0},{5,1},{6,2},{7,3},{8,12},{9,13},{10,... | collective-permute-start | bytes 258056 | tf_op jit(solution)/shard_map/ppermute | solution.py:579
  96.6 5.6 %collective-permute-start.28 = (f32[8,2688]{1,0:T(8,128)S(1)}, f32[8,2688]{1,0:T(8,128)S(1)}, u32[]{:S(2)}, u32[]{:S(2)}) collective-permute-start(f32[8,2688]{1,0:T(8,128)S(1)} %add_add_fusion), channel_id=1, source_target_pairs={{0,6},{1,7},{2,4},{3,5},{4,2},{5,3},{6,0},{7,1},{8,14},{9,15},{10,... | collective-permute-start | bytes 258056 | tf_op jit(solution)/shard_map/ppermute | solution.py:579
  97.7 4.6 %collective-permute-start.26 = (f32[8,2688]{1,0:T(8,128)S(1)}, f32[8,2688]{1,0:T(8,128)S(1)}, u32[]{:S(2)}, u32[]{:S(2)}) collective-permute-start(f32[8,2688]{1,0:T(8,128)S(1)} %add_add_fusion), channel_id=1, source_target_pairs={{0,2},{1,3},{2,0},{3,1},{4,6},{5,7},{6,4},{7,5},{8,10},{9,11},{10,... | collective-permute-start | bytes 258056 | tf_op jit(solution)/shard_map/ppermute | solution.py:579
  97.7 7.9 %collective-permute-start.21 = (f32[3,5376]{1,0:T(4,128)S(1)}, f32[3,5376]{1,0:T(4,128)S(1)}, u32[]{:S(2)}, u32[]{:S(2)}) collective-permute-start(f32[3,5376]{1,0:T(4,128)S(1)} %slice.28), channel_id=1, source_target_pairs={{1,0},{2,1},{3,2},{4,3},{5,4},{6,5},{7,6},{9,8},{10,9},{11,10},{12... | collective-permute-start | bytes 193544 | tf_op jit(solution)/shard_map/ppermute | solution.py:796
  102.2 5.1 %collective-permute-start.29 = (f32[8,2688]{1,0:T(8,128)S(1)}, f32[8,2688]{1,0:T(8,128)S(1)}, u32[]{:S(2)}, u32[]{:S(2)}) collective-permute-start(f32[8,2688]{1,0:T(8,128)S(1)} %add_multiply_fusion), channel_id=1, source_target_pairs={{0,1},{1,0},{2,3},{3,2},{4,5},{5,4},{6,7},{7,6},{8,9},{9,8},{10,11... | collective-permute-start | bytes 258056 | tf_op jit(solution)/shard_map/ppermute | solution.py:579
  (4 other events, 3.1 us)

commit v2 on v1

--- a/solution.py
+++ b/solution.py
@@ -25,7 +25,11 @@
 BC = 2 * STATE
 BC_AT = INNER // BC
 FAR = -1e30
+STATES, SMALL = 0, 256
+BC_ACT, BC_SLOPE, SCORES, SMALLS = 0, 256, 512, 640
+WORK_ROWS = 3328
 CODE = 32766.0
+THIRD = CH // 3
 PER = CHUNK // HEAD_DIM
 
 F32 = jnp.float32
@@ -35,7 +39,6 @@
 ACROSS = ((1,), (1,))
 ANY = pl.BlockSpec(memory_space=pl.ANY)
 HBM = pl.BlockSpec(memory_space=pltpu.HBM)
-SMEM = pl.BlockSpec(memory_space=pltpu.SMEM)
 VMEM_LIMIT = 24 * 1024 * 1024
 
 MASK, ENTRY, LEAVE, PULL, RATE, DECAY, RUN, FAR_AT, ROW, SMASK = range(0, 1280, 128)
@@ -105,6 +108,13 @@
         made = pltpu.make_async_copy(source, target, self.sems.at[self.used])
         self.used += 1
         return made
+
+
+def position(hops):
+    index = lax.axis_index("seq")
+    core = lax.rem(index, 2)
+    chip = lax.div(index, 2)
+    return core, jnp.where(core == 1, chip, hops - chip)
 
 
 def at(first, width=CHUNK):
@@ -204,72 +214,63 @@
     )
 
 
-def local_kernel(turn, flag_ref, x_ref, halo_ref, w_ref, b_ref, cot_ref, tab_ref, *refs):
-    lead = turn == 0
-    refs = list(refs)
-    if lead:
-        bch_ref, bcw_ref, bcb_ref = refs[:3]
-        refs = refs[3:]
-    else:
-        turned_ref = refs.pop(0)
-    send_refs, mine_refs = refs[:STREAMS], refs[STREAMS : 2 * STREAMS]
-    if lead:
-        bca_ref, bcs_ref, turned_ref, scores_ref = refs[2 * STREAMS : 4 + 2 * STREAMS]
-    xb, cb, nb, mb, ext_ref, bx, in_sems, out_sems = refs[-8:]
+def local_kernel(x_ref, halo_ref, w_ref, b_ref, cot_ref, tab_ref, *refs):
+    send_refs = refs[:PIECES]
+    work_ref = refs[PIECES]
+    xb, cb, nb, mb, sb, ext_ref, in_sems, out_sems = refs[-8:]
     count = xb.shape[0]
     come, go = Flow(in_sems), Flow(out_sems)
-    if lead:
-        first = come.copy(x_ref.at[:, at(INNER, BC)], bx)
-        first.start()
+    first = come.copy(x_ref.at[:, at(INNER, BC)], xb.at[:, at(INNER, BC)])
+    first.start()
     arriving, leaving = [], []
-    for stream in range(STREAMS):
-        cols, whole_cols = at(stream * WIDTH, WIDTH), at(turn * SPAN + stream * WIDTH, WIDTH)
+    for piece in range(PIECES):
+        cols = at(piece * WIDTH, WIDTH)
         pair = (
-            come.copy(x_ref.at[:, whole_cols], xb.at[:, cols]),
-            come.copy(cot_ref.at[:, whole_cols], cb.at[:, cols]),
+            come.copy(x_ref.at[:, cols], xb.at[:, cols]),
+            come.copy(cot_ref.at[:, cols], cb.at[:, cols]),
         )
         for copy in pair:
             copy.start()
         arriving.append(pair)
     mask = columns(tab_ref[MASK : MASK + count, :], CHUNK)
 
-    def load(cols, source, halo):
-        ext_ref[8 : 8 + count, cols] = source.astype(F32)
-        ext_ref[8 - CONV + 1 : 8, cols] = halo.astype(F32)
-        return taps_of(ext_ref, cols, count, mask)
-
-    if lead:
-        first.wait()
-        act, slope = activate(load(at(SPAN, BC), bx[...], bch_ref[...]), at(0), bcw_ref, bcb_ref)
-        bca_ref[...] = act
-        bcs_ref[...] = slope
-        turned = rows(act[:, :STATE].T, act[:, STATE:].T)
-        turned_ref[...] = turned
-        scores_ref[...] = scores_of(act)
-    else:
-        turned = turned_ref[...]
+    def act_of(cols):
+        ext_ref[8 : 8 + count, cols] = xb[:, cols].astype(F32)
+        ext_ref[8 - CONV + 1 : 8, cols] = halo_ref[:, cols].astype(F32)
+        return activate(taps_of(ext_ref, cols, count, mask), cols, w_ref, b_ref)
+
+    first.wait()
+    act, slope = act_of(at(INNER, BC))
+    sb[:, at(BC_ACT)] = act
+    sb[:, at(BC_SLOPE)] = slope
+    sb[:, at(SCORES, 128)] = scores_of(act)
+    copy = go.copy(sb, work_ref.at[at(SMALL, count), at(0, SMALLS)])
+    copy.start()
+    leaving.append(copy)
+    turned = rows(act[:, :STATE].T, act[:, STATE:].T)
     keys, reads = halves(turned[:STATE, :]), halves(turned[STATE:, :])
     keys_both, reads_both = lanes(*keys), lanes(*reads)
     entry, leave = tab_ref[ENTRY : ENTRY + count, :], tab_ref[LEAVE : LEAVE + count, :]
-    first_core = flag_ref[0] == 0
-    for stream in range(STREAMS):
-        for copy in arriving[stream]:
+    first_core = lax.rem(lax.axis_index("seq"), 2) == 0
+    for piece in range(PIECES):
+        for copy in arriving[piece]:
             copy.wait()
-        for start in range(stream * WIDTH, (stream + 1) * WIDTH, CHUNK):
+        for start in range(piece * WIDTH, (piece + 1) * WIDTH, CHUNK):
             cols = at(start)
-            head = (turn * SPAN + start) // HEAD_DIM
-            taps = load(cols, xb[:, cols], halo_ref[:, cols])
-            act, _ = activate(taps, cols, w_ref, b_ref)
+            head = start // HEAD_DIM
+            act, _ = act_of(cols)
             e = by_head(entry, head, PER)
             lx_high, lx_low = halves(act * by_head(leave, head, PER))
             ey_high, ey_low = halves(cb[:, cols].astype(F32) * e)
             state = mm(keys_both, rows(lx_high, lx_high)) + mm(keys[0], lx_low)
             adjoint = mm(reads_both, rows(ey_high, ey_high)) + mm(reads[0], ey_low)
             nb[:STATE, cols] = jnp.where(first_core, state, adjoint)
-            mb[:, cols] = jnp.where(first_core, adjoint, state)
-            nb[STATE:, cols] = jnp.broadcast_to(e[count - 1 : count, :], (8, CHUNK))
-        cols = at(stream * WIDTH, WIDTH)
-        for source, target in ((nb, send_refs[stream]), (mb, mine_refs[stream])):
+            mb[:STATE, cols] = jnp.where(first_core, adjoint, state)
+            through = jnp.broadcast_to(e[count - 1 : count, :], (8, CHUNK))
+            nb[STATE:, cols] = through
+            mb[STATE:, cols] = through
+        cols = at(piece * WIDTH, WIDTH)
+        for source, target in ((nb, send_refs[piece]), (mb, work_ref.at[at(STATES, STATE + 8), cols])):
             copy = go.copy(source.at[:, cols], target)
             copy.start()
             leaving.append(copy)
@@ -291,49 +292,48 @@
     return rows(codes, tail).astype(I16)
 
 
-def chip_kernel(lead, mine_ref, met_ref, own_ref, *refs):
+def chip_kernel(piece, work_ref, met_ref, *refs):
     chip_ref = refs[0]
-    mb, eb, ob, sem = refs[-4:]
+    mb, eb, sem = refs[-3:]
     come = Flow(sem)
-    copies = [
-        come.copy(mine_ref, mb),
-        come.copy(met_ref, eb),
-        come.copy(own_ref.at[pl.ds(STATE, 8), :], ob),
-    ]
+    mine = work_ref.at[at(STATES, STATE + 8), at(piece * WIDTH, WIDTH)]
+    copies = [come.copy(mine, mb), come.copy(met_ref, eb)]
     for copy in copies:
         copy.start()
     for copy in copies:
         copy.wait()
     for start in range(0, WIDTH, CHUNK):
         cols = at(start)
-        own = ob[0:1, cols]
-        value = mb[:, cols] + own * eb[:STATE, cols]
+        own = mb[STATE : STATE + 1, cols]
+        value = mb[:STATE, cols] + own * eb[:STATE, cols]
         chip_ref[:STATE, cols] = value
         chip_ref[STATE:, cols] = own * eb[STATE:, cols]
-        if lead:
+        if piece < STREAMS:
             refs[1][:, cols] = encode(value)
 
 
-def hop_kernel(pick_ref, previous_ref, *refs):
+def hop_kernel(turn, hops, previous_ref, *refs):
     chip_refs, out_ref = refs[:-1], refs[-1]
+    _, place = position(hops)
     for start in range(0, WIDTH, CHUNK):
         cols = at(start)
         chip = chip_refs[0][:, cols]
         for i, ref in enumerate(chip_refs[1:]):
-            chip = jnp.where(pick_ref[0] > i, ref[:, cols], chip)
-        before = jnp.where(pick_ref[1] == 0, 0.0, decode(previous_ref[:, cols]))
+            chip = jnp.where(turn - place > i, ref[:, cols], chip)
+        before = jnp.where(place == 0, 0.0, decode(previous_ref[:, cols]))
         out_ref[:, cols] = encode(chip[:STATE, :] + chip[STATE : STATE + 1, :] * before)
 
 
 def within_kernel(
-    piece, x_ref, cot_ref, halo_ref, w_ref, b_ref, tab_ref, scores_ref, y_ref, dx_ref, dscores_ref, *refs
+    piece, x_ref, cot_ref, work_ref, halo_ref, w_ref, b_ref, tab_ref, y_ref, dx_ref, dscores_ref, *refs
 ):
-    xb, cb, yb, db, ext_ref, in_sems, out_sems = refs
+    xb, cb, sb, yb, db, ext_ref, in_sems, out_sems = refs
     count = xb.shape[0]
     come, go = Flow(in_sems), Flow(out_sems)
     copies = (
         come.copy(x_ref.at[:, at(piece * WIDTH, WIDTH)], xb),
         come.copy(cot_ref.at[:, at(piece * WIDTH, WIDTH)], cb),
+        come.copy(work_ref.at[at(SMALL, count), at(SCORES, count)], sb),
     )
     for copy in copies:
         copy.start()
@@ -341,7 +341,7 @@
     for copy in copies:
         copy.wait()
     run = tab_ref[RUN : RUN + count, :]
-    far, scores = tab_ref[FAR_AT : FAR_AT + count, :], scores_ref[...]
+    far, scores = tab_ref[FAR_AT : FAR_AT + count, :], sb[...]
     left = iota((count, PAIR), 1) < HEAD_DIM
     total = jnp.zeros((count, count), F32)
     zero = jnp.zeros((count, PAIR), BF16)
@@ -400,16 +400,18 @@
     z_ref[8 + count : 16 + count, :] = jnp.zeros((8, z_ref.shape[1]), F32)
 
 
-def finish_kernel(piece, hops, flag_ref, *refs):
+def finish_kernel(piece, hops, *refs):
     incs, exchs = refs[:hops], refs[hops : 2 * hops]
     refs = refs[2 * hops :]
-    met_ref, y_ref, dx_ref, cot_ref, x_ref, halo_ref, w_ref, b_ref, tab_ref, bc_ref = refs[:10]
-    out_ref, gin_ref, misc_ref, dreads_ref, dkeys_ref, scal_ref = refs[-20:-14]
-    ib, hb, eb, yb, db, cb, xb, ob, gb, nb, ext_ref, z_ref, in_sems, out_sems = refs[-14:]
+    met_ref, work_ref, y_ref, dx_ref, cot_ref, x_ref, halo_ref, w_ref, b_ref, tab_ref = refs[:10]
+    out_ref, gin_ref, misc_ref, dreads_ref, dkeys_ref, scal_ref = refs[-21:-15]
+    ib, hb, eb, bc, yb, db, cb, xb, ob, gb, nb, ext_ref, z_ref, in_sems, out_sems = refs[-15:]
     count = xb.shape[0]
     come, go = Flow(in_sems), Flow(out_sems)
     base = piece * WIDTH
-    place = flag_ref[1]
+    core, place = position(hops)
+    first = come.copy(work_ref.at[at(SMALL, count), at(BC_ACT)], bc)
+    first.start()
     choices = []
     for here, sources, buffer in ((place, incs, ib), (hops - place, exchs, hb)):
         sem = come.used
@@ -438,11 +440,12 @@
             copy.start()
         arriving.append(group)
     clear_edges(z_ref, count)
-    keys, reads = halves(bc_ref[:, :STATE]), halves(bc_ref[:, STATE:])
+    first.wait()
+    keys, reads = halves(bc[:, :STATE]), halves(bc[:, STATE:])
     keys_both, reads_both = lanes(*keys), lanes(*reads)
     entry, leave = tab_ref[ENTRY : ENTRY + count, :], tab_ref[LEAVE : LEAVE + count, :]
     skip = tab_ref[SKIP : SKIP + 1, :]
-    first_core = flag_ref[0] == 0
+    first_core = core == 0
     mask = columns(tab_ref[MASK : MASK + count, :], CHUNK)
     smask = columns(tab_ref[SMASK : SMASK + count + 8, :], CHUNK)
     dreads = jnp.zeros((count, STATE), F32)
@@ -510,10 +513,14 @@
         copy.wait()
 
 
-def final_kernel(x_ref, halo_ref, w_ref, tab_ref, bc_ref, slope_ref, *refs):
-    gin_ref, misc_ref, ext_ref, z_ref = refs[-4:]
+def final_kernel(x_ref, halo_ref, w_ref, tab_ref, work_ref, *refs):
+    gin_ref, misc_ref, packed_ref, ext_ref, z_ref, sb, gb, sem = refs[-8:]
+    gathered = pltpu.make_async_copy(refs[-9].at[at(16, 8), at(0, INNER)], gb, sem.at[1])
+    gathered.start()
     parts = refs[: 4 * PIECES]
     count = x_ref.shape[0]
+    copy = pltpu.make_async_copy(work_ref.at[at(SMALL, count), at(0, SCORES)], sb, sem.at[0])
+    copy.start()
     ext_ref[8 : 8 + count, :] = x_ref[...].astype(F32)
     ext_ref[8 - CONV + 1 : 8, :] = halo_ref[...].astype(F32)
     clear_edges(z_ref, count)
@@ -524,16 +531,24 @@
             value = value + parts[kind * PIECES + piece][...]
         total.append(value)
     dreads, dkeys, dscores, scal = total
-    keys, reads = bc_ref[:, :STATE], bc_ref[:, STATE:]
+    copy.wait()
+    keys, reads = sb[:, at(BC_ACT, STATE)], sb[:, at(BC_ACT + STATE, STATE)]
     dreads = dreads + jnp.dot(dscores, keys, precision=EXACT, preferred_element_type=F32)
     dkeys = dkeys + jnp.dot(dscores.T, reads, precision=EXACT, preferred_element_type=F32)
     cols = slice(0, BC)
-    dconv = lanes(dkeys, dreads) * slope_ref[...]
+    dconv = lanes(dkeys, dreads) * sb[:, at(BC_SLOPE)]
     taps = taps_of(ext_ref, cols, count, columns(tab_ref[MASK : MASK + count, :], BC))
     smask = columns(tab_ref[SMASK : SMASK + count + 8, :], BC)
     gin_ref[...], misc = conv_back(dconv, taps, w_ref[...], z_ref, cols, smask)
     misc_ref[...] = misc
-    misc_ref[16 + CONV + 1 : 24, :128] = scal[:3, :]
+    gathered.wait()
+    grads = lanes(gb[...], misc[16:, :])
+    thirds = [grads[:, at(i * THIRD, THIRD)] for i in range(3)]
+    packed_ref[0:8, :] = rows(thirds[0][:CONV], thirds[1][:CONV])
+    fill = jnp.zeros((1, THIRD - 384), F32)
+    params = lanes(scal[0:1, :], scal[1:2, :], scal[2:3, :], fill)
+    last = [third[CONV : CONV + 1] for third in thirds]
+    packed_ref[8:16, :] = rows(thirds[2][:CONV], *last, params)
 
 
 def cost(us):
@@ -608,27 +623,27 @@
     return value
 
 
-def chip_of(lead, mine, met, own):
+def chip_of(piece, work, met):
     state = (STATE + 8, WIDTH)
     payload = (STATE + 16, WIDTH)
-    outs = [(state, F32)] + [(payload, I16)] * lead
+    outs = [(state, F32)] + [(payload, I16)] * (piece < STREAMS)
     return call(
-        functools.partial(chip_kernel, lead),
-        (mine, met, own),
-        [HBM] * 3,
+        functools.partial(chip_kernel, piece),
+        (work, met),
+        [HBM] * 2,
         outs,
         [whole(s) for s, _ in outs],
-        [vmem(STATE, WIDTH), vmem(*state), vmem(8, WIDTH), sems(3)],
+        [vmem(*state), vmem(*state), sems(2)],
         us=1.5,
     )
 
 
-def hop(pick, previous, chips):
+def hop(turn, hops, previous, chips):
     payload = (STATE + 16, WIDTH)
     return call(
-        hop_kernel,
-        (pick, previous, *chips),
-        [SMEM, *full(previous, *chips)],
+        functools.partial(hop_kernel, turn, hops),
+        (previous, *chips),
+        full(previous, *chips),
         [(payload, I16)],
         [whole(payload)],
         us=0.8,
@@ -640,12 +655,8 @@
 ):
     count = conv_input.shape[0]
     size = lax.axis_size("seq")
-    index = lax.axis_index("seq")
-    core = lax.rem(index, 2)
-    chip = lax.div(index, 2)
+    core = lax.rem(lax.axis_index("seq"), 2)
     hops = size // 2 - 1
-    place = jnp.where(core == 1, chip, hops - chip)
-    flag = jnp.stack([core, place]).astype(jnp.int32)
     docs = doc_start[None, :]
     edge = part((16, CH), count // 16 - 1, 0)
 
@@ -663,46 +674,28 @@
     square = (count, count)
     payload = (STATE + 16, WIDTH)
     shape = (count, WIDTH)
-    chips, sent, mets = [], [], []
-    given = tab
-    for turn in range(TURNS):
-        lead = turn == 0
-        here = [part((height, SPAN), 0, turn) for height in (CONV - 1, CONV, 1)]
-        ins = [flag, conv_input, halo, conv_weight, bias, cotangent, given]
-        specs = [SMEM, HBM, *here, HBM, whole(table)]
-        outs = [(STATE + 8, WIDTH)] * STREAMS + [(STATE, WIDTH)] * STREAMS
-        out_specs = [HBM] * len(outs)
-        if lead:
-            ins += [halo, conv_weight, bias]
-            specs += [part((height, BC), 0, BC_AT) for height in (CONV - 1, CONV, 1)]
-            bc_out = [(count, BC), (count, BC), (BC, count), square]
-            outs += bc_out
-            out_specs += [whole(s) for s in bc_out]
-        else:
-            ins.append(turned)
-            specs.append(whole(turned.shape))
-        got = call(
-            functools.partial(local_kernel, turn),
-            ins,
-            specs,
-            [(s, F32) for s in outs],
-            out_specs,
-            [
-                vmem(count, SPAN, BF16), vmem(count, SPAN, BF16), vmem(STATE + 8, SPAN),
-                vmem(STATE, SPAN), vmem(count + 8, SPAN + BC), vmem(count, BC, BF16),
-                sems(2 * STREAMS + 1), sems(2 * STREAMS),
-            ],
-            us=5.0,
-        )
-        if lead:
-            bc_act, bc_slope, turned, scores = got[2 * STREAMS :]
-        for stream in range(STREAMS):
-            send, mine = got[stream], got[STREAMS + stream]
-            met = other_core(send)
-            mets.append(met)
-            chip, *first = chip_of(lead, mine, met, send)
-            chips.append(chip)
-            sent += first
+    ins = (conv_input, halo, conv_weight, bias, cotangent, tab)
+    outs = [(STATE + 8, WIDTH)] * PIECES + [(WORK_ROWS, INNER)]
+    got = call(
+        local_kernel,
+        ins,
+        [HBM, *full(halo, conv_weight, bias), HBM, whole(table)],
+        [(s, F32) for s in outs],
+        [HBM] * len(outs),
+        [
+            vmem(count, CH, BF16), vmem(count, INNER, BF16), vmem(STATE + 8, INNER),
+            vmem(STATE + 8, INNER), vmem(count, SMALLS), vmem(count + 8, CH),
+            sems(2 * PIECES + 1), sems(2 * PIECES + 1),
+        ],
+        us=8.0,
+    )
+    *sends, work = got
+    mets = [other_core(send) for send in sends]
+    chips, sent = [], []
+    for j in range(PIECES):
+        chip, *first = chip_of(j, work, mets[j])
+        chips.append(chip)
+        sent += first
 
     withins = []
     for j in range(PIECES):
@@ -710,13 +703,13 @@
         withins.append(
             call(
                 functools.partial(within_kernel, j),
-                (conv_input, cotangent, halo, conv_weight, bias, tab, scores),
-                [HBM, HBM, *here, *full(tab, scores)],
+                (conv_input, cotangent, work, halo, conv_weight, bias, tab),
+                [HBM, HBM, HBM, *here, whole(table)],
                 [(shape, F32), (shape, F32), (square, F32)],
                 [HBM, HBM, whole(square)],
                 [
-                    vmem(*shape, BF16), vmem(*shape, BF16), vmem(*shape), vmem(*shape),
-                    vmem(count + 8, WIDTH), sems(2), sems(2),
+                    vmem(*shape, BF16), vmem(*shape, BF16), vmem(*square), vmem(*shape),
+                    vmem(*shape), vmem(count + 8, WIDTH), sems(3), sems(2),
                 ],
                 us=2.0,
             )
@@ -730,10 +723,10 @@
         turn, stream = j // STREAMS, j % STREAMS
         here = [part((height, WIDTH), 0, j) for height in (CONV - 1, CONV, 1)]
         y, dx, _ = withins[j]
-        ins = [flag, *received[stream][turn : turn + hops], *swapped[stream][turn : turn + hops]]
-        specs = [SMEM] + [ANY] * (2 * hops)
-        ins += [mets[j], y, dx, cotangent, conv_input, halo, conv_weight, bias, tab, bc_act]
-        specs += [HBM] * 5 + here + full(tab, bc_act)
+        ins = [*received[stream][turn : turn + hops], *swapped[stream][turn : turn + hops]]
+        specs = [ANY] * (2 * hops)
+        ins += [mets[j], work, y, dx, cotangent, conv_input, halo, conv_weight, bias, tab]
+        specs += [HBM] * 6 + here + [whole(table)]
         aliases = None
         if shared is not None:
             aliases = {len(ins) + i: i for i in range(3)}
@@ -746,10 +739,10 @@
             shared_out + small_out,
             [HBM] * 3 + [whole(s) for s, _ in small_out],
             [
-                vmem(*payload, I16), vmem(*payload, I16), vmem(STATE + 8, WIDTH),
+                vmem(*payload, I16), vmem(*payload, I16), vmem(STATE + 8, WIDTH), vmem(count, BC),
                 vmem(*shape), vmem(*shape), vmem(*shape, BF16), vmem(*shape, BF16),
                 vmem(*shape, BF16), vmem(*shape, BF16), vmem(24, WIDTH),
-                vmem(count + 8, WIDTH), vmem(count + 16, WIDTH), sems(2 + 10), sems(3),
+                vmem(count + 8, WIDTH), vmem(count + 16, WIDTH), sems(3 + 10), sems(3),
             ],
             aliases,
             us=5.0,
@@ -762,10 +755,9 @@
     turns = TURNS + hops - 1
     for turn in range(turns):
         if turn:
-            piece = jnp.clip(turn - place, 0, TURNS - 1)
-            pick = jnp.stack([piece, place]).astype(jnp.int32)
             sent = [
-                hop(pick, received[stream][-1], chips[stream::STREAMS]) for stream in range(STREAMS)
+                hop(turn, hops, received[stream][-1], chips[stream::STREAMS])
+                for stream in range(STREAMS)
             ]
         arrived = [permute(value, "seq", along(size)) for value in sent]
         for stream in range(STREAMS):
@@ -780,22 +772,30 @@
     output, gin, misc = shared
 
     dscores = [group[2] for group in withins]
-    small = (tab, bc_act, bc_slope, *dreads, *dkeys, *dscores, *scals)
-    ins = (conv_input, halo, conv_weight) + small + (gin, misc)
+    small = (*dreads, *dkeys, *dscores, *scals)
+    ins = (conv_input, halo, conv_weight, tab, work) + small + (gin, misc)
     bc_common = [part((count, BC), 0, BC_AT), part((CONV - 1, BC), 0, BC_AT), part((CONV, BC), 0, BC_AT)]
-    gin, misc = call(
+    gin, misc, packed = call(
         final_kernel,
         ins,
-        bc_common + full(*small) + [ANY] * 2,
-        shared_out[1:],
-        [part((count, BC), 0, BC_AT), part((24, BC), 0, BC_AT)],
-        [vmem(count + 8, BC), vmem(count + 16, BC)],
+        bc_common + [whole(table), HBM] + full(*small) + [HBM] * 2,
+        shared_out[1:] + [((16, THIRD), F32)],
+        [part((count, BC), 0, BC_AT), part((24, BC), 0, BC_AT), whole((16, THIRD))],
+        [
+            vmem(count + 8, BC), vmem(count + 16, BC), vmem(count, SCORES), vmem(8, INNER), sems(2),
+        ],
         {len(ins) - 2: 0, len(ins) - 1: 1},
     )
 
     returned = lax.ppermute(
         misc[8 - CONV + 1 : 8], "seq", [(i, i - 1) for i in range(1, size)]
     )
+    lower, upper = packed[:8], packed[8:]
+    first = core == 0
+    value = jnp.where(first, lower, upper)
+    value = value + other_core(jnp.where(first, upper, lower))
+    value = xor_sum(value, "dp", 1)
+    value, returned = lax.optimization_barrier((value, returned))
     grad_input = call(
         edge_kernel,
         (gin, misc, returned, docs),
@@ -804,21 +804,16 @@
         [edge],
         aliases={0: 0},
     )[0]
-
-    half = CH // 2
-    lower, upper = misc[16:24, :half], misc[16:24, half:]
-    first = core == 0
-    value = jnp.where(first, lower, upper)
-    value = value + other_core(jnp.where(first, upper, lower))
-    value = xor_sum(value, "dp", 1)
     value = xor_sum(value, "seq", 2)
+    value, grad_input = lax.optimization_barrier((value, grad_input))
     value = value * float(lax.axis_size("dp") * size * count) ** (-0.5)
     other = other_core(value)
     lower = jnp.where(first, value, other)
     upper = jnp.where(first, other, value)
-    summed = jnp.concatenate([lower, upper], axis=1)
-    scal = summed[CONV + 1 :, INNER : INNER + HEADS]
-    return (output, grad_input, summed[:CONV], summed[CONV], scal[0], scal[1], scal[2])
+    grad_weight = jnp.concatenate([lower[:CONV], lower[CONV:], upper[:CONV]], axis=1)
+    grad_bias = upper[CONV : CONV + 3].reshape(CH)
+    params = [upper[CONV + 3, i : i + HEADS] for i in (0, 128, 256)]
+    return (output, grad_input, grad_weight, grad_bias, *params)
 
 
 def solution(mesh):

time: 110 us -> 105 us (0.955)
  starting transfers between devices: 34.7 us -> 30.4 us
  local copies, waits for them, and re-layouts: 8.95 us -> 5.14 us
  waiting for transfers between devices: 7.93 us -> 11.6 us
    unnamed x44 -> x30, local copies, waits for them, and re-layouts: 8.4 us -> 3.94 us
    ppermute x28, starting transfers between devices: 26.5 us -> 22.7 us  [permute(): return lax.ppermute(value, axis, [(i, target(i)) for i in range(size)])]
    ppermute x1, waiting for transfers between devices: 0.14 us -> 2.88 us  [on_device(): lax.ppermute(misc[8 - CONV + 1:8], 'seq', [(i, i - 1) for i in range(1, s...]
    pallas_call x24 -> x23, Pallas kernels: 54.8 us -> 55.2 us  [call(): pl.pallas_call(kernel, grid=(1,), in_specs=specs, out_specs=out_specs, ou...]
  transfers between devices with their start and end apart: 30 -> 30, of which waited for: 10 -> 10; matrix products, arithmetic and copies ran while one was open for 0% -> 0% of each run, Pallas kernels for 40% -> 39%
where the time goes in v2:
time: 105 us; the launch traced here: 104 us
  Pallas kernels  55.2 us (53%)
  starting transfers between devices  30.4 us (29%)
  waiting for transfers between devices  11.6 us (11%)
  local copies, waits for them, and re-layouts  5.14 us (5%)
  between operations  1.1 us (1%)
    pallas_call x23, Pallas kernels, call(): pl.pallas_call(kernel, grid=(1,), in_specs=specs, out_specs=out_specs, ou...  55.2 us
    ppermute x28, starting transfers between devices, permute(): return lax.ppermute(value, axis, [(i, target(i)) for i in range(size)])  22.7 us
    ppermute x28, waiting for transfers between devices, permute(): return lax.ppermute(value, axis, [(i, target(i)) for i in range(size)])  8.46 us
    ppermute x1, starting transfers between devices, on_device(): halo = lax.ppermute(tail_out, 'seq', [(i, i + 1) for i in range(size - 1)])  4.59 us
    unnamed x30, local copies, waits for them, and re-layouts  3.94 us
    ppermute x1, starting transfers between devices, on_device(): lax.ppermute(misc[8 - CONV + 1:8], 'seq', [(i, i - 1) for i in range(1, s...  3.1 us
    ppermute x1, waiting for transfers between devices, on_device(): lax.ppermute(misc[8 - CONV + 1:8], 'seq', [(i, i - 1) for i in range(1, s...  2.88 us
  transfers between devices with their start and end apart: 30, of which 10 were waited for; matrix products, arithmetic and copies ran while one was open for 0% of the time, Pallas kernels for 39%

profile of v2, /device:TPU:1, one launch (start us, length us, event | category | flops | bytes accessed | tf_op | source)
XLA Modules:
  0.0 104.2 jit_solution(1684950667924386885)
XLA Ops:
  0.6 1.3 %copy-done = bf16[128,5376]{1,0:T(8,128)(2,1)S(1)} copy-done((bf16[128,5376]{1,0:T(8,128)(2,1)S(1)}, bf16[128,5376]{1,0:T(8,128)(2,1)}, u32[]{:S(2)}) %copy-start) | copy-done | bytes 1376280
  2.0 0.7 copy-done.12
  2.8 4.6 %collective-permute-start = (bf16[3,5376]{1,0:T(4,128)(2,1)S(1)}, bf16[3,5376]{1,0:T(4,128)(2,1)S(1)}, u32[]{:S(2)}, u32[]{:S(2)}) collective-permute-start(bf16[3,5376]{1,0:T(4,128)(2,1)S(1)} %shard_map.144), channel_id=1, source_target_pairs={{0,1},{1,2},{2,3},{3,4},{4,5},{5,6},{6,7},{8,9},{9,10},{10,11},{11... | collective-permute-start | bytes 96776 | tf_op jit(solution)/shard_map/ppermute | solution.py:667
  9.3 7.0 %shard_map.146 = (f32[136,1280]{1,0:T(8,128)S(1)}, f32[136,1280]{1,0:T(8,128)}, f32[136,1280]{1,0:T(8,128)}, f32[136,1280]{1,0:T(8,128)}, f32[3328,5120]{1,0:T(8,128)}) custom-call(bf16[128,5376]{1,0:T(8,128)(2,1)S(1)} %copy-done.1, bf16[3,5376]{1,0:T(4,128)(2,1)S(1)} %collective-permute-done.halo_ref.refs_12_, f32[4,5376]{1,0:T(4,128)S(1)} %copy-done.3, ...), custom_call_target="tpu_custom_call" | custom-call | flops 8800000000 | bytes 1000 | tf_op jit(solution)/shard_map/pallas_call | solution.py:571
  16.3 0.5 collective-permute-start.1
  17.3 1.3 %collective-permute-done.10.met_ref.refs_6_ = f32[136,1280]{1,0:T(8,128)S(1)} collective-permute-done((f32[136,1280]{1,0:T(8,128)S(1)}, f32[136,1280]{1,0:T(8,128)S(1)}, u32[]{:S(2)}, u32[]{:S(2)}) %collective-permute-start.10) | collective-permute-done | bytes 696352 | tf_op jit(solution)/shard_map/ppermute | solution.py:594
  18.7 2.3 %shard_map.153 = (f32[136,1280]{1,0:T(8,128)S(1)}, s16[144,1280]{1,0:T(8,128)(2,1)}) custom-call(f32[3328,5120]{1,0:T(8,128)} %get-tuple-element.67.work_ref.refs_7_, f32[136,1280]{1,0:T(8,128)S(1)} %collective-permute-done.10.met_ref.refs_6_), custom_call_target="tpu_custom_call" | custom-call | flops 1650000000 | bytes 1000 | tf_op jit(solution)/shard_map/pallas_call | solution.py:571
  21.0 0.9 copy-done.6
  21.9 1.1 %collective-permute-start.11 = (s16[144,1280]{1,0:T(8,128)(2,1)}, s16[144,1280]{1,0:T(8,128)(2,1)}, u32[]{:S(2)}, u32[]{:S(2)}) collective-permute-start(s16[144,1280]{1,0:T(8,128)(2,1)} %get-tuple-element.75), channel_id=1, source_target_pairs={{0,1},{1,3},{2,0},{3,5},{4,2},{5,7},{6,4},{7,6},{8,9},{9,11},{10,8... | collective-permute-start | bytes 1105928 | tf_op jit(solution)/shard_map/ppermute | solution.py:594
  23.0 1.6 %shard_map.147 = (f32[136,1280]{1,0:T(8,128)S(1)}, s16[144,1280]{1,0:T(8,128)(2,1)S(1)}) custom-call(f32[3328,5120]{1,0:T(8,128)} %get-tuple-element.67.work_ref.refs_7_, f32[136,1280]{1,0:T(8,128)} %collective-permute-done.1.met_ref.refs_6_), custom_call_target="tpu_custom_call" | custom-call | flops 1650000000 | bytes 1000 | tf_op jit(solution)/shard_map/pallas_call | solution.py:571
  24.6 1.3 %collective-permute-start.2 = (s16[144,1280]{1,0:T(8,128)(2,1)S(1)}, s16[144,1280]{1,0:T(8,128)(2,1)S(1)}, u32[]{:S(2)}, u32[]{:S(2)}) collective-permute-start(s16[144,1280]{1,0:T(8,128)(2,1)S(1)} %get-tuple-element.69), channel_id=1, source_target_pairs={{0,1},{1,3},{2,0},{3,5},{4,2},{5,7},{6,4},{7,6},{8,9},{9,11},{10,8... | collective-permute-start | bytes 1105928 | tf_op jit(solution)/shard_map/ppermute | solution.py:594
  25.9 1.4 %shard_map.154.refs_1_ = f32[136,1280]{1,0:T(8,128)S(1)} custom-call(f32[3328,5120]{1,0:T(8,128)} %get-tuple-element.67.work_ref.refs_7_, f32[136,1280]{1,0:T(8,128)} %collective-permute-done.12.met_ref.refs_6_), custom_call_target="tpu_custom_call" | custom-call | flops 1650000000 | bytes 1000 | tf_op jit(solution)/shard_map/pallas_call | solution.py:571
  27.8 1.3 %shard_map.155 = s16[144,1280]{1,0:T(8,128)(2,1)S(1)} custom-call(s16[144,1280]{1,0:T(8,128)(2,1)} %collective-permute-done.11.previous_ref.refs_0_, f32[136,1280]{1,0:T(8,128)S(1)} %copy-done.7, f32[136,1280]{1,0:T(8,128)S(1)} %shard_map.154.refs_1_), custom_call_target="tpu_custom_call" | custom-call | flops 880000000 | bytes 1000 | tf_op jit(solution)/shard_map/pallas_call | solution.py:571
  29.2 2.2 %collective-permute-start.13 = (s16[144,1280]{1,0:T(8,128)(2,1)S(1)}, s16[144,1280]{1,0:T(8,128)(2,1)S(1)}, u32[]{:S(2)}, u32[]{:S(2)}) collective-permute-start(s16[144,1280]{1,0:T(8,128)(2,1)S(1)} %shard_map.155), channel_id=1, source_target_pairs={{0,1},{1,3},{2,0},{3,5},{4,2},{5,7},{6,4},{7,6},{8,9},{9,11},{10,8... | collective-permute-start | bytes 1105928 | tf_op jit(solution)/shard_map/ppermute | solution.py:594
  31.4 1.4 %shard_map.148.refs_1_ = f32[136,1280]{1,0:T(8,128)S(1)} custom-call(f32[3328,5120]{1,0:T(8,128)} %get-tuple-element.67.work_ref.refs_7_, f32[136,1280]{1,0:T(8,128)} %collective-permute-done.3.met_ref.refs_6_), custom_call_target="tpu_custom_call" | custom-call | flops 1650000000 | bytes 1000 | tf_op jit(solution)/shard_map/pallas_call | solution.py:571
  33.2 1.3 %collective-permute-start.4 = (s16[144,1280]{1,0:T(8,128)(2,1)S(1)}, s16[144,1280]{1,0:T(8,128)(2,1)S(1)}, u32[]{:S(2)}, u32[]{:S(2)}) collective-permute-start(s16[144,1280]{1,0:T(8,128)(2,1)S(1)} %shard_map.149), channel_id=1, source_target_pairs={{0,1},{1,3},{2,0},{3,5},{4,2},{5,7},{6,4},{7,6},{8,9},{9,11},{10,8... | collective-permute-start | bytes 1105928 | tf_op jit(solution)/shard_map/ppermute | solution.py:594
  34.5 3.0 %shard_map.152 = (f32[128,1280]{1,0:T(8,128)S(1)}, f32[128,1280]{1,0:T(8,128)S(1)}, f32[128,128]{1,0:T(8,128)S(1)}) custom-call(bf16[128,5376]{1,0:T(8,128)(2,1)S(1)} %copy-done.1, bf16[128,5120]{1,0:T(8,128)(2,1)S(1)} %copy-done.2, f32[3328,5120]{1,0:T(8,128)} %get-tuple-element.67.work_ref.refs_7_, ...), custom_call_target="tpu_custom_call" | custom-call | flops 2200000000 | bytes 1000 | tf_op jit(solution)/shard_map/pallas_call | solution.py:571
  37.9 1.2 %collective-permute-start.14 = (s16[144,1280]{1,0:T(8,128)(2,1)S(1)}, s16[144,1280]{1,0:T(8,128)(2,1)S(1)}, u32[]{:S(2)}, u32[]{:S(2)}) collective-permute-start(s16[144,1280]{1,0:T(8,128)(2,1)S(1)} %shard_map.156), channel_id=1, source_target_pairs={{0,1},{1,3},{2,0},{3,5},{4,2},{5,7},{6,4},{7,6},{8,9},{9,11},{10,8... | collective-permute-start | bytes 1105928 | tf_op jit(solution)/shard_map/ppermute | solution.py:594
  39.1 3.0 %shard_map.158 = (f32[128,1280]{1,0:T(8,128)S(1)}, f32[128,1280]{1,0:T(8,128)S(1)}, f32[128,128]{1,0:T(8,128)S(1)}) custom-call(bf16[128,5376]{1,0:T(8,128)(2,1)S(1)} %copy-done.1, bf16[128,5120]{1,0:T(8,128)(2,1)S(1)} %copy-done.2, f32[3328,5120]{1,0:T(8,128)} %get-tuple-element.67.work_ref.refs_7_, ...), custom_call_target="tpu_custom_call" | custom-call | flops 2200000000 | bytes 1000 | tf_op jit(solution)/shard_map/pallas_call | solution.py:571
  42.5 1.1 %collective-permute-start.5 = (s16[144,1280]{1,0:T(8,128)(2,1)S(1)}, s16[144,1280]{1,0:T(8,128)(2,1)S(1)}, u32[]{:S(2)}, u32[]{:S(2)}) collective-permute-start(s16[144,1280]{1,0:T(8,128)(2,1)S(1)} %shard_map.150), channel_id=1, source_target_pairs={{0,1},{1,3},{2,0},{3,5},{4,2},{5,7},{6,4},{7,6},{8,9},{9,11},{10,8... | collective-permute-start | bytes 1105928 | tf_op jit(solution)/shard_map/ppermute | solution.py:594
  43.6 3.2 %shard_map.161 = (f32[128,1280]{1,0:T(8,128)S(1)}, f32[128,1280]{1,0:T(8,128)S(1)}, f32[128,128]{1,0:T(8,128)S(1)}) custom-call(bf16[128,5376]{1,0:T(8,128)(2,1)S(1)} %copy-done.1, bf16[128,5120]{1,0:T(8,128)(2,1)S(1)} %copy-done.2, f32[3328,5120]{1,0:T(8,128)} %get-tuple-element.67.work_ref.refs_7_, ...), custom_call_target="tpu_custom_call" | custom-call | flops 2200000000 | bytes 1000 | tf_op jit(solution)/shard_map/pallas_call | solution.py:571
  46.8 0.5 collective-permute-start.17
  47.4 3.0 %shard_map.162 = (f32[128,1280]{1,0:T(8,128)S(1)}, f32[128,1280]{1,0:T(8,128)S(1)}, f32[128,128]{1,0:T(8,128)S(1)}) custom-call(bf16[128,5376]{1,0:T(8,128)(2,1)S(1)} %copy-done.1, bf16[128,5120]{1,0:T(8,128)(2,1)S(1)} %copy-done.2, f32[3328,5120]{1,0:T(8,128)} %get-tuple-element.67.work_ref.refs_7_, ...), custom_call_target="tpu_custom_call" | custom-call | flops 2200000000 | bytes 1000 | tf_op jit(solution)/shard_map/pallas_call | solution.py:571
  50.4 0.5 collective-permute-start.7
  51.8 1.2 %collective-permute-start.6 = (s16[144,1280]{1,0:T(8,128)(2,1)S(1)}, s16[144,1280]{1,0:T(8,128)(2,1)S(1)}, u32[]{:S(2)}, u32[]{:S(2)}) collective-permute-start(s16[144,1280]{1,0:T(8,128)(2,1)S(1)} %shard_map.151), channel_id=1, source_target_pairs={{0,1},{1,3},{2,0},{3,5},{4,2},{5,7},{6,4},{7,6},{8,9},{9,11},{10,8... | collective-permute-start | bytes 1105928 | tf_op jit(solution)/shard_map/ppermute | solution.py:594
  53.0 1.4 %collective-permute-start.15 = (s16[144,1280]{1,0:T(8,128)(2,1)S(1)}, s16[144,1280]{1,0:T(8,128)(2,1)S(1)}, u32[]{:S(2)}, u32[]{:S(2)}) collective-permute-start(s16[144,1280]{1,0:T(8,128)(2,1)S(1)} %shard_map.157), channel_id=1, source_target_pairs={{0,1},{1,3},{2,0},{3,5},{4,2},{5,7},{6,4},{7,6},{8,9},{9,11},{10,8... | collective-permute-start | bytes 1105928 | tf_op jit(solution)/shard_map/ppermute | solution.py:594
  54.4 5.4 %shard_map.159 = (bf16[128,5120]{1,0:T(8,128)(2,1)}, bf16[128,5376]{1,0:T(8,128)(2,1)}, f32[24,5376]{1,0:T(8,128)S(1)}, f32[128,128]{1,0:T(8,128)S(1)}, f32[128,128]{1,0:T(8,128)S(1)}, /*index=5*/f32[8,128]{1,0:T(8,128)S(1)}) custom-call(s16[144,1280]{1,0:T(8,128)(2,1)} %collective-permute-done.11.previous_ref.refs_0_, ...), custom_call_target="tpu_custom_call" | custom-call | flops 5500000256 | bytes 1000 | tf_op jit(solution)/shard_map/pallas_call | solution.py:571
  59.8 1.6 %collective-permute-done.15.refs_2_ = s16[144,1280]{1,0:T(8,128)(2,1)S(1)} collective-permute-done((s16[144,1280]{1,0:T(8,128)(2,1)S(1)}, s16[144,1280]{1,0:T(8,128)(2,1)S(1)}, u32[]{:S(2)}, u32[]{:S(2)}) %collective-permute-start.15) | collective-permute-done | bytes 368672 | tf_op jit(solution)/shard_map/ppermute | solution.py:594
  61.4 2.3 %collective-permute-start.20 = (s16[144,1280]{1,0:T(8,128)(2,1)S(1)}, s16[144,1280]{1,0:T(8,128)(2,1)S(1)}, u32[]{:S(2)}, u32[]{:S(2)}) collective-permute-start(s16[144,1280]{1,0:T(8,128)(2,1)S(1)} %collective-permute-done.15.refs_2_), channel_id=1, source_target_pairs={{0,1},{1,0},{2,3},{3,2},{4,5},{5,4},{6,7},{7,6},{8,9},{9,8},{10,11... | collective-permute-start | bytes 1105928 | tf_op jit(solution)/shard_map/ppermute | solution.py:594
  63.7 5.4 %shard_map.160 = (bf16[128,5120]{1,0:T(8,128)(2,1)}, bf16[128,5376]{1,0:T(8,128)(2,1)}, f32[24,5376]{1,0:T(8,128)S(1)}, f32[128,128]{1,0:T(8,128)S(1)}, f32[128,128]{1,0:T(8,128)S(1)}, /*index=5*/f32[8,128]{1,0:T(8,128)S(1)}) custom-call(s16[144,1280]{1,0:T(8,128)(2,1)S(1)} %collective-permute-done.2.pr, ...), custom_call_target="tpu_custom_call", output_to_operand_aliasing={{0}: (16, {}), {1}: (17, {}), {2}: (18, {})} | custom-call | flops 5500000256 | bytes 1000 | tf_op jit(solution)/shard_map/pallas_call | solution.py:571
  69.3 5.4 %shard_map.163 = (bf16[128,5120]{1,0:T(8,128)(2,1)}, bf16[128,5376]{1,0:T(8,128)(2,1)}, f32[24,5376]{1,0:T(8,128)S(1)}, f32[128,128]{1,0:T(8,128)S(1)}, f32[128,128]{1,0:T(8,128)S(1)}, /*index=5*/f32[8,128]{1,0:T(8,128)S(1)}) custom-call(s16[144,1280]{1,0:T(8,128)(2,1)S(1)} %collective-permute-done.13.p, ...), custom_call_target="tpu_custom_call", output_to_operand_aliasing={{0}: (16, {}), {1}: (17, {}), {2}: (18, {})} | custom-call | flops 5500000256 | bytes 1000 | tf_op jit(solution)/shard_map/pallas_call | solution.py:571
  74.7 5.4 %shard_map.164 = (bf16[128,5120]{1,0:T(8,128)(2,1)}, bf16[128,5376]{1,0:T(8,128)(2,1)}, f32[24,5376]{1,0:T(8,128)S(1)}, f32[128,128]{1,0:T(8,128)S(1)}, f32[128,128]{1,0:T(8,128)S(1)}, /*index=5*/f32[8,128]{1,0:T(8,128)S(1)}) custom-call(s16[144,1280]{1,0:T(8,128)(2,1)S(1)} %collective-permute-done.4.pr, ...), custom_call_target="tpu_custom_call", output_to_operand_aliasing={{0}: (16, {}), {1}: (17, {}), {2}: (18, {})} | custom-call | flops 5500000256 | bytes 1000 | tf_op jit(solution)/shard_map/pallas_call | solution.py:571
  80.1 2.2 %shard_map.165 = (bf16[128,5376]{1,0:T(8,128)(2,1)}, f32[24,5376]{1,0:T(8,128)S(1)}, f32[16,1792]{1,0:T(8,128)S(1)}) custom-call(bf16[128,5376]{1,0:T(8,128)(2,1)S(1)} %copy-done.1, bf16[3,5376]{1,0:T(4,128)(2,1)S(1)} %collective-permute-done.halo_ref.refs_12_, f32[4,5376]{1,0:T(4,128)S(1)} %copy-done.3, ...), custom_call_target="tpu_custom_call", output_to_operand_aliasing={{0}: (21, {}), {1}: (22, {})} | custom-call | flops 1100000000 | bytes 1000 | tf_op jit(solution)/shard_map/pallas_call | solution.py:571
  82.3 0.5 collective-permute-start.21
  82.9 0.9 collective-permute-done.21
  83.8 1.3 %collective-permute-start.23 = (f32[8,1792]{1,0:T(8,128)S(1)}, f32[8,1792]{1,0:T(8,128)S(1)}, u32[]{:S(2)}, u32[]{:S(2)}) collective-permute-start(f32[8,1792]{1,0:T(8,128)S(1)} %select_add_fusion), channel_id=1, source_target_pairs={{0,16},{8,24},{16,0},{24,8},{1,17},{9,25},{17,1},{25,9},{2,18},{10... | collective-permute-start | bytes 172040 | tf_op jit(solution)/shard_map/ppermute | solution.py:594
  85.1 1.2 %collective-permute-start.24 = (f32[8,1792]{1,0:T(8,128)S(1)}, f32[8,1792]{1,0:T(8,128)S(1)}, u32[]{:S(2)}, u32[]{:S(2)}) collective-permute-start(f32[8,1792]{1,0:T(8,128)S(1)} %select_add_fusion), channel_id=1, source_target_pairs={{0,24},{8,16},{16,8},{24,0},{1,25},{9,17},{17,9},{25,1},{2,26},{10... | collective-permute-start | bytes 172040 | tf_op jit(solution)/shard_map/ppermute | solution.py:594
  86.5 3.1 %collective-permute-start.25 = (f32[3,5376]{1,0:T(4,128)S(1)}, f32[3,5376]{1,0:T(4,128)S(1)}, u32[]{:S(2)}, u32[]{:S(2)}) collective-permute-start(f32[3,5376]{1,0:T(4,128)S(1)} %slice.32), channel_id=1, source_target_pairs={{1,0},{2,1},{3,2},{4,3},{5,4},{6,5},{7,6},{9,8},{10,9},{11,10},{12... | collective-permute-start | bytes 193544 | tf_op jit(solution)/shard_map/ppermute | solution.py:790
  90.1 2.9 %collective-permute-done.25.back_ref = f32[3,5376]{1,0:T(4,128)S(1)} collective-permute-done((f32[3,5376]{1,0:T(4,128)S(1)}, f32[3,5376]{1,0:T(4,128)S(1)}, u32[]{:S(2)}, u32[]{:S(2)}) %collective-permute-start.25) | collective-permute-done | bytes 64544 | tf_op jit(solution)/shard_map/ppermute | solution.py:790
  93.0 1.7 %collective-permute-start.27 = (f32[8,1792]{1,0:T(8,128)S(1)}, f32[8,1792]{1,0:T(8,128)S(1)}, u32[]{:S(2)}, u32[]{:S(2)}) collective-permute-start(f32[8,1792]{1,0:T(8,128)S(1)} %add_add_fusion.1), channel_id=1, source_target_pairs={{0,4},{1,5},{2,6},{3,7},{4,0},{5,1},{6,2},{7,3},{8,12},{9,13},{10,... | collective-permute-start | bytes 172040 | tf_op jit(solution)/shard_map/ppermute | solution.py:594
  94.7 1.7 %collective-permute-start.28 = (f32[8,1792]{1,0:T(8,128)S(1)}, f32[8,1792]{1,0:T(8,128)S(1)}, u32[]{:S(2)}, u32[]{:S(2)}) collective-permute-start(f32[8,1792]{1,0:T(8,128)S(1)} %add_add_fusion.1), channel_id=1, source_target_pairs={{0,6},{1,7},{2,4},{3,5},{4,2},{5,3},{6,0},{7,1},{8,14},{9,15},{10,... | collective-permute-start | bytes 172040 | tf_op jit(solution)/shard_map/ppermute | solution.py:594
  96.4 1.8 %shard_map.166 = bf16[128,5376]{1,0:T(8,128)(2,1)} custom-call(bf16[128,5376]{1,0:T(8,128)(2,1)} %get-tuple-element.123.gin_ref, f32[24,5376]{1,0:T(8,128)S(1)} %get-tuple-element.121.misc_ref, f32[3,5376]{1,0:T(4,128)S(1)} %collective-permute-done.25.back_ref, s32[1,128]{1,0:T(1,128)S(1)} %bitcast.17), custom_call_target="tpu_custom_call", output_to_operand_aliasing={{}: (0, {})} | custom-call | flops 1100000000 | bytes 1000 | tf_op jit(solution)/shard_map/pallas_call | solution.py:571
  98.2 2.1 %collective-permute-done.28 = f32[8,1792]{1,0:T(8,128)S(1)} collective-permute-done((f32[8,1792]{1,0:T(8,128)S(1)}, f32[8,1792]{1,0:T(8,128)S(1)}, u32[]{:S(2)}, u32[]{:S(2)}) %collective-permute-start.28) | collective-permute-done | bytes 57376 | tf_op jit(solution)/shard_map/ppermute | solution.py:594
  100.3 0.6 collective-permute-done.26
  101.5 0.9 collective-permute-done.29
  102.4 0.5 slice_bitcast_fusion
  102.9 0.6 reshape.17
  103.6 0.7 pad_maximum_fusion
  (79 shorter events, 6.5 us)
Async XLA Ops:
  0.6 1.3 %copy-start = (bf16[128,5376]{1,0:T(8,128)(2,1)S(1)}, bf16[128,5376]{1,0:T(8,128)(2,1)}, u32[]{:S(2)}) copy-start(bf16[128,5376]{1,0:T(8,128)(2,1)} %x_ref.13) | copy-start | bytes 4128772
  2.0 0.7 copy-start.12
  2.6 4.8 %copy-start.8 = (f32[128,80]{0,1:T(8,128)S(1)}, f32[128,80]{0,1:T(8,128)}, u32[]{:S(2)}) copy-start(f32[128,80]{0,1:T(8,128)} %param.13) | copy-start | bytes 122884
  2.6 4.8 %copy-start.9 = (f32[80]{0:T(128)S(1)}, f32[80]{0:T(128)}, u32[]{:S(2)}) copy-start(f32[80]{0:T(128)} %param.14) | copy-start | bytes 964
  2.6 4.8 %copy-start.10 = (f32[80]{0:T(128)S(1)}, f32[80]{0:T(128)}, u32[]{:S(2)}) copy-start(f32[80]{0:T(128)} %param.15) | copy-start | bytes 964
  2.6 4.8 %copy-start.11 = (f32[80]{0:T(128)S(1)}, f32[80]{0:T(128)}, u32[]{:S(2)}) copy-start(f32[80]{0:T(128)} %param.16) | copy-start | bytes 964
  2.8 5.7 %collective-permute-start = (bf16[3,5376]{1,0:T(4,128)(2,1)S(1)}, bf16[3,5376]{1,0:T(4,128)(2,1)S(1)}, u32[]{:S(2)}, u32[]{:S(2)}) collective-permute-start(bf16[3,5376]{1,0:T(4,128)(2,1)S(1)} %shard_map.144), channel_id=1, source_target_pairs={{0,1},{1,2},{2,3},{3,4},{4,5},{5,6},{6,7},{8,9},{9,10},{10,11},{11... | collective-permute-start | bytes 96776 | tf_op jit(solution)/shard_map/ppermute | solution.py:667
  7.4 0.7 copy-start.14
  7.5 1.3 %copy-start.1 = (bf16[128,5376]{1,0:T(8,128)(2,1)S(1)}, bf16[128,5376]{1,0:T(8,128)(2,1)}, u32[]{:S(2)}) copy-start(bf16[128,5376]{1,0:T(8,128)(2,1)} %x_ref.13) | copy-start | bytes 4128772
  7.5 1.8 %copy-start.2 = (bf16[128,5120]{1,0:T(8,128)(2,1)S(1)}, bf16[128,5120]{1,0:T(8,128)(2,1)}, u32[]{:S(2)}) copy-start(bf16[128,5120]{1,0:T(8,128)(2,1)} %refs_10_.7) | copy-start | bytes 3932164
  7.5 1.8 %copy-start.3 = (f32[4,5376]{1,0:T(4,128)S(1)}, f32[4,5376]{1,0:T(4,128)}, u32[]{:S(2)}) copy-start(f32[4,5376]{1,0:T(4,128)} %w_ref.11) | copy-start | bytes 258052
  16.2 2.4 %collective-permute-start.10 = (f32[136,1280]{1,0:T(8,128)S(1)}, f32[136,1280]{1,0:T(8,128)S(1)}, u32[]{:S(2)}, u32[]{:S(2)}) collective-permute-start(f32[136,1280]{1,0:T(8,128)S(1)} %get-tuple-element.74), channel_id=1, source_target_pairs={{0,1},{1,0},{2,3},{3,2},{4,5},{5,4},{6,7},{7,6},{8,9},{9,8},{10,11... | collective-permute-start | bytes 2088968 | tf_op jit(solution)/shard_map/ppermute | solution.py:594
  16.3 6.7 %collective-permute-start.1 = (f32[136,1280]{1,0:T(8,128)}, f32[136,1280]{1,0:T(8,128)}, u32[]{:S(2)}, u32[]{:S(2)}) collective-permute-start(f32[136,1280]{1,0:T(8,128)} %get-tuple-element.68), channel_id=1, source_target_pairs={{0,1},{1,0},{2,3},{3,2},{4,5},{5,4},{6,7},{7,6},{8,9},{9,8},{10,11... | collective-permute-start | bytes 2088968 | tf_op jit(solution)/shard_map/ppermute | solution.py:594
  16.8 9.1 %collective-permute-start.12 = (f32[136,1280]{1,0:T(8,128)}, f32[136,1280]{1,0:T(8,128)}, u32[]{:S(2)}, u32[]{:S(2)}) collective-permute-start(f32[136,1280]{1,0:T(8,128)} %get-tuple-element.77), channel_id=1, source_target_pairs={{0,1},{1,0},{2,3},{3,2},{4,5},{5,4},{6,7},{7,6},{8,9},{9,8},{10,11... | collective-permute-start | bytes 2088968 | tf_op jit(solution)/shard_map/ppermute | solution.py:594
  16.9 14.5 %collective-permute-start.3 = (f32[136,1280]{1,0:T(8,128)}, f32[136,1280]{1,0:T(8,128)}, u32[]{:S(2)}, u32[]{:S(2)}) collective-permute-start(f32[136,1280]{1,0:T(8,128)} %get-tuple-element.71), channel_id=1, source_target_pairs={{0,1},{1,0},{2,3},{3,2},{4,5},{5,4},{6,7},{7,6},{8,9},{9,8},{10,11... | collective-permute-start | bytes 2088968 | tf_op jit(solution)/shard_map/ppermute | solution.py:594
  18.7 2.3 %copy-start.4 = (f32[136,1280]{1,0:T(8,128)}, f32[136,1280]{1,0:T(8,128)S(1)}, u32[]{:S(2)}) copy-start(f32[136,1280]{1,0:T(8,128)S(1)} %collective-permute-done.10.met_ref.refs_6_) | copy-start | bytes 2088964
  21.0 0.9 copy-start.6
  21.9 5.9 %collective-permute-start.11 = (s16[144,1280]{1,0:T(8,128)(2,1)}, s16[144,1280]{1,0:T(8,128)(2,1)}, u32[]{:S(2)}, u32[]{:S(2)}) collective-permute-start(s16[144,1280]{1,0:T(8,128)(2,1)} %get-tuple-element.75), channel_id=1, source_target_pairs={{0,1},{1,3},{2,0},{3,5},{4,2},{5,7},{6,4},{7,6},{8,9},{9,11},{10,8... | collective-permute-start | bytes 1105928 | tf_op jit(solution)/shard_map/ppermute | solution.py:594
  24.6 3.2 %copy-start.7 = (f32[136,1280]{1,0:T(8,128)S(1)}, f32[136,1280]{1,0:T(8,128)}, u32[]{:S(2)}) copy-start(f32[136,1280]{1,0:T(8,128)} %copy-done.6) | copy-start | bytes 2088964
  24.6 8.2 %collective-permute-start.2 = (s16[144,1280]{1,0:T(8,128)(2,1)S(1)}, s16[144,1280]{1,0:T(8,128)(2,1)S(1)}, u32[]{:S(2)}, u32[]{:S(2)}) collective-permute-start(s16[144,1280]{1,0:T(8,128)(2,1)S(1)} %get-tuple-element.69), channel_id=1, source_target_pairs={{0,1},{1,3},{2,0},{3,5},{4,2},{5,7},{6,4},{7,6},{8,9},{9,11},{10,8... | collective-permute-start | bytes 1105928 | tf_op jit(solution)/shard_map/ppermute | solution.py:594
  29.2 8.3 %collective-permute-start.13 = (s16[144,1280]{1,0:T(8,128)(2,1)S(1)}, s16[144,1280]{1,0:T(8,128)(2,1)S(1)}, u32[]{:S(2)}, u32[]{:S(2)}) collective-permute-start(s16[144,1280]{1,0:T(8,128)(2,1)S(1)} %shard_map.155), channel_id=1, source_target_pairs={{0,1},{1,3},{2,0},{3,5},{4,2},{5,7},{6,4},{7,6},{8,9},{9,11},{10,8... | collective-permute-start | bytes 1105928 | tf_op jit(solution)/shard_map/ppermute | solution.py:594
  33.2 9.0 %collective-permute-start.4 = (s16[144,1280]{1,0:T(8,128)(2,1)S(1)}, s16[144,1280]{1,0:T(8,128)(2,1)S(1)}, u32[]{:S(2)}, u32[]{:S(2)}) collective-permute-start(s16[144,1280]{1,0:T(8,128)(2,1)S(1)} %shard_map.149), channel_id=1, source_target_pairs={{0,1},{1,3},{2,0},{3,5},{4,2},{5,7},{6,4},{7,6},{8,9},{9,11},{10,8... | collective-permute-start | bytes 1105928 | tf_op jit(solution)/shard_map/ppermute | solution.py:594
  37.9 9.5 %collective-permute-start.14 = (s16[144,1280]{1,0:T(8,128)(2,1)S(1)}, s16[144,1280]{1,0:T(8,128)(2,1)S(1)}, u32[]{:S(2)}, u32[]{:S(2)}) collective-permute-start(s16[144,1280]{1,0:T(8,128)(2,1)S(1)} %shard_map.156), channel_id=1, source_target_pairs={{0,1},{1,3},{2,0},{3,5},{4,2},{5,7},{6,4},{7,6},{8,9},{9,11},{10,8... | collective-permute-start | bytes 1105928 | tf_op jit(solution)/shard_map/ppermute | solution.py:594
  42.5 8.8 %collective-permute-start.5 = (s16[144,1280]{1,0:T(8,128)(2,1)S(1)}, s16[144,1280]{1,0:T(8,128)(2,1)S(1)}, u32[]{:S(2)}, u32[]{:S(2)}) collective-permute-start(s16[144,1280]{1,0:T(8,128)(2,1)S(1)} %shard_map.150), channel_id=1, source_target_pairs={{0,1},{1,3},{2,0},{3,5},{4,2},{5,7},{6,4},{7,6},{8,9},{9,11},{10,8... | collective-permute-start | bytes 1105928 | tf_op jit(solution)/shard_map/ppermute | solution.py:594
  46.8 5.0 %collective-permute-start.16 = (s16[144,1280]{1,0:T(8,128)(2,1)}, s16[144,1280]{1,0:T(8,128)(2,1)S(1)}, u32[]{:S(2)}, u32[]{:S(2)}) collective-permute-start(s16[144,1280]{1,0:T(8,128)(2,1)} %collective-permute-done.11.previous_ref.refs_0_), channel_id=1, source_target_pairs={{0,1},{1,0},{2,3},{3,2},{4,5},{5,4},{6,7},{7,6},{8,9},{9,8},{10,11... | collective-permute-start | bytes 1105928 | tf_op jit(solution)/shard_map/ppermute | solution.py:594
  46.8 6.2 %collective-permute-start.17 = (s16[144,1280]{1,0:T(8,128)(2,1)S(1)}, s16[144,1280]{1,0:T(8,128)(2,1)S(1)}, u32[]{:S(2)}, u32[]{:S(2)}) collective-permute-start(s16[144,1280]{1,0:T(8,128)(2,1)S(1)} %collective-permute-done.13.previous_ref.refs_1_.refs_0_), channel_id=1, source_target_pairs={{0,1},{1,0},{2,3},{3,2},{4,5},{5,4},{6,7},{7,6},{8,9},{9,8},{10,11... | collective-permute-start | bytes 1105928 | tf_op jit(solution)/shard_map/ppermute | solution.py:594
  47.3 7.1 %collective-permute-start.18 = (s16[144,1280]{1,0:T(8,128)(2,1)S(1)}, s16[144,1280]{1,0:T(8,128)(2,1)S(1)}, u32[]{:S(2)}, u32[]{:S(2)}) collective-permute-start(s16[144,1280]{1,0:T(8,128)(2,1)S(1)} %collective-permute-done.14.previous_ref.refs_2_.refs_1_), channel_id=1, source_target_pairs={{0,1},{1,0},{2,3},{3,2},{4,5},{5,4},{6,7},{7,6},{8,9},{9,8},{10,11... | collective-permute-start | bytes 1105928 | tf_op jit(solution)/shard_map/ppermute | solution.py:594
  50.4 13.3 %collective-permute-start.7 = (s16[144,1280]{1,0:T(8,128)(2,1)S(1)}, s16[144,1280]{1,0:T(8,128)(2,1)S(1)}, u32[]{:S(2)}, u32[]{:S(2)}) collective-permute-start(s16[144,1280]{1,0:T(8,128)(2,1)S(1)} %collective-permute-done.2.previous_ref.refs_0_), channel_id=1, source_target_pairs={{0,1},{1,0},{2,3},{3,2},{4,5},{5,4},{6,7},{7,6},{8,9},{9,8},{10,11... | collective-permute-start | bytes 1105928 | tf_op jit(solution)/shard_map/ppermute | solution.py:594
  51.3 3.1 %copy-start.5 = (f32[136,1280]{1,0:T(8,128)S(1)}, f32[136,1280]{1,0:T(8,128)}, u32[]{:S(2)}) copy-start(f32[136,1280]{1,0:T(8,128)} %copy-done.4) | copy-start | bytes 2088964
  51.3 12.4 %collective-permute-start.8 = (s16[144,1280]{1,0:T(8,128)(2,1)S(1)}, s16[144,1280]{1,0:T(8,128)(2,1)S(1)}, u32[]{:S(2)}, u32[]{:S(2)}) collective-permute-start(s16[144,1280]{1,0:T(8,128)(2,1)S(1)} %collective-permute-done.4.previous_ref.refs_1_.refs_0_), channel_id=1, source_target_pairs={{0,1},{1,0},{2,3},{3,2},{4,5},{5,4},{6,7},{7,6},{8,9},{9,8},{10,11... | collective-permute-start | bytes 1105928 | tf_op jit(solution)/shard_map/ppermute | solution.py:594
  51.8 17.3 %collective-permute-start.6 = (s16[144,1280]{1,0:T(8,128)(2,1)S(1)}, s16[144,1280]{1,0:T(8,128)(2,1)S(1)}, u32[]{:S(2)}, u32[]{:S(2)}) collective-permute-start(s16[144,1280]{1,0:T(8,128)(2,1)S(1)} %shard_map.151), channel_id=1, source_target_pairs={{0,1},{1,3},{2,0},{3,5},{4,2},{5,7},{6,4},{7,6},{8,9},{9,11},{10,8... | collective-permute-start | bytes 1105928 | tf_op jit(solution)/shard_map/ppermute | solution.py:594
  53.0 8.4 %collective-permute-start.15 = (s16[144,1280]{1,0:T(8,128)(2,1)S(1)}, s16[144,1280]{1,0:T(8,128)(2,1)S(1)}, u32[]{:S(2)}, u32[]{:S(2)}) collective-permute-start(s16[144,1280]{1,0:T(8,128)(2,1)S(1)} %shard_map.157), channel_id=1, source_target_pairs={{0,1},{1,3},{2,0},{3,5},{4,2},{5,7},{6,4},{7,6},{8,9},{9,11},{10,8... | collective-permute-start | bytes 1105928 | tf_op jit(solution)/shard_map/ppermute | solution.py:594
  54.4 9.4 %collective-permute-start.9 = (s16[144,1280]{1,0:T(8,128)(2,1)S(1)}, s16[144,1280]{1,0:T(8,128)(2,1)S(1)}, u32[]{:S(2)}, u32[]{:S(2)}) collective-permute-start(s16[144,1280]{1,0:T(8,128)(2,1)S(1)} %collective-permute-done.5.previous_ref.refs_2_.refs_1_), channel_id=1, source_target_pairs={{0,1},{1,0},{2,3},{3,2},{4,5},{5,4},{6,7},{7,6},{8,9},{9,8},{10,11... | collective-permute-start | bytes 1105928 | tf_op jit(solution)/shard_map/ppermute | solution.py:594
  61.4 7.8 %collective-permute-start.20 = (s16[144,1280]{1,0:T(8,128)(2,1)S(1)}, s16[144,1280]{1,0:T(8,128)(2,1)S(1)}, u32[]{:S(2)}, u32[]{:S(2)}) collective-permute-start(s16[144,1280]{1,0:T(8,128)(2,1)S(1)} %collective-permute-done.15.refs_2_), channel_id=1, source_target_pairs={{0,1},{1,0},{2,3},{3,2},{4,5},{5,4},{6,7},{7,6},{8,9},{9,8},{10,11... | collective-permute-start | bytes 1105928 | tf_op jit(solution)/shard_map/ppermute | solution.py:594
  69.2 5.5 %collective-permute-start.19 = (s16[144,1280]{1,0:T(8,128)(2,1)S(1)}, s16[144,1280]{1,0:T(8,128)(2,1)S(1)}, u32[]{:S(2)}, u32[]{:S(2)}) collective-permute-start(s16[144,1280]{1,0:T(8,128)(2,1)S(1)} %collective-permute-done.6.refs_2_), channel_id=1, source_target_pairs={{0,1},{1,0},{2,3},{3,2},{4,5},{5,4},{6,7},{7,6},{8,9},{9,8},{10,11... | collective-permute-start | bytes 1105928 | tf_op jit(solution)/shard_map/ppermute | solution.py:594
  80.1 16.3 %copy-start.13 = (s32[128]{0:T(128)S(1)}, s32[128]{0:T(128)}, u32[]{:S(2)}) copy-start(s32[128]{0:T(128)} %param.10) | copy-start | bytes 1540
  82.3 1.4 %collective-permute-start.21 = (f32[8,1792]{1,0:T(8,128)S(1)}, f32[8,1792]{1,0:T(8,128)S(1)}, u32[]{:S(2)}, u32[]{:S(2)}) collective-permute-start(f32[8,1792]{1,0:T(8,128)S(1)} %slice_select_fusion), channel_id=1, source_target_pairs={{0,1},{1,0},{2,3},{3,2},{4,5},{5,4},{6,7},{7,6},{8,9},{9,8},{10,11... | collective-permute-start | bytes 172040 | tf_op jit(solution)/shard_map/ppermute | solution.py:594
  83.8 5.8 %collective-permute-start.23 = (f32[8,1792]{1,0:T(8,128)S(1)}, f32[8,1792]{1,0:T(8,128)S(1)}, u32[]{:S(2)}, u32[]{:S(2)}) collective-permute-start(f32[8,1792]{1,0:T(8,128)S(1)} %select_add_fusion), channel_id=1, source_target_pairs={{0,16},{8,24},{16,0},{24,8},{1,17},{9,25},{17,1},{25,9},{2,18},{10... | collective-permute-start | bytes 172040 | tf_op jit(solution)/shard_map/ppermute | solution.py:594
  85.1 4.6 %collective-permute-start.24 = (f32[8,1792]{1,0:T(8,128)S(1)}, f32[8,1792]{1,0:T(8,128)S(1)}, u32[]{:S(2)}, u32[]{:S(2)}) collective-permute-start(f32[8,1792]{1,0:T(8,128)S(1)} %select_add_fusion), channel_id=1, source_target_pairs={{0,24},{8,16},{16,8},{24,0},{1,25},{9,17},{17,9},{25,1},{2,26},{10... | collective-permute-start | bytes 172040 | tf_op jit(solution)/shard_map/ppermute | solution.py:594
  86.2 3.8 %collective-permute-start.22 = (f32[8,1792]{1,0:T(8,128)S(1)}, f32[8,1792]{1,0:T(8,128)S(1)}, u32[]{:S(2)}, u32[]{:S(2)}) collective-permute-start(f32[8,1792]{1,0:T(8,128)S(1)} %select_add_fusion), channel_id=1, source_target_pairs={{0,8},{8,0},{16,24},{24,16},{1,9},{9,1},{17,25},{25,17},{2,10},{10... | collective-permute-start | bytes 172040 | tf_op jit(solution)/shard_map/ppermute | solution.py:594
  86.5 6.4 %collective-permute-start.25 = (f32[3,5376]{1,0:T(4,128)S(1)}, f32[3,5376]{1,0:T(4,128)S(1)}, u32[]{:S(2)}, u32[]{:S(2)}) collective-permute-start(f32[3,5376]{1,0:T(4,128)S(1)} %slice.32), channel_id=1, source_target_pairs={{1,0},{2,1},{3,2},{4,3},{5,4},{6,5},{7,6},{9,8},{10,9},{11,10},{12... | collective-permute-start | bytes 193544 | tf_op jit(solution)/shard_map/ppermute | solution.py:790
  93.0 5.3 %collective-permute-start.27 = (f32[8,1792]{1,0:T(8,128)S(1)}, f32[8,1792]{1,0:T(8,128)S(1)}, u32[]{:S(2)}, u32[]{:S(2)}) collective-permute-start(f32[8,1792]{1,0:T(8,128)S(1)} %add_add_fusion.1), channel_id=1, source_target_pairs={{0,4},{1,5},{2,6},{3,7},{4,0},{5,1},{6,2},{7,3},{8,12},{9,13},{10,... | collective-permute-start | bytes 172040 | tf_op jit(solution)/shard_map/ppermute | solution.py:594
  94.7 5.7 %collective-permute-start.28 = (f32[8,1792]{1,0:T(8,128)S(1)}, f32[8,1792]{1,0:T(8,128)S(1)}, u32[]{:S(2)}, u32[]{:S(2)}) collective-permute-start(f32[8,1792]{1,0:T(8,128)S(1)} %add_add_fusion.1), channel_id=1, source_target_pairs={{0,6},{1,7},{2,4},{3,5},{4,2},{5,3},{6,0},{7,1},{8,14},{9,15},{10,... | collective-permute-start | bytes 172040 | tf_op jit(solution)/shard_map/ppermute | solution.py:594
  96.4 4.6 %collective-permute-start.26 = (f32[8,1792]{1,0:T(8,128)S(1)}, f32[8,1792]{1,0:T(8,128)S(1)}, u32[]{:S(2)}, u32[]{:S(2)}) collective-permute-start(f32[8,1792]{1,0:T(8,128)S(1)} %add_add_fusion.1), channel_id=1, source_target_pairs={{0,2},{1,3},{2,0},{3,1},{4,6},{5,7},{6,4},{7,5},{8,10},{9,11},{10,... | collective-permute-start | bytes 172040 | tf_op jit(solution)/shard_map/ppermute | solution.py:594
  101.0 1.3 %collective-permute-start.29 = (f32[8,1792]{1,0:T(8,128)S(1)}, f32[8,1792]{1,0:T(8,128)S(1)}, u32[]{:S(2)}, u32[]{:S(2)}) collective-permute-start(f32[8,1792]{1,0:T(8,128)S(1)} %broadcast_multiply_fusion), channel_id=1, source_target_pairs={{0,1},{1,0},{2,3},{3,2},{4,5},{5,4},{6,7},{7,6},{8,9},{9,8},{10,11... | collective-permute-start | bytes 172040 | tf_op jit(solution)/shard_map/ppermute | solution.py:594

commit v3 on v2

--- a/solution.py
+++ b/solution.py
@@ -697,24 +697,22 @@
         chips.append(chip)
         sent += first
 
-    withins = []
-    for j in range(PIECES):
+    def within(j, work):
         here = [part((height, WIDTH), 0, j) for height in (CONV - 1, CONV, 1)]
-        withins.append(
-            call(
-                functools.partial(within_kernel, j),
-                (conv_input, cotangent, work, halo, conv_weight, bias, tab),
-                [HBM, HBM, HBM, *here, whole(table)],
-                [(shape, F32), (shape, F32), (square, F32)],
-                [HBM, HBM, whole(square)],
-                [
-                    vmem(*shape, BF16), vmem(*shape, BF16), vmem(*square), vmem(*shape),
-                    vmem(*shape), vmem(count + 8, WIDTH), sems(3), sems(2),
-                ],
-                us=2.0,
-            )
+        return call(
+            functools.partial(within_kernel, j),
+            (conv_input, cotangent, work, halo, conv_weight, bias, tab),
+            [HBM, HBM, HBM, *here, whole(table)],
+            [(shape, F32), (shape, F32), (square, F32)],
+            [HBM, HBM, whole(square)],
+            [
+                vmem(*shape, BF16), vmem(*shape, BF16), vmem(*square), vmem(*shape),
+                vmem(*shape), vmem(count + 8, WIDTH), sems(3), sems(2),
+            ],
+            us=2.0,
         )
 
+    withins = [within(j, work) for j in range(PIECES - 1)]
     dreads, dkeys, scals = [None] * PIECES, [None] * PIECES, [None] * PIECES
     shared_out = [((count, INNER), BF16), ((count, CH), BF16), ((24, CH), F32)]
     small_out = [((count, STATE), F32), ((count, STATE), F32), ((8, 128), F32)]
@@ -759,6 +757,9 @@
                 hop(turn, hops, received[stream][-1], chips[stream::STREAMS])
                 for stream in range(STREAMS)
             ]
+        if turn == turns - 1:
+            *sent, late = lax.optimization_barrier((*sent, work))
+            withins.append(within(PIECES - 1, late))
         arrived = [permute(value, "seq", along(size)) for value in sent]
         for stream in range(STREAMS):
             got = arrived[stream]

time: 105 us -> 105 us (level)
  waiting for transfers between devices: 11.6 us -> 8.06 us
  Pallas kernels: 55.2 us -> 57.6 us
  starting transfers between devices: 30.4 us -> 31.8 us
    ppermute x28, waiting for transfers between devices: 8.46 us -> 5.03 us  [permute(): return lax.ppermute(value, axis, [(i, target(i)) for i in range(size)])]
    pallas_call x23, Pallas kernels: 55.2 us -> 57.6 us  [call(): pl.pallas_call(kernel, grid=(1,), in_specs=specs, out_specs=out_specs, ou...]
    ppermute x28, starting transfers between devices: 22.7 us -> 24.1 us  [permute(): return lax.ppermute(value, axis, [(i, target(i)) for i in range(size)])]
    unnamed x30 -> x62, local copies, waits for them, and re-layouts: 3.94 us -> 3.07 us
  transfers between devices with their start and end apart: 30 -> 30, of which waited for: 10 -> 7; matrix products, arithmetic and copies ran while one was open for 0% -> 0% of each run, Pallas kernels for 39% -> 41%
where the time goes in v3:
time: 105 us; the launch traced here: 104 us
  Pallas kernels  57.6 us (55%)
  starting transfers between devices  31.8 us (30%)
  waiting for transfers between devices  8.06 us (8%)
  local copies, waits for them, and re-layouts  4.27 us (4%)
  between operations  1.26 us (1%)
    pallas_call x23, Pallas kernels, call(): pl.pallas_call(kernel, grid=(1,), in_specs=specs, out_specs=out_specs, ou...  57.6 us
    ppermute x28, starting transfers between devices, permute(): return lax.ppermute(value, axis, [(i, target(i)) for i in range(size)])  24.1 us
    ppermute x28, waiting for transfers between devices, permute(): return lax.ppermute(value, axis, [(i, target(i)) for i in range(size)])  5.03 us
    ppermute x1, starting transfers between devices, on_device(): halo = lax.ppermute(tail_out, 'seq', [(i, i + 1) for i in range(size - 1)])  4.59 us
    ppermute x1, starting transfers between devices, on_device(): lax.ppermute(misc[8 - CONV + 1:8], 'seq', [(i, i - 1) for i in range(1, s...  3.1 us
    unnamed x62, local copies, waits for them, and re-layouts  3.07 us
    ppermute x1, waiting for transfers between devices, on_device(): lax.ppermute(misc[8 - CONV + 1:8], 'seq', [(i, i - 1) for i in range(1, s...  2.73 us
  transfers between devices with their start and end apart: 30, of which 7 were waited for; matrix products, arithmetic and copies ran while one was open for 0% of the time, Pallas kernels for 41%

profile of v3, /device:TPU:1, one launch (start us, length us, event | category | flops | bytes accessed | tf_op | source)
XLA Modules:
  0.0 103.7 jit_solution(3149323324570119747)
XLA Ops:
  0.6 1.3 %copy-done = bf16[128,5376]{1,0:T(8,128)(2,1)S(1)} copy-done((bf16[128,5376]{1,0:T(8,128)(2,1)S(1)}, bf16[128,5376]{1,0:T(8,128)(2,1)}, u32[]{:S(2)}) %copy-start) | copy-done | bytes 1376280
  2.0 0.7 copy-done.28
  2.8 4.6 %collective-permute-start = (bf16[3,5376]{1,0:T(4,128)(2,1)S(1)}, bf16[3,5376]{1,0:T(4,128)(2,1)S(1)}, u32[]{:S(2)}, u32[]{:S(2)}) collective-permute-start(bf16[3,5376]{1,0:T(4,128)(2,1)S(1)} %shard_map.144), channel_id=1, source_target_pairs={{0,1},{1,2},{2,3},{3,4},{4,5},{5,6},{6,7},{8,9},{9,10},{10,11},{11... | collective-permute-start | bytes 96776 | tf_op jit(solution)/shard_map/ppermute | solution.py:667
  9.2 6.9 %shard_map.146 = (f32[136,1280]{1,0:T(8,128)S(1)}, f32[136,1280]{1,0:T(8,128)S(1)}, f32[136,1280]{1,0:T(8,128)S(1)}, f32[136,1280]{1,0:T(8,128)S(1)}, f32[3328,5120]{1,0:T(8,128)}) custom-call(bf16[128,5376]{1,0:T(8,128)(2,1)S(1)} %copy-done.1, bf16[3,5376]{1,0:T(4,128)(2,1)S(1)} %collective-permute-done.halo_ref.refs_12_, f32[4,5376]{1,0:T(4,128)S(1)} %copy-done.3, ...), custom_call_target="tpu_custom_call" | custom-call | flops 8800000000 | bytes 1000 | tf_op jit(solution)/shard_map/pallas_call | solution.py:571
  16.2 0.5 collective-permute-start.1
  17.2 1.1 %collective-permute-done.6.met_ref.refs_6_ = f32[136,1280]{1,0:T(8,128)S(1)} collective-permute-done((f32[136,1280]{1,0:T(8,128)S(1)}, f32[136,1280]{1,0:T(8,128)S(1)}, u32[]{:S(2)}, u32[]{:S(2)}) %collective-permute-start.6) | collective-permute-done | bytes 696352 | tf_op jit(solution)/shard_map/ppermute | solution.py:594
  18.4 1.6 %shard_map.151 = (f32[136,1280]{1,0:T(8,128)S(1)}, s16[144,1280]{1,0:T(8,128)(2,1)S(1)}) custom-call(f32[3328,5120]{1,0:T(8,128)} %get-tuple-element.95.work_ref.refs_7_, f32[136,1280]{1,0:T(8,128)S(1)} %collective-permute-done.6.met_ref.refs_6_), custom_call_target="tpu_custom_call" | custom-call | flops 1650000000 | bytes 1000 | tf_op jit(solution)/shard_map/pallas_call | solution.py:571
  20.0 1.4 %collective-permute-start.7 = (s16[144,1280]{1,0:T(8,128)(2,1)S(1)}, s16[144,1280]{1,0:T(8,128)(2,1)S(1)}, u32[]{:S(2)}, u32[]{:S(2)}) collective-permute-start(s16[144,1280]{1,0:T(8,128)(2,1)S(1)} %get-tuple-element.76), channel_id=1, source_target_pairs={{0,1},{1,3},{2,0},{3,5},{4,2},{5,7},{6,4},{7,6},{8,9},{9,11},{10,8... | collective-permute-start | bytes 1105928 | tf_op jit(solution)/shard_map/ppermute | solution.py:594
  21.4 1.6 %shard_map.147 = (f32[136,1280]{1,0:T(8,128)S(1)}, s16[144,1280]{1,0:T(8,128)(2,1)S(1)}) custom-call(f32[3328,5120]{1,0:T(8,128)} %get-tuple-element.95.work_ref.refs_7_, f32[136,1280]{1,0:T(8,128)S(1)} %collective-permute-done.1.met_ref.refs_6_), custom_call_target="tpu_custom_call" | custom-call | flops 1650000000 | bytes 1000 | tf_op jit(solution)/shard_map/pallas_call | solution.py:571
  23.0 1.3 %collective-permute-start.2 = (s16[144,1280]{1,0:T(8,128)(2,1)S(1)}, s16[144,1280]{1,0:T(8,128)(2,1)S(1)}, u32[]{:S(2)}, u32[]{:S(2)}) collective-permute-start(s16[144,1280]{1,0:T(8,128)(2,1)S(1)} %get-tuple-element.72), channel_id=1, source_target_pairs={{0,1},{1,3},{2,0},{3,5},{4,2},{5,7},{6,4},{7,6},{8,9},{9,11},{10,8... | collective-permute-start | bytes 1105928 | tf_op jit(solution)/shard_map/ppermute | solution.py:594
  24.3 1.4 %shard_map.152.refs_1_ = f32[136,1280]{1,0:T(8,128)S(1)} custom-call(f32[3328,5120]{1,0:T(8,128)} %get-tuple-element.95.work_ref.refs_7_, f32[136,1280]{1,0:T(8,128)S(1)} %collective-permute-done.8.met_ref.refs_6_), custom_call_target="tpu_custom_call" | custom-call | flops 1650000000 | bytes 1000 | tf_op jit(solution)/shard_map/pallas_call | solution.py:571
  25.8 1.7 %shard_map.148.refs_1_ = f32[136,1280]{1,0:T(8,128)S(1)} custom-call(f32[3328,5120]{1,0:T(8,128)} %get-tuple-element.95.work_ref.refs_7_, f32[136,1280]{1,0:T(8,128)S(1)} %collective-permute-done.3.met_ref.refs_6_), custom_call_target="tpu_custom_call" | custom-call | flops 1650000000 | bytes 1000 | tf_op jit(solution)/shard_map/pallas_call | solution.py:571
  27.6 1.1 %shard_map.153 = s16[144,1280]{1,0:T(8,128)(2,1)} custom-call(s16[144,1280]{1,0:T(8,128)(2,1)S(1)} %collective-permute-done.7.previous_ref.refs_0_, f32[136,1280]{1,0:T(8,128)S(1)} %get-tuple-element.77.refs_0_, f32[136,1280]{1,0:T(8,128)S(1)} %shard_map.152.refs_1_), custom_call_target="tpu_custom_call" | custom-call | flops 880000000 | bytes 1000 | tf_op jit(solution)/shard_map/pallas_call | solution.py:571
  28.7 1.3 %collective-permute-start.9 = (s16[144,1280]{1,0:T(8,128)(2,1)}, s16[144,1280]{1,0:T(8,128)(2,1)}, u32[]{:S(2)}, u32[]{:S(2)}) collective-permute-start(s16[144,1280]{1,0:T(8,128)(2,1)} %shard_map.153), channel_id=1, source_target_pairs={{0,1},{1,3},{2,0},{3,5},{4,2},{5,7},{6,4},{7,6},{8,9},{9,11},{10,8... | collective-permute-start | bytes 1105928 | tf_op jit(solution)/shard_map/ppermute | solution.py:594
  30.0 1.1 %shard_map.149 = s16[144,1280]{1,0:T(8,128)(2,1)} custom-call(s16[144,1280]{1,0:T(8,128)(2,1)S(1)} %collective-permute-done.2.previous_ref.refs_0_, f32[136,1280]{1,0:T(8,128)S(1)} %get-tuple-element.73.refs_0_, f32[136,1280]{1,0:T(8,128)S(1)} %shard_map.148.refs_1_), custom_call_target="tpu_custom_call" | custom-call | flops 880000000 | bytes 1000 | tf_op jit(solution)/shard_map/pallas_call | solution.py:571
  31.1 2.0 %collective-permute-start.4 = (s16[144,1280]{1,0:T(8,128)(2,1)}, s16[144,1280]{1,0:T(8,128)(2,1)}, u32[]{:S(2)}, u32[]{:S(2)}) collective-permute-start(s16[144,1280]{1,0:T(8,128)(2,1)} %shard_map.149), channel_id=1, source_target_pairs={{0,1},{1,3},{2,0},{3,5},{4,2},{5,7},{6,4},{7,6},{8,9},{9,11},{10,8... | collective-permute-start | bytes 1105928 | tf_op jit(solution)/shard_map/ppermute | solution.py:594
  33.1 3.1 %shard_map.158 = (f32[128,1280]{1,0:T(8,128)S(1)}, f32[128,1280]{1,0:T(8,128)S(1)}, f32[128,128]{1,0:T(8,128)S(1)}) custom-call(bf16[128,5376]{1,0:T(8,128)(2,1)S(1)} %copy-done.1, bf16[128,5120]{1,0:T(8,128)(2,1)S(1)} %copy-done.2, f32[3328,5120]{1,0:T(8,128)} %get-tuple-element.95.work_ref.refs_7_, ...), custom_call_target="tpu_custom_call" | custom-call | flops 2200000000 | bytes 1000 | tf_op jit(solution)/shard_map/pallas_call | solution.py:571
  36.3 1.4 %shard_map.154 = s16[144,1280]{1,0:T(8,128)(2,1)S(1)} custom-call(s16[144,1280]{1,0:T(8,128)(2,1)} %collective-permute-done.9.previous_ref.refs_1_.refs_0_, f32[136,1280]{1,0:T(8,128)S(1)} %copy-done.21, f32[136,1280]{1,0:T(8,128)S(1)} %copy-done.15), custom_call_target="tpu_custom_call" | custom-call | flops 880000000 | bytes 1000 | tf_op jit(solution)/shard_map/pallas_call | solution.py:571
  37.8 1.3 %collective-permute-start.10 = (s16[144,1280]{1,0:T(8,128)(2,1)S(1)}, s16[144,1280]{1,0:T(8,128)(2,1)S(1)}, u32[]{:S(2)}, u32[]{:S(2)}) collective-permute-start(s16[144,1280]{1,0:T(8,128)(2,1)S(1)} %shard_map.154), channel_id=1, source_target_pairs={{0,1},{1,3},{2,0},{3,5},{4,2},{5,7},{6,4},{7,6},{8,9},{9,11},{10,8... | collective-permute-start | bytes 1105928 | tf_op jit(solution)/shard_map/ppermute | solution.py:594
  39.1 1.3 %shard_map.150 = s16[144,1280]{1,0:T(8,128)(2,1)S(1)} custom-call(s16[144,1280]{1,0:T(8,128)(2,1)} %collective-permute-done.4.previous_ref.refs_1_.refs_0_, f32[136,1280]{1,0:T(8,128)S(1)} %copy-done.23, f32[136,1280]{1,0:T(8,128)S(1)} %copy-done.13), custom_call_target="tpu_custom_call" | custom-call | flops 880000000 | bytes 1000 | tf_op jit(solution)/shard_map/pallas_call | solution.py:571
  40.4 1.9 %collective-permute-start.5 = (s16[144,1280]{1,0:T(8,128)(2,1)S(1)}, s16[144,1280]{1,0:T(8,128)(2,1)S(1)}, u32[]{:S(2)}, u32[]{:S(2)}) collective-permute-start(s16[144,1280]{1,0:T(8,128)(2,1)S(1)} %shard_map.150), channel_id=1, source_target_pairs={{0,1},{1,3},{2,0},{3,5},{4,2},{5,7},{6,4},{7,6},{8,9},{9,11},{10,8... | collective-permute-start | bytes 1105928 | tf_op jit(solution)/shard_map/ppermute | solution.py:594
  42.3 3.0 %shard_map.157 = (f32[128,1280]{1,0:T(8,128)S(1)}, f32[128,1280]{1,0:T(8,128)S(1)}, f32[128,128]{1,0:T(8,128)S(1)}) custom-call(bf16[128,5376]{1,0:T(8,128)(2,1)S(1)} %copy-done.1, bf16[128,5120]{1,0:T(8,128)(2,1)S(1)} %copy-done.2, f32[3328,5120]{1,0:T(8,128)} %get-tuple-element.95.work_ref.refs_7_, ...), custom_call_target="tpu_custom_call" | custom-call | flops 2200000000 | bytes 1000 | tf_op jit(solution)/shard_map/pallas_call | solution.py:571
  45.3 3.2 %shard_map.162 = (f32[128,1280]{1,0:T(8,128)S(1)}, f32[128,1280]{1,0:T(8,128)S(1)}, f32[128,128]{1,0:T(8,128)S(1)}) custom-call(bf16[128,5376]{1,0:T(8,128)(2,1)S(1)} %copy-done.1, bf16[128,5120]{1,0:T(8,128)(2,1)S(1)} %copy-done.2, f32[3328,5120]{1,0:T(8,128)} %get-tuple-element.95.work_ref.refs_7_, ...), custom_call_target="tpu_custom_call" | custom-call | flops 2200000000 | bytes 1000 | tf_op jit(solution)/shard_map/pallas_call | solution.py:571
  50.5 3.1 %shard_map.161 = (f32[128,1280]{1,0:T(8,128)S(1)}, f32[128,1280]{1,0:T(8,128)S(1)}, f32[128,128]{1,0:T(8,128)S(1)}) custom-call(bf16[128,5376]{1,0:T(8,128)(2,1)S(1)} %copy-done.1, bf16[128,5120]{1,0:T(8,128)(2,1)S(1)} %copy-done.2, f32[3328,5120]{1,0:T(8,128)} %get-tuple-element.95.work_ref.refs_7_, ...), custom_call_target="tpu_custom_call" | custom-call | flops 2200000000 | bytes 1000 | tf_op jit(solution)/shard_map/pallas_call | solution.py:571
  53.6 1.3 %collective-permute-start.15 = (s16[144,1280]{1,0:T(8,128)(2,1)S(1)}, s16[144,1280]{1,0:T(8,128)(2,1)S(1)}, u32[]{:S(2)}, u32[]{:S(2)}) collective-permute-start(s16[144,1280]{1,0:T(8,128)(2,1)S(1)} %shard_map.155), channel_id=1, source_target_pairs={{0,1},{1,3},{2,0},{3,5},{4,2},{5,7},{6,4},{7,6},{8,9},{9,11},{10,8... | collective-permute-start | bytes 1105928 | tf_op jit(solution)/shard_map/ppermute | solution.py:594
  54.9 1.6 %collective-permute-start.11 = (s16[144,1280]{1,0:T(8,128)(2,1)S(1)}, s16[144,1280]{1,0:T(8,128)(2,1)S(1)}, u32[]{:S(2)}, u32[]{:S(2)}) collective-permute-start(s16[144,1280]{1,0:T(8,128)(2,1)S(1)} %shard_map.156), channel_id=1, source_target_pairs={{0,1},{1,3},{2,0},{3,5},{4,2},{5,7},{6,4},{7,6},{8,9},{9,11},{10,8... | collective-permute-start | bytes 1105928 | tf_op jit(solution)/shard_map/ppermute | solution.py:594
  56.6 5.5 %shard_map.159 = (bf16[128,5120]{1,0:T(8,128)(2,1)}, bf16[128,5376]{1,0:T(8,128)(2,1)}, f32[24,5376]{1,0:T(8,128)S(1)}, f32[128,128]{1,0:T(8,128)S(1)}, f32[128,128]{1,0:T(8,128)S(1)}, /*index=5*/f32[8,128]{1,0:T(8,128)S(1)}) custom-call(s16[144,1280]{1,0:T(8,128)(2,1)S(1)} %copy-done.17, ...), custom_call_target="tpu_custom_call" | custom-call | flops 5500000256 | bytes 1000 | tf_op jit(solution)/shard_map/pallas_call | solution.py:571
  62.1 0.6 collective-permute-start.20
  62.6 5.4 %shard_map.160 = (bf16[128,5120]{1,0:T(8,128)(2,1)}, bf16[128,5376]{1,0:T(8,128)(2,1)}, f32[24,5376]{1,0:T(8,128)S(1)}, f32[128,128]{1,0:T(8,128)S(1)}, f32[128,128]{1,0:T(8,128)S(1)}, /*index=5*/f32[8,128]{1,0:T(8,128)S(1)}) custom-call(s16[144,1280]{1,0:T(8,128)(2,1)S(1)} %copy-done.19, ...), custom_call_target="tpu_custom_call", output_to_operand_aliasing={{0}: (16, {}), {1}: (17, {}), {2}: (18, {})} | custom-call | flops 5500000256 | bytes 1000 | tf_op jit(solution)/shard_map/pallas_call | solution.py:571
  68.2 5.4 %shard_map.163 = (bf16[128,5120]{1,0:T(8,128)(2,1)}, bf16[128,5376]{1,0:T(8,128)(2,1)}, f32[24,5376]{1,0:T(8,128)S(1)}, f32[128,128]{1,0:T(8,128)S(1)}, f32[128,128]{1,0:T(8,128)S(1)}, /*index=5*/f32[8,128]{1,0:T(8,128)S(1)}) custom-call(s16[144,1280]{1,0:T(8,128)(2,1)} %collective-permute-done.9.previo, ...), custom_call_target="tpu_custom_call", output_to_operand_aliasing={{0}: (16, {}), {1}: (17, {}), {2}: (18, {})} | custom-call | flops 5500000256 | bytes 1000 | tf_op jit(solution)/shard_map/pallas_call | solution.py:571
  73.7 5.4 %shard_map.164 = (bf16[128,5120]{1,0:T(8,128)(2,1)}, bf16[128,5376]{1,0:T(8,128)(2,1)}, f32[24,5376]{1,0:T(8,128)S(1)}, f32[128,128]{1,0:T(8,128)S(1)}, f32[128,128]{1,0:T(8,128)S(1)}, /*index=5*/f32[8,128]{1,0:T(8,128)S(1)}) custom-call(s16[144,1280]{1,0:T(8,128)(2,1)} %collective-permute-done.4.previo, ...), custom_call_target="tpu_custom_call", output_to_operand_aliasing={{0}: (16, {}), {1}: (17, {}), {2}: (18, {})} | custom-call | flops 5500000256 | bytes 1000 | tf_op jit(solution)/shard_map/pallas_call | solution.py:571
  79.0 2.2 %shard_map.165 = (bf16[128,5376]{1,0:T(8,128)(2,1)}, f32[24,5376]{1,0:T(8,128)S(1)}, f32[16,1792]{1,0:T(8,128)S(1)}) custom-call(bf16[128,5376]{1,0:T(8,128)(2,1)S(1)} %copy-done.1, bf16[3,5376]{1,0:T(4,128)(2,1)S(1)} %collective-permute-done.halo_ref.refs_12_, f32[4,5376]{1,0:T(4,128)S(1)} %copy-done.3, ...), custom_call_target="tpu_custom_call", output_to_operand_aliasing={{0}: (21, {}), {1}: (22, {})} | custom-call | flops 1100000000 | bytes 1000 | tf_op jit(solution)/shard_map/pallas_call | solution.py:571
  81.3 0.5 collective-permute-start.21
  81.8 0.9 collective-permute-done.21
  82.7 1.3 %collective-permute-start.22 = (f32[8,1792]{1,0:T(8,128)S(1)}, f32[8,1792]{1,0:T(8,128)S(1)}, u32[]{:S(2)}, u32[]{:S(2)}) collective-permute-start(f32[8,1792]{1,0:T(8,128)S(1)} %select_add_fusion), channel_id=1, source_target_pairs={{0,8},{8,0},{16,24},{24,16},{1,9},{9,1},{17,25},{25,17},{2,10},{10... | collective-permute-start | bytes 172040 | tf_op jit(solution)/shard_map/ppermute | solution.py:594
  84.0 1.2 %collective-permute-start.23 = (f32[8,1792]{1,0:T(8,128)S(1)}, f32[8,1792]{1,0:T(8,128)S(1)}, u32[]{:S(2)}, u32[]{:S(2)}) collective-permute-start(f32[8,1792]{1,0:T(8,128)S(1)} %select_add_fusion), channel_id=1, source_target_pairs={{0,16},{8,24},{16,0},{24,8},{1,17},{9,25},{17,1},{25,9},{2,18},{10... | collective-permute-start | bytes 172040 | tf_op jit(solution)/shard_map/ppermute | solution.py:594
  85.4 3.1 %collective-permute-start.25 = (f32[3,5376]{1,0:T(4,128)S(1)}, f32[3,5376]{1,0:T(4,128)S(1)}, u32[]{:S(2)}, u32[]{:S(2)}) collective-permute-start(f32[3,5376]{1,0:T(4,128)S(1)} %slice.32), channel_id=1, source_target_pairs={{1,0},{2,1},{3,2},{4,3},{5,4},{6,5},{7,6},{9,8},{10,9},{11,10},{12... | collective-permute-start | bytes 193544 | tf_op jit(solution)/shard_map/ppermute | solution.py:791
  88.6 0.6 collective-permute-done.24
  89.2 2.7 %collective-permute-done.25.back_ref = f32[3,5376]{1,0:T(4,128)S(1)} collective-permute-done((f32[3,5376]{1,0:T(4,128)S(1)}, f32[3,5376]{1,0:T(4,128)S(1)}, u32[]{:S(2)}, u32[]{:S(2)}) %collective-permute-start.25) | collective-permute-done | bytes 64544 | tf_op jit(solution)/shard_map/ppermute | solution.py:791
  91.9 0.7 collective-permute-start.26
  92.6 2.9 %collective-permute-start.28 = (f32[8,1792]{1,0:T(8,128)S(1)}, f32[8,1792]{1,0:T(8,128)S(1)}, u32[]{:S(2)}, u32[]{:S(2)}) collective-permute-start(f32[8,1792]{1,0:T(8,128)S(1)} %add_add_fusion.1), channel_id=1, source_target_pairs={{0,6},{1,7},{2,4},{3,5},{4,2},{5,3},{6,0},{7,1},{8,14},{9,15},{10,... | collective-permute-start | bytes 172040 | tf_op jit(solution)/shard_map/ppermute | solution.py:594
  95.5 1.8 %shard_map.166 = bf16[128,5376]{1,0:T(8,128)(2,1)} custom-call(bf16[128,5376]{1,0:T(8,128)(2,1)} %get-tuple-element.129.gin_ref, f32[24,5376]{1,0:T(8,128)S(1)} %get-tuple-element.127.misc_ref, f32[3,5376]{1,0:T(4,128)S(1)} %collective-permute-done.25.back_ref, s32[1,128]{1,0:T(1,128)S(1)} %bitcast.17), custom_call_target="tpu_custom_call", output_to_operand_aliasing={{}: (0, {})} | custom-call | flops 1100000000 | bytes 1000 | tf_op jit(solution)/shard_map/pallas_call | solution.py:571
  97.2 1.5 %collective-permute-done.28 = f32[8,1792]{1,0:T(8,128)S(1)} collective-permute-done((f32[8,1792]{1,0:T(8,128)S(1)}, f32[8,1792]{1,0:T(8,128)S(1)}, u32[]{:S(2)}, u32[]{:S(2)}) %collective-permute-start.28) | collective-permute-done | bytes 57376 | tf_op jit(solution)/shard_map/ppermute | solution.py:594
  98.7 2.2 %collective-permute-start.29 = (f32[8,1792]{1,0:T(8,128)S(1)}, f32[8,1792]{1,0:T(8,128)S(1)}, u32[]{:S(2)}, u32[]{:S(2)}) collective-permute-start(f32[8,1792]{1,0:T(8,128)S(1)} %broadcast_multiply_fusion), channel_id=1, source_target_pairs={{0,1},{1,0},{2,3},{3,2},{4,5},{5,4},{6,7},{7,6},{8,9},{9,8},{10,11... | collective-permute-start | bytes 172040 | tf_op jit(solution)/shard_map/ppermute | solution.py:594
  100.9 0.9 collective-permute-done.29
  101.9 0.5 slice_bitcast_fusion
  102.4 0.6 reshape.17
  103.0 0.7 pad_maximum_fusion
  (111 shorter events, 5.0 us)
Async XLA Ops:
  2.6 4.8 %copy-start.24 = (f32[128,80]{0,1:T(8,128)S(1)}, f32[128,80]{0,1:T(8,128)}, u32[]{:S(2)}) copy-start(f32[128,80]{0,1:T(8,128)} %param.13) | copy-start | bytes 122884
  2.6 4.8 %copy-start.25 = (f32[80]{0:T(128)S(1)}, f32[80]{0:T(128)}, u32[]{:S(2)}) copy-start(f32[80]{0:T(128)} %param.14) | copy-start | bytes 964
  2.6 4.8 %copy-start.26 = (f32[80]{0:T(128)S(1)}, f32[80]{0:T(128)}, u32[]{:S(2)}) copy-start(f32[80]{0:T(128)} %param.15) | copy-start | bytes 964
  2.6 4.8 %copy-start.27 = (f32[80]{0:T(128)S(1)}, f32[80]{0:T(128)}, u32[]{:S(2)}) copy-start(f32[80]{0:T(128)} %param.16) | copy-start | bytes 964
  2.8 5.7 %collective-permute-start = (bf16[3,5376]{1,0:T(4,128)(2,1)S(1)}, bf16[3,5376]{1,0:T(4,128)(2,1)S(1)}, u32[]{:S(2)}, u32[]{:S(2)}) collective-permute-start(bf16[3,5376]{1,0:T(4,128)(2,1)S(1)} %shard_map.144), channel_id=1, source_target_pairs={{0,1},{1,2},{2,3},{3,4},{4,5},{5,6},{6,7},{8,9},{9,10},{10,11},{11... | collective-permute-start | bytes 96776 | tf_op jit(solution)/shard_map/ppermute | solution.py:667
  16.1 2.2 %collective-permute-start.6 = (f32[136,1280]{1,0:T(8,128)S(1)}, f32[136,1280]{1,0:T(8,128)S(1)}, u32[]{:S(2)}, u32[]{:S(2)}) collective-permute-start(f32[136,1280]{1,0:T(8,128)S(1)} %get-tuple-element.75), channel_id=1, source_target_pairs={{0,1},{1,0},{2,3},{3,2},{4,5},{5,4},{6,7},{7,6},{8,9},{9,8},{10,11... | collective-permute-start | bytes 2088968 | tf_op jit(solution)/shard_map/ppermute | solution.py:594
  16.2 5.2 %collective-permute-start.1 = (f32[136,1280]{1,0:T(8,128)S(1)}, f32[136,1280]{1,0:T(8,128)S(1)}, u32[]{:S(2)}, u32[]{:S(2)}) collective-permute-start(f32[136,1280]{1,0:T(8,128)S(1)} %get-tuple-element.71), channel_id=1, source_target_pairs={{0,1},{1,0},{2,3},{3,2},{4,5},{5,4},{6,7},{7,6},{8,9},{9,8},{10,11... | collective-permute-start | bytes 2088968 | tf_op jit(solution)/shard_map/ppermute | solution.py:594
  16.7 7.6 %collective-permute-start.8 = (f32[136,1280]{1,0:T(8,128)S(1)}, f32[136,1280]{1,0:T(8,128)S(1)}, u32[]{:S(2)}, u32[]{:S(2)}) collective-permute-start(f32[136,1280]{1,0:T(8,128)S(1)} %get-tuple-element.78), channel_id=1, source_target_pairs={{0,1},{1,0},{2,3},{3,2},{4,5},{5,4},{6,7},{7,6},{8,9},{9,8},{10,11... | collective-permute-start | bytes 2088968 | tf_op jit(solution)/shard_map/ppermute | solution.py:594
  16.8 9.0 %collective-permute-start.3 = (f32[136,1280]{1,0:T(8,128)S(1)}, f32[136,1280]{1,0:T(8,128)S(1)}, u32[]{:S(2)}, u32[]{:S(2)}) collective-permute-start(f32[136,1280]{1,0:T(8,128)S(1)} %get-tuple-element.74), channel_id=1, source_target_pairs={{0,1},{1,0},{2,3},{3,2},{4,5},{5,4},{6,7},{7,6},{8,9},{9,8},{10,11... | collective-permute-start | bytes 2088968 | tf_op jit(solution)/shard_map/ppermute | solution.py:594
  20.0 7.6 %copy-start.20 = (f32[136,1280]{1,0:T(8,128)}, f32[136,1280]{1,0:T(8,128)S(1)}, u32[]{:S(2)}) copy-start(f32[136,1280]{1,0:T(8,128)S(1)} %get-tuple-element.77.refs_0_) | copy-start | bytes 2088964
  20.0 7.6 %collective-permute-start.7 = (s16[144,1280]{1,0:T(8,128)(2,1)S(1)}, s16[144,1280]{1,0:T(8,128)(2,1)S(1)}, u32[]{:S(2)}, u32[]{:S(2)}) collective-permute-start(s16[144,1280]{1,0:T(8,128)(2,1)S(1)} %get-tuple-element.76), channel_id=1, source_target_pairs={{0,1},{1,3},{2,0},{3,5},{4,2},{5,7},{6,4},{7,6},{8,9},{9,11},{10,8... | collective-permute-start | bytes 1105928 | tf_op jit(solution)/shard_map/ppermute | solution.py:594
  23.0 7.0 %copy-start.22 = (f32[136,1280]{1,0:T(8,128)}, f32[136,1280]{1,0:T(8,128)S(1)}, u32[]{:S(2)}) copy-start(f32[136,1280]{1,0:T(8,128)S(1)} %get-tuple-element.73.refs_0_) | copy-start | bytes 2088964
  23.0 7.0 %collective-permute-start.2 = (s16[144,1280]{1,0:T(8,128)(2,1)S(1)}, s16[144,1280]{1,0:T(8,128)(2,1)S(1)}, u32[]{:S(2)}, u32[]{:S(2)}) collective-permute-start(s16[144,1280]{1,0:T(8,128)(2,1)S(1)} %get-tuple-element.72), channel_id=1, source_target_pairs={{0,1},{1,3},{2,0},{3,5},{4,2},{5,7},{6,4},{7,6},{8,9},{9,11},{10,8... | collective-permute-start | bytes 1105928 | tf_op jit(solution)/shard_map/ppermute | solution.py:594
  27.5 2.5 %copy-start.12 = (f32[136,1280]{1,0:T(8,128)}, f32[136,1280]{1,0:T(8,128)S(1)}, u32[]{:S(2)}) copy-start(f32[136,1280]{1,0:T(8,128)S(1)} %shard_map.148.refs_1_) | copy-start | bytes 2088964
  28.7 7.6 %collective-permute-start.9 = (s16[144,1280]{1,0:T(8,128)(2,1)}, s16[144,1280]{1,0:T(8,128)(2,1)}, u32[]{:S(2)}, u32[]{:S(2)}) collective-permute-start(s16[144,1280]{1,0:T(8,128)(2,1)} %shard_map.153), channel_id=1, source_target_pairs={{0,1},{1,3},{2,0},{3,5},{4,2},{5,7},{6,4},{7,6},{8,9},{9,11},{10,8... | collective-permute-start | bytes 1105928 | tf_op jit(solution)/shard_map/ppermute | solution.py:594
  31.1 7.9 %collective-permute-start.4 = (s16[144,1280]{1,0:T(8,128)(2,1)}, s16[144,1280]{1,0:T(8,128)(2,1)}, u32[]{:S(2)}, u32[]{:S(2)}) collective-permute-start(s16[144,1280]{1,0:T(8,128)(2,1)} %shard_map.149), channel_id=1, source_target_pairs={{0,1},{1,3},{2,0},{3,5},{4,2},{5,7},{6,4},{7,6},{8,9},{9,11},{10,8... | collective-permute-start | bytes 1105928 | tf_op jit(solution)/shard_map/ppermute | solution.py:594
  33.1 3.2 %copy-start.15 = (f32[136,1280]{1,0:T(8,128)S(1)}, f32[136,1280]{1,0:T(8,128)}, u32[]{:S(2)}) copy-start(f32[136,1280]{1,0:T(8,128)} %copy-done.14) | copy-start | bytes 2088964
  33.1 3.2 %copy-start.21 = (f32[136,1280]{1,0:T(8,128)S(1)}, f32[136,1280]{1,0:T(8,128)}, u32[]{:S(2)}) copy-start(f32[136,1280]{1,0:T(8,128)} %copy-done.20) | copy-start | bytes 2088964
  36.3 2.8 %copy-start.13 = (f32[136,1280]{1,0:T(8,128)S(1)}, f32[136,1280]{1,0:T(8,128)}, u32[]{:S(2)}) copy-start(f32[136,1280]{1,0:T(8,128)} %copy-done.12) | copy-start | bytes 2088964
  36.3 2.8 %copy-start.23 = (f32[136,1280]{1,0:T(8,128)S(1)}, f32[136,1280]{1,0:T(8,128)}, u32[]{:S(2)}) copy-start(f32[136,1280]{1,0:T(8,128)} %copy-done.22) | copy-start | bytes 2088964
  37.8 11.4 %collective-permute-start.10 = (s16[144,1280]{1,0:T(8,128)(2,1)S(1)}, s16[144,1280]{1,0:T(8,128)(2,1)S(1)}, u32[]{:S(2)}, u32[]{:S(2)}) collective-permute-start(s16[144,1280]{1,0:T(8,128)(2,1)S(1)} %shard_map.154), channel_id=1, source_target_pairs={{0,1},{1,3},{2,0},{3,5},{4,2},{5,7},{6,4},{7,6},{8,9},{9,11},{10,8... | collective-permute-start | bytes 1105928 | tf_op jit(solution)/shard_map/ppermute | solution.py:594
  40.4 9.6 %collective-permute-start.5 = (s16[144,1280]{1,0:T(8,128)(2,1)S(1)}, s16[144,1280]{1,0:T(8,128)(2,1)S(1)}, u32[]{:S(2)}, u32[]{:S(2)}) collective-permute-start(s16[144,1280]{1,0:T(8,128)(2,1)S(1)} %shard_map.150), channel_id=1, source_target_pairs={{0,1},{1,3},{2,0},{3,5},{4,2},{5,7},{6,4},{7,6},{8,9},{9,11},{10,8... | collective-permute-start | bytes 1105928 | tf_op jit(solution)/shard_map/ppermute | solution.py:594
  45.3 3.2 %copy-start.17 = (s16[144,1280]{1,0:T(8,128)(2,1)S(1)}, s16[144,1280]{1,0:T(8,128)(2,1)}, u32[]{:S(2)}) copy-start(s16[144,1280]{1,0:T(8,128)(2,1)} %copy-done.16) | copy-start | bytes 1105924
  45.3 3.3 %copy-start.19 = (s16[144,1280]{1,0:T(8,128)(2,1)S(1)}, s16[144,1280]{1,0:T(8,128)(2,1)}, u32[]{:S(2)}) copy-start(s16[144,1280]{1,0:T(8,128)(2,1)} %copy-done.18) | copy-start | bytes 1105924
  48.5 5.1 %collective-permute-start.16 = (s16[144,1280]{1,0:T(8,128)(2,1)S(1)}, s16[144,1280]{1,0:T(8,128)(2,1)S(1)}, u32[]{:S(2)}, u32[]{:S(2)}) collective-permute-start(s16[144,1280]{1,0:T(8,128)(2,1)S(1)} %copy-done.17), channel_id=1, source_target_pairs={{0,1},{1,0},{2,3},{3,2},{4,5},{5,4},{6,7},{7,6},{8,9},{9,8},{10,11... | collective-permute-start | bytes 1105928 | tf_op jit(solution)/shard_map/ppermute | solution.py:594
  48.6 14.0 %collective-permute-start.12 = (s16[144,1280]{1,0:T(8,128)(2,1)S(1)}, s16[144,1280]{1,0:T(8,128)(2,1)S(1)}, u32[]{:S(2)}, u32[]{:S(2)}) collective-permute-start(s16[144,1280]{1,0:T(8,128)(2,1)S(1)} %copy-done.19), channel_id=1, source_target_pairs={{0,1},{1,0},{2,3},{3,2},{4,5},{5,4},{6,7},{7,6},{8,9},{9,8},{10,11... | collective-permute-start | bytes 1105928 | tf_op jit(solution)/shard_map/ppermute | solution.py:594
  49.1 5.8 %collective-permute-start.17 = (s16[144,1280]{1,0:T(8,128)(2,1)}, s16[144,1280]{1,0:T(8,128)(2,1)S(1)}, u32[]{:S(2)}, u32[]{:S(2)}) collective-permute-start(s16[144,1280]{1,0:T(8,128)(2,1)} %collective-permute-done.9.previous_ref.refs_1_.refs_0_), channel_id=1, source_target_pairs={{0,1},{1,0},{2,3},{3,2},{4,5},{5,4},{6,7},{7,6},{8,9},{9,8},{10,11... | collective-permute-start | bytes 1105928 | tf_op jit(solution)/shard_map/ppermute | solution.py:594
  49.2 7.3 %collective-permute-start.18 = (s16[144,1280]{1,0:T(8,128)(2,1)S(1)}, s16[144,1280]{1,0:T(8,128)(2,1)S(1)}, u32[]{:S(2)}, u32[]{:S(2)}) collective-permute-start(s16[144,1280]{1,0:T(8,128)(2,1)S(1)} %collective-permute-done.10.previous_ref.refs_2_.refs_1_), channel_id=1, source_target_pairs={{0,1},{1,0},{2,3},{3,2},{4,5},{5,4},{6,7},{7,6},{8,9},{9,8},{10,11... | collective-permute-start | bytes 1105928 | tf_op jit(solution)/shard_map/ppermute | solution.py:594
  50.0 12.6 %collective-permute-start.13 = (s16[144,1280]{1,0:T(8,128)(2,1)}, s16[144,1280]{1,0:T(8,128)(2,1)S(1)}, u32[]{:S(2)}, u32[]{:S(2)}) collective-permute-start(s16[144,1280]{1,0:T(8,128)(2,1)} %collective-permute-done.4.previous_ref.refs_1_.refs_0_), channel_id=1, source_target_pairs={{0,1},{1,0},{2,3},{3,2},{4,5},{5,4},{6,7},{7,6},{8,9},{9,8},{10,11... | collective-permute-start | bytes 1105928 | tf_op jit(solution)/shard_map/ppermute | solution.py:594
  50.5 6.0 %copy-start.5 = (f32[136,1280]{1,0:T(8,128)S(1)}, f32[136,1280]{1,0:T(8,128)}, u32[]{:S(2)}) copy-start(f32[136,1280]{1,0:T(8,128)} %copy-done.4) | copy-start | bytes 2088964
  53.6 8.5 %collective-permute-start.15 = (s16[144,1280]{1,0:T(8,128)(2,1)S(1)}, s16[144,1280]{1,0:T(8,128)(2,1)S(1)}, u32[]{:S(2)}, u32[]{:S(2)}) collective-permute-start(s16[144,1280]{1,0:T(8,128)(2,1)S(1)} %shard_map.155), channel_id=1, source_target_pairs={{0,1},{1,3},{2,0},{3,5},{4,2},{5,7},{6,4},{7,6},{8,9},{9,11},{10,8... | collective-permute-start | bytes 1105928 | tf_op jit(solution)/shard_map/ppermute | solution.py:594
  54.9 13.2 %collective-permute-start.11 = (s16[144,1280]{1,0:T(8,128)(2,1)S(1)}, s16[144,1280]{1,0:T(8,128)(2,1)S(1)}, u32[]{:S(2)}, u32[]{:S(2)}) collective-permute-start(s16[144,1280]{1,0:T(8,128)(2,1)S(1)} %shard_map.156), channel_id=1, source_target_pairs={{0,1},{1,3},{2,0},{3,5},{4,2},{5,7},{6,4},{7,6},{8,9},{9,11},{10,8... | collective-permute-start | bytes 1105928 | tf_op jit(solution)/shard_map/ppermute | solution.py:594
  56.5 6.1 %collective-permute-start.14 = (s16[144,1280]{1,0:T(8,128)(2,1)S(1)}, s16[144,1280]{1,0:T(8,128)(2,1)S(1)}, u32[]{:S(2)}, u32[]{:S(2)}) collective-permute-start(s16[144,1280]{1,0:T(8,128)(2,1)S(1)} %collective-permute-done.5.previous_ref.refs_2_.refs_1_), channel_id=1, source_target_pairs={{0,1},{1,0},{2,3},{3,2},{4,5},{5,4},{6,7},{7,6},{8,9},{9,8},{10,11... | collective-permute-start | bytes 1105928 | tf_op jit(solution)/shard_map/ppermute | solution.py:594
  56.5 6.1 %copy-start.11 = (f32[136,1280]{1,0:T(8,128)S(1)}, f32[136,1280]{1,0:T(8,128)}, u32[]{:S(2)}) copy-start(f32[136,1280]{1,0:T(8,128)} %copy-done.10) | copy-start | bytes 2088964
  62.1 6.1 %collective-permute-start.20 = (s16[144,1280]{1,0:T(8,128)(2,1)S(1)}, s16[144,1280]{1,0:T(8,128)(2,1)S(1)}, u32[]{:S(2)}, u32[]{:S(2)}) collective-permute-start(s16[144,1280]{1,0:T(8,128)(2,1)S(1)} %collective-permute-done.15.refs_2_), channel_id=1, source_target_pairs={{0,1},{1,0},{2,3},{3,2},{4,5},{5,4},{6,7},{7,6},{8,9},{9,8},{10,11... | collective-permute-start | bytes 1105928 | tf_op jit(solution)/shard_map/ppermute | solution.py:594
  62.6 5.6 %copy-start.9 = (f32[136,1280]{1,0:T(8,128)S(1)}, f32[136,1280]{1,0:T(8,128)}, u32[]{:S(2)}) copy-start(f32[136,1280]{1,0:T(8,128)} %copy-done.8) | copy-start | bytes 2088964
  68.1 5.5 %collective-permute-start.19 = (s16[144,1280]{1,0:T(8,128)(2,1)S(1)}, s16[144,1280]{1,0:T(8,128)(2,1)S(1)}, u32[]{:S(2)}, u32[]{:S(2)}) collective-permute-start(s16[144,1280]{1,0:T(8,128)(2,1)S(1)} %collective-permute-done.11.refs_2_), channel_id=1, source_target_pairs={{0,1},{1,0},{2,3},{3,2},{4,5},{5,4},{6,7},{7,6},{8,9},{9,8},{10,11... | collective-permute-start | bytes 1105928 | tf_op jit(solution)/shard_map/ppermute | solution.py:594
  68.2 5.4 %copy-start.7 = (f32[136,1280]{1,0:T(8,128)S(1)}, f32[136,1280]{1,0:T(8,128)}, u32[]{:S(2)}) copy-start(f32[136,1280]{1,0:T(8,128)} %copy-done.6) | copy-start | bytes 2088964
  79.0 16.4 %copy-start.29 = (s32[128]{0:T(128)S(1)}, s32[128]{0:T(128)}, u32[]{:S(2)}) copy-start(s32[128]{0:T(128)} %param.10) | copy-start | bytes 1540
  81.3 1.4 %collective-permute-start.21 = (f32[8,1792]{1,0:T(8,128)S(1)}, f32[8,1792]{1,0:T(8,128)S(1)}, u32[]{:S(2)}, u32[]{:S(2)}) collective-permute-start(f32[8,1792]{1,0:T(8,128)S(1)} %slice_select_fusion), channel_id=1, source_target_pairs={{0,1},{1,0},{2,3},{3,2},{4,5},{5,4},{6,7},{7,6},{8,9},{9,8},{10,11... | collective-permute-start | bytes 172040 | tf_op jit(solution)/shard_map/ppermute | solution.py:594
  82.7 5.8 %collective-permute-start.22 = (f32[8,1792]{1,0:T(8,128)S(1)}, f32[8,1792]{1,0:T(8,128)S(1)}, u32[]{:S(2)}, u32[]{:S(2)}) collective-permute-start(f32[8,1792]{1,0:T(8,128)S(1)} %select_add_fusion), channel_id=1, source_target_pairs={{0,8},{8,0},{16,24},{24,16},{1,9},{9,1},{17,25},{25,17},{2,10},{10... | collective-permute-start | bytes 172040 | tf_op jit(solution)/shard_map/ppermute | solution.py:594
  84.0 4.6 %collective-permute-start.23 = (f32[8,1792]{1,0:T(8,128)S(1)}, f32[8,1792]{1,0:T(8,128)S(1)}, u32[]{:S(2)}, u32[]{:S(2)}) collective-permute-start(f32[8,1792]{1,0:T(8,128)S(1)} %select_add_fusion), channel_id=1, source_target_pairs={{0,16},{8,24},{16,0},{24,8},{1,17},{9,25},{17,1},{25,9},{2,18},{10... | collective-permute-start | bytes 172040 | tf_op jit(solution)/shard_map/ppermute | solution.py:594
  85.2 3.9 %collective-permute-start.24 = (f32[8,1792]{1,0:T(8,128)S(1)}, f32[8,1792]{1,0:T(8,128)S(1)}, u32[]{:S(2)}, u32[]{:S(2)}) collective-permute-start(f32[8,1792]{1,0:T(8,128)S(1)} %select_add_fusion), channel_id=1, source_target_pairs={{0,24},{8,16},{16,8},{24,0},{1,25},{9,17},{17,9},{25,1},{2,26},{10... | collective-permute-start | bytes 172040 | tf_op jit(solution)/shard_map/ppermute | solution.py:594
  85.4 6.5 %collective-permute-start.25 = (f32[3,5376]{1,0:T(4,128)S(1)}, f32[3,5376]{1,0:T(4,128)S(1)}, u32[]{:S(2)}, u32[]{:S(2)}) collective-permute-start(f32[3,5376]{1,0:T(4,128)S(1)} %slice.32), channel_id=1, source_target_pairs={{1,0},{2,1},{3,2},{4,3},{5,4},{6,5},{7,6},{9,8},{10,9},{11,10},{12... | collective-permute-start | bytes 193544 | tf_op jit(solution)/shard_map/ppermute | solution.py:791
  91.9 5.3 %collective-permute-start.26 = (f32[8,1792]{1,0:T(8,128)S(1)}, f32[8,1792]{1,0:T(8,128)S(1)}, u32[]{:S(2)}, u32[]{:S(2)}) collective-permute-start(f32[8,1792]{1,0:T(8,128)S(1)} %add_add_fusion.1), channel_id=1, source_target_pairs={{0,2},{1,3},{2,0},{3,1},{4,6},{5,7},{6,4},{7,5},{8,10},{9,11},{10,... | collective-permute-start | bytes 172040 | tf_op jit(solution)/shard_map/ppermute | solution.py:594
  92.6 4.7 %collective-permute-start.27 = (f32[8,1792]{1,0:T(8,128)S(1)}, f32[8,1792]{1,0:T(8,128)S(1)}, u32[]{:S(2)}, u32[]{:S(2)}) collective-permute-start(f32[8,1792]{1,0:T(8,128)S(1)} %add_add_fusion.1), channel_id=1, source_target_pairs={{0,4},{1,5},{2,6},{3,7},{4,0},{5,1},{6,2},{7,3},{8,12},{9,13},{10,... | collective-permute-start | bytes 172040 | tf_op jit(solution)/shard_map/ppermute | solution.py:594
  92.6 6.1 %collective-permute-start.28 = (f32[8,1792]{1,0:T(8,128)S(1)}, f32[8,1792]{1,0:T(8,128)S(1)}, u32[]{:S(2)}, u32[]{:S(2)}) collective-permute-start(f32[8,1792]{1,0:T(8,128)S(1)} %add_add_fusion.1), channel_id=1, source_target_pairs={{0,6},{1,7},{2,4},{3,5},{4,2},{5,3},{6,0},{7,1},{8,14},{9,15},{10,... | collective-permute-start | bytes 172040 | tf_op jit(solution)/shard_map/ppermute | solution.py:594
  98.7 3.1 %collective-permute-start.29 = (f32[8,1792]{1,0:T(8,128)S(1)}, f32[8,1792]{1,0:T(8,128)S(1)}, u32[]{:S(2)}, u32[]{:S(2)}) collective-permute-start(f32[8,1792]{1,0:T(8,128)S(1)} %broadcast_multiply_fusion), channel_id=1, source_target_pairs={{0,1},{1,0},{2,3},{3,2},{4,5},{5,4},{6,7},{7,6},{8,9},{9,8},{10,11... | collective-permute-start | bytes 172040 | tf_op jit(solution)/shard_map/ppermute | solution.py:594
  (13 other events, 17.9 us)

commit v4 on v3

--- a/solution.py
+++ b/solution.py
@@ -39,7 +39,7 @@
 ACROSS = ((1,), (1,))
 ANY = pl.BlockSpec(memory_space=pl.ANY)
 HBM = pl.BlockSpec(memory_space=pltpu.HBM)
-VMEM_LIMIT = 24 * 1024 * 1024
+VMEM_LIMIT = 40 * 1024 * 1024
 
 MASK, ENTRY, LEAVE, PULL, RATE, DECAY, RUN, FAR_AT, ROW, SMASK = range(0, 1280, 128)
 SKIP = ROW + HEADS
@@ -812,7 +812,7 @@
     lower = jnp.where(first, value, other)
     upper = jnp.where(first, other, value)
     grad_weight = jnp.concatenate([lower[:CONV], lower[CONV:], upper[:CONV]], axis=1)
-    grad_bias = upper[CONV : CONV + 3].reshape(CH)
+    grad_bias = jnp.concatenate([upper[CONV + i] for i in range(3)])
     params = [upper[CONV + 3, i : i + HEADS] for i in (0, 128, 256)]
     return (output, grad_input, grad_weight, grad_bias, *params)
 

time: 105 us -> 105 us (level)
  no operation moved by 1% of the time
where the time goes in v4:
time: 105 us; the launch traced here: 104 us
  Pallas kernels  57.6 us (55%)
  starting transfers between devices  31.8 us (30%)
  waiting for transfers between devices  8.06 us (8%)
  local copies, waits for them, and re-layouts  3.71 us (4%)
  other arithmetic  1.34 us (1%)
  between operations  1.26 us (1%)
    pallas_call x23, Pallas kernels, call(): pl.pallas_call(kernel, grid=(1,), in_specs=specs, out_specs=out_specs, ou...  57.6 us
    ppermute x28, starting transfers between devices, permute(): return lax.ppermute(value, axis, [(i, target(i)) for i in range(size)])  24.1 us
    ppermute x28, waiting for transfers between devices, permute(): return lax.ppermute(value, axis, [(i, target(i)) for i in range(size)])  5.04 us
    ppermute x1, starting transfers between devices, on_device(): halo = lax.ppermute(tail_out, 'seq', [(i, i + 1) for i in range(size - 1)])  4.59 us
    ppermute x1, starting transfers between devices, on_device(): lax.ppermute(misc[8 - CONV + 1:8], 'seq', [(i, i - 1) for i in range(1, s...  3.1 us
    unnamed x62, local copies, waits for them, and re-layouts  3.07 us
    ppermute x1, waiting for transfers between devices, on_device(): lax.ppermute(misc[8 - CONV + 1:8], 'seq', [(i, i - 1) for i in range(1, s...  2.72 us
  transfers between devices with their start and end apart: 30, of which 7 were waited for; matrix products, arithmetic and copies ran while one was open for 0% of the time, Pallas kernels for 41%

profile of v4, /device:TPU:1, one launch (start us, length us, event | category | flops | bytes accessed | tf_op | source)
XLA Modules:
  0.0 103.7 jit_solution(6592701819352993385)
XLA Ops:
  0.6 1.3 %copy-done = bf16[128,5376]{1,0:T(8,128)(2,1)S(1)} copy-done((bf16[128,5376]{1,0:T(8,128)(2,1)S(1)}, bf16[128,5376]{1,0:T(8,128)(2,1)}, u32[]{:S(2)}) %copy-start) | copy-done | bytes 1376280
  2.0 0.7 copy-done.28
  2.8 4.6 %collective-permute-start = (bf16[3,5376]{1,0:T(4,128)(2,1)S(1)}, bf16[3,5376]{1,0:T(4,128)(2,1)S(1)}, u32[]{:S(2)}, u32[]{:S(2)}) collective-permute-start(bf16[3,5376]{1,0:T(4,128)(2,1)S(1)} %shard_map.144), channel_id=1, source_target_pairs={{0,1},{1,2},{2,3},{3,4},{4,5},{5,6},{6,7},{8,9},{9,10},{10,11},{11... | collective-permute-start | bytes 96776 | tf_op jit(solution)/shard_map/ppermute | solution.py:667
  9.2 6.9 %shard_map.146 = (f32[136,1280]{1,0:T(8,128)S(1)}, f32[136,1280]{1,0:T(8,128)S(1)}, f32[136,1280]{1,0:T(8,128)S(1)}, f32[136,1280]{1,0:T(8,128)S(1)}, f32[3328,5120]{1,0:T(8,128)}) custom-call(bf16[128,5376]{1,0:T(8,128)(2,1)S(1)} %copy-done.1, bf16[3,5376]{1,0:T(4,128)(2,1)S(1)} %collective-permute-done.halo_ref.refs_12_, f32[4,5376]{1,0:T(4,128)S(1)} %copy-done.3, ...), custom_call_target="tpu_custom_call" | custom-call | flops 8800000000 | bytes 1000 | tf_op jit(solution)/shard_map/pallas_call | solution.py:571
  16.2 0.5 collective-permute-start.1
  17.2 1.1 %collective-permute-done.6.met_ref.refs_6_ = f32[136,1280]{1,0:T(8,128)S(1)} collective-permute-done((f32[136,1280]{1,0:T(8,128)S(1)}, f32[136,1280]{1,0:T(8,128)S(1)}, u32[]{:S(2)}, u32[]{:S(2)}) %collective-permute-start.6) | collective-permute-done | bytes 696352 | tf_op jit(solution)/shard_map/ppermute | solution.py:594
  18.3 1.6 %shard_map.151 = (f32[136,1280]{1,0:T(8,128)S(1)}, s16[144,1280]{1,0:T(8,128)(2,1)S(1)}) custom-call(f32[3328,5120]{1,0:T(8,128)} %get-tuple-element.95.work_ref.refs_7_, f32[136,1280]{1,0:T(8,128)S(1)} %collective-permute-done.6.met_ref.refs_6_), custom_call_target="tpu_custom_call" | custom-call | flops 1650000000 | bytes 1000 | tf_op jit(solution)/shard_map/pallas_call | solution.py:571
  20.0 1.4 %collective-permute-start.7 = (s16[144,1280]{1,0:T(8,128)(2,1)S(1)}, s16[144,1280]{1,0:T(8,128)(2,1)S(1)}, u32[]{:S(2)}, u32[]{:S(2)}) collective-permute-start(s16[144,1280]{1,0:T(8,128)(2,1)S(1)} %get-tuple-element.76), channel_id=1, source_target_pairs={{0,1},{1,3},{2,0},{3,5},{4,2},{5,7},{6,4},{7,6},{8,9},{9,11},{10,8... | collective-permute-start | bytes 1105928 | tf_op jit(solution)/shard_map/ppermute | solution.py:594
  21.4 1.6 %shard_map.147 = (f32[136,1280]{1,0:T(8,128)S(1)}, s16[144,1280]{1,0:T(8,128)(2,1)S(1)}) custom-call(f32[3328,5120]{1,0:T(8,128)} %get-tuple-element.95.work_ref.refs_7_, f32[136,1280]{1,0:T(8,128)S(1)} %collective-permute-done.1.met_ref.refs_6_), custom_call_target="tpu_custom_call" | custom-call | flops 1650000000 | bytes 1000 | tf_op jit(solution)/shard_map/pallas_call | solution.py:571
  23.0 1.3 %collective-permute-start.2 = (s16[144,1280]{1,0:T(8,128)(2,1)S(1)}, s16[144,1280]{1,0:T(8,128)(2,1)S(1)}, u32[]{:S(2)}, u32[]{:S(2)}) collective-permute-start(s16[144,1280]{1,0:T(8,128)(2,1)S(1)} %get-tuple-element.72), channel_id=1, source_target_pairs={{0,1},{1,3},{2,0},{3,5},{4,2},{5,7},{6,4},{7,6},{8,9},{9,11},{10,8... | collective-permute-start | bytes 1105928 | tf_op jit(solution)/shard_map/ppermute | solution.py:594
  24.3 1.4 %shard_map.152.refs_1_ = f32[136,1280]{1,0:T(8,128)S(1)} custom-call(f32[3328,5120]{1,0:T(8,128)} %get-tuple-element.95.work_ref.refs_7_, f32[136,1280]{1,0:T(8,128)S(1)} %collective-permute-done.8.met_ref.refs_6_), custom_call_target="tpu_custom_call" | custom-call | flops 1650000000 | bytes 1000 | tf_op jit(solution)/shard_map/pallas_call | solution.py:571
  25.8 1.7 %shard_map.148.refs_1_ = f32[136,1280]{1,0:T(8,128)S(1)} custom-call(f32[3328,5120]{1,0:T(8,128)} %get-tuple-element.95.work_ref.refs_7_, f32[136,1280]{1,0:T(8,128)S(1)} %collective-permute-done.3.met_ref.refs_6_), custom_call_target="tpu_custom_call" | custom-call | flops 1650000000 | bytes 1000 | tf_op jit(solution)/shard_map/pallas_call | solution.py:571
  27.6 1.1 %shard_map.153 = s16[144,1280]{1,0:T(8,128)(2,1)} custom-call(s16[144,1280]{1,0:T(8,128)(2,1)S(1)} %collective-permute-done.7.previous_ref.refs_0_, f32[136,1280]{1,0:T(8,128)S(1)} %get-tuple-element.77.refs_0_, f32[136,1280]{1,0:T(8,128)S(1)} %shard_map.152.refs_1_), custom_call_target="tpu_custom_call" | custom-call | flops 880000000 | bytes 1000 | tf_op jit(solution)/shard_map/pallas_call | solution.py:571
  28.7 1.3 %collective-permute-start.9 = (s16[144,1280]{1,0:T(8,128)(2,1)}, s16[144,1280]{1,0:T(8,128)(2,1)}, u32[]{:S(2)}, u32[]{:S(2)}) collective-permute-start(s16[144,1280]{1,0:T(8,128)(2,1)} %shard_map.153), channel_id=1, source_target_pairs={{0,1},{1,3},{2,0},{3,5},{4,2},{5,7},{6,4},{7,6},{8,9},{9,11},{10,8... | collective-permute-start | bytes 1105928 | tf_op jit(solution)/shard_map/ppermute | solution.py:594
  30.0 1.1 %shard_map.149 = s16[144,1280]{1,0:T(8,128)(2,1)} custom-call(s16[144,1280]{1,0:T(8,128)(2,1)S(1)} %collective-permute-done.2.previous_ref.refs_0_, f32[136,1280]{1,0:T(8,128)S(1)} %get-tuple-element.73.refs_0_, f32[136,1280]{1,0:T(8,128)S(1)} %shard_map.148.refs_1_), custom_call_target="tpu_custom_call" | custom-call | flops 880000000 | bytes 1000 | tf_op jit(solution)/shard_map/pallas_call | solution.py:571
  31.1 2.0 %collective-permute-start.4 = (s16[144,1280]{1,0:T(8,128)(2,1)}, s16[144,1280]{1,0:T(8,128)(2,1)}, u32[]{:S(2)}, u32[]{:S(2)}) collective-permute-start(s16[144,1280]{1,0:T(8,128)(2,1)} %shard_map.149), channel_id=1, source_target_pairs={{0,1},{1,3},{2,0},{3,5},{4,2},{5,7},{6,4},{7,6},{8,9},{9,11},{10,8... | collective-permute-start | bytes 1105928 | tf_op jit(solution)/shard_map/ppermute | solution.py:594
  33.1 3.1 %shard_map.158 = (f32[128,1280]{1,0:T(8,128)S(1)}, f32[128,1280]{1,0:T(8,128)S(1)}, f32[128,128]{1,0:T(8,128)S(1)}) custom-call(bf16[128,5376]{1,0:T(8,128)(2,1)S(1)} %copy-done.1, bf16[128,5120]{1,0:T(8,128)(2,1)S(1)} %copy-done.2, f32[3328,5120]{1,0:T(8,128)} %get-tuple-element.95.work_ref.refs_7_, ...), custom_call_target="tpu_custom_call" | custom-call | flops 2200000000 | bytes 1000 | tf_op jit(solution)/shard_map/pallas_call | solution.py:571
  36.3 1.4 %shard_map.154 = s16[144,1280]{1,0:T(8,128)(2,1)S(1)} custom-call(s16[144,1280]{1,0:T(8,128)(2,1)} %collective-permute-done.9.previous_ref.refs_1_.refs_0_, f32[136,1280]{1,0:T(8,128)S(1)} %copy-done.21, f32[136,1280]{1,0:T(8,128)S(1)} %copy-done.15), custom_call_target="tpu_custom_call" | custom-call | flops 880000000 | bytes 1000 | tf_op jit(solution)/shard_map/pallas_call | solution.py:571
  37.7 1.3 %collective-permute-start.10 = (s16[144,1280]{1,0:T(8,128)(2,1)S(1)}, s16[144,1280]{1,0:T(8,128)(2,1)S(1)}, u32[]{:S(2)}, u32[]{:S(2)}) collective-permute-start(s16[144,1280]{1,0:T(8,128)(2,1)S(1)} %shard_map.154), channel_id=1, source_target_pairs={{0,1},{1,3},{2,0},{3,5},{4,2},{5,7},{6,4},{7,6},{8,9},{9,11},{10,8... | collective-permute-start | bytes 1105928 | tf_op jit(solution)/shard_map/ppermute | solution.py:594
  39.1 1.3 %shard_map.150 = s16[144,1280]{1,0:T(8,128)(2,1)S(1)} custom-call(s16[144,1280]{1,0:T(8,128)(2,1)} %collective-permute-done.4.previous_ref.refs_1_.refs_0_, f32[136,1280]{1,0:T(8,128)S(1)} %copy-done.23, f32[136,1280]{1,0:T(8,128)S(1)} %copy-done.13), custom_call_target="tpu_custom_call" | custom-call | flops 880000000 | bytes 1000 | tf_op jit(solution)/shard_map/pallas_call | solution.py:571
  40.4 1.9 %collective-permute-start.5 = (s16[144,1280]{1,0:T(8,128)(2,1)S(1)}, s16[144,1280]{1,0:T(8,128)(2,1)S(1)}, u32[]{:S(2)}, u32[]{:S(2)}) collective-permute-start(s16[144,1280]{1,0:T(8,128)(2,1)S(1)} %shard_map.150), channel_id=1, source_target_pairs={{0,1},{1,3},{2,0},{3,5},{4,2},{5,7},{6,4},{7,6},{8,9},{9,11},{10,8... | collective-permute-start | bytes 1105928 | tf_op jit(solution)/shard_map/ppermute | solution.py:594
  42.3 3.0 %shard_map.157 = (f32[128,1280]{1,0:T(8,128)S(1)}, f32[128,1280]{1,0:T(8,128)S(1)}, f32[128,128]{1,0:T(8,128)S(1)}) custom-call(bf16[128,5376]{1,0:T(8,128)(2,1)S(1)} %copy-done.1, bf16[128,5120]{1,0:T(8,128)(2,1)S(1)} %copy-done.2, f32[3328,5120]{1,0:T(8,128)} %get-tuple-element.95.work_ref.refs_7_, ...), custom_call_target="tpu_custom_call" | custom-call | flops 2200000000 | bytes 1000 | tf_op jit(solution)/shard_map/pallas_call | solution.py:571
  45.3 3.2 %shard_map.162 = (f32[128,1280]{1,0:T(8,128)S(1)}, f32[128,1280]{1,0:T(8,128)S(1)}, f32[128,128]{1,0:T(8,128)S(1)}) custom-call(bf16[128,5376]{1,0:T(8,128)(2,1)S(1)} %copy-done.1, bf16[128,5120]{1,0:T(8,128)(2,1)S(1)} %copy-done.2, f32[3328,5120]{1,0:T(8,128)} %get-tuple-element.95.work_ref.refs_7_, ...), custom_call_target="tpu_custom_call" | custom-call | flops 2200000000 | bytes 1000 | tf_op jit(solution)/shard_map/pallas_call | solution.py:571
  50.5 3.1 %shard_map.161 = (f32[128,1280]{1,0:T(8,128)S(1)}, f32[128,1280]{1,0:T(8,128)S(1)}, f32[128,128]{1,0:T(8,128)S(1)}) custom-call(bf16[128,5376]{1,0:T(8,128)(2,1)S(1)} %copy-done.1, bf16[128,5120]{1,0:T(8,128)(2,1)S(1)} %copy-done.2, f32[3328,5120]{1,0:T(8,128)} %get-tuple-element.95.work_ref.refs_7_, ...), custom_call_target="tpu_custom_call" | custom-call | flops 2200000000 | bytes 1000 | tf_op jit(solution)/shard_map/pallas_call | solution.py:571
  53.6 1.3 %collective-permute-start.15 = (s16[144,1280]{1,0:T(8,128)(2,1)S(1)}, s16[144,1280]{1,0:T(8,128)(2,1)S(1)}, u32[]{:S(2)}, u32[]{:S(2)}) collective-permute-start(s16[144,1280]{1,0:T(8,128)(2,1)S(1)} %shard_map.155), channel_id=1, source_target_pairs={{0,1},{1,3},{2,0},{3,5},{4,2},{5,7},{6,4},{7,6},{8,9},{9,11},{10,8... | collective-permute-start | bytes 1105928 | tf_op jit(solution)/shard_map/ppermute | solution.py:594
  54.9 1.6 %collective-permute-start.11 = (s16[144,1280]{1,0:T(8,128)(2,1)S(1)}, s16[144,1280]{1,0:T(8,128)(2,1)S(1)}, u32[]{:S(2)}, u32[]{:S(2)}) collective-permute-start(s16[144,1280]{1,0:T(8,128)(2,1)S(1)} %shard_map.156), channel_id=1, source_target_pairs={{0,1},{1,3},{2,0},{3,5},{4,2},{5,7},{6,4},{7,6},{8,9},{9,11},{10,8... | collective-permute-start | bytes 1105928 | tf_op jit(solution)/shard_map/ppermute | solution.py:594
  56.5 5.5 %shard_map.159 = (bf16[128,5120]{1,0:T(8,128)(2,1)}, bf16[128,5376]{1,0:T(8,128)(2,1)}, f32[24,5376]{1,0:T(8,128)S(1)}, f32[128,128]{1,0:T(8,128)S(1)}, f32[128,128]{1,0:T(8,128)S(1)}, /*index=5*/f32[8,128]{1,0:T(8,128)S(1)}) custom-call(s16[144,1280]{1,0:T(8,128)(2,1)S(1)} %copy-done.17, ...), custom_call_target="tpu_custom_call" | custom-call | flops 5500000256 | bytes 1000 | tf_op jit(solution)/shard_map/pallas_call | solution.py:571
  62.0 0.6 collective-permute-start.20
  62.6 5.4 %shard_map.160 = (bf16[128,5120]{1,0:T(8,128)(2,1)}, bf16[128,5376]{1,0:T(8,128)(2,1)}, f32[24,5376]{1,0:T(8,128)S(1)}, f32[128,128]{1,0:T(8,128)S(1)}, f32[128,128]{1,0:T(8,128)S(1)}, /*index=5*/f32[8,128]{1,0:T(8,128)S(1)}) custom-call(s16[144,1280]{1,0:T(8,128)(2,1)S(1)} %copy-done.19, ...), custom_call_target="tpu_custom_call", output_to_operand_aliasing={{0}: (16, {}), {1}: (17, {}), {2}: (18, {})} | custom-call | flops 5500000256 | bytes 1000 | tf_op jit(solution)/shard_map/pallas_call | solution.py:571
  68.2 5.4 %shard_map.163 = (bf16[128,5120]{1,0:T(8,128)(2,1)}, bf16[128,5376]{1,0:T(8,128)(2,1)}, f32[24,5376]{1,0:T(8,128)S(1)}, f32[128,128]{1,0:T(8,128)S(1)}, f32[128,128]{1,0:T(8,128)S(1)}, /*index=5*/f32[8,128]{1,0:T(8,128)S(1)}) custom-call(s16[144,1280]{1,0:T(8,128)(2,1)} %collective-permute-done.9.previo, ...), custom_call_target="tpu_custom_call", output_to_operand_aliasing={{0}: (16, {}), {1}: (17, {}), {2}: (18, {})} | custom-call | flops 5500000256 | bytes 1000 | tf_op jit(solution)/shard_map/pallas_call | solution.py:571
  73.6 5.4 %shard_map.164 = (bf16[128,5120]{1,0:T(8,128)(2,1)}, bf16[128,5376]{1,0:T(8,128)(2,1)}, f32[24,5376]{1,0:T(8,128)S(1)}, f32[128,128]{1,0:T(8,128)S(1)}, f32[128,128]{1,0:T(8,128)S(1)}, /*index=5*/f32[8,128]{1,0:T(8,128)S(1)}) custom-call(s16[144,1280]{1,0:T(8,128)(2,1)} %collective-permute-done.4.previo, ...), custom_call_target="tpu_custom_call", output_to_operand_aliasing={{0}: (16, {}), {1}: (17, {}), {2}: (18, {})} | custom-call | flops 5500000256 | bytes 1000 | tf_op jit(solution)/shard_map/pallas_call | solution.py:571
  79.0 2.2 %shard_map.165 = (bf16[128,5376]{1,0:T(8,128)(2,1)}, f32[24,5376]{1,0:T(8,128)S(1)}, f32[16,1792]{1,0:T(8,128)S(1)}) custom-call(bf16[128,5376]{1,0:T(8,128)(2,1)S(1)} %copy-done.1, bf16[3,5376]{1,0:T(4,128)(2,1)S(1)} %collective-permute-done.halo_ref.refs_12_, f32[4,5376]{1,0:T(4,128)S(1)} %copy-done.3, ...), custom_call_target="tpu_custom_call", output_to_operand_aliasing={{0}: (21, {}), {1}: (22, {})} | custom-call | flops 1100000000 | bytes 1000 | tf_op jit(solution)/shard_map/pallas_call | solution.py:571
  81.3 0.5 collective-permute-start.21
  81.8 0.9 collective-permute-done.21
  82.7 1.3 %collective-permute-start.22 = (f32[8,1792]{1,0:T(8,128)S(1)}, f32[8,1792]{1,0:T(8,128)S(1)}, u32[]{:S(2)}, u32[]{:S(2)}) collective-permute-start(f32[8,1792]{1,0:T(8,128)S(1)} %select_add_fusion), channel_id=1, source_target_pairs={{0,8},{8,0},{16,24},{24,16},{1,9},{9,1},{17,25},{25,17},{2,10},{10... | collective-permute-start | bytes 172040 | tf_op jit(solution)/shard_map/ppermute | solution.py:594
  84.0 1.2 %collective-permute-start.23 = (f32[8,1792]{1,0:T(8,128)S(1)}, f32[8,1792]{1,0:T(8,128)S(1)}, u32[]{:S(2)}, u32[]{:S(2)}) collective-permute-start(f32[8,1792]{1,0:T(8,128)S(1)} %select_add_fusion), channel_id=1, source_target_pairs={{0,16},{8,24},{16,0},{24,8},{1,17},{9,25},{17,1},{25,9},{2,18},{10... | collective-permute-start | bytes 172040 | tf_op jit(solution)/shard_map/ppermute | solution.py:594
  85.4 3.1 %collective-permute-start.25 = (f32[3,5376]{1,0:T(4,128)S(1)}, f32[3,5376]{1,0:T(4,128)S(1)}, u32[]{:S(2)}, u32[]{:S(2)}) collective-permute-start(f32[3,5376]{1,0:T(4,128)S(1)} %slice.38), channel_id=1, source_target_pairs={{1,0},{2,1},{3,2},{4,3},{5,4},{6,5},{7,6},{9,8},{10,9},{11,10},{12... | collective-permute-start | bytes 193544 | tf_op jit(solution)/shard_map/ppermute | solution.py:791
  88.6 0.6 collective-permute-done.24
  89.2 2.7 %collective-permute-done.25.back_ref = f32[3,5376]{1,0:T(4,128)S(1)} collective-permute-done((f32[3,5376]{1,0:T(4,128)S(1)}, f32[3,5376]{1,0:T(4,128)S(1)}, u32[]{:S(2)}, u32[]{:S(2)}) %collective-permute-start.25) | collective-permute-done | bytes 64544 | tf_op jit(solution)/shard_map/ppermute | solution.py:791
  91.9 0.7 collective-permute-start.26
  92.5 2.9 %collective-permute-start.28 = (f32[8,1792]{1,0:T(8,128)S(1)}, f32[8,1792]{1,0:T(8,128)S(1)}, u32[]{:S(2)}, u32[]{:S(2)}) collective-permute-start(f32[8,1792]{1,0:T(8,128)S(1)} %add_add_fusion.1), channel_id=1, source_target_pairs={{0,6},{1,7},{2,4},{3,5},{4,2},{5,3},{6,0},{7,1},{8,14},{9,15},{10,... | collective-permute-start | bytes 172040 | tf_op jit(solution)/shard_map/ppermute | solution.py:594
  95.4 1.8 %shard_map.166 = bf16[128,5376]{1,0:T(8,128)(2,1)} custom-call(bf16[128,5376]{1,0:T(8,128)(2,1)} %get-tuple-element.129.gin_ref, f32[24,5376]{1,0:T(8,128)S(1)} %get-tuple-element.127.misc_ref, f32[3,5376]{1,0:T(4,128)S(1)} %collective-permute-done.25.back_ref, s32[1,128]{1,0:T(1,128)S(1)} %bitcast.17), custom_call_target="tpu_custom_call", output_to_operand_aliasing={{}: (0, {})} | custom-call | flops 1100000000 | bytes 1000 | tf_op jit(solution)/shard_map/pallas_call | solution.py:571
  97.2 1.5 %collective-permute-done.28 = f32[8,1792]{1,0:T(8,128)S(1)} collective-permute-done((f32[8,1792]{1,0:T(8,128)S(1)}, f32[8,1792]{1,0:T(8,128)S(1)}, u32[]{:S(2)}, u32[]{:S(2)}) %collective-permute-start.28) | collective-permute-done | bytes 57376 | tf_op jit(solution)/shard_map/ppermute | solution.py:594
  98.7 2.2 %collective-permute-start.29 = (f32[8,1792]{1,0:T(8,128)S(1)}, f32[8,1792]{1,0:T(8,128)S(1)}, u32[]{:S(2)}, u32[]{:S(2)}) collective-permute-start(f32[8,1792]{1,0:T(8,128)S(1)} %broadcast_multiply_fusion), channel_id=1, source_target_pairs={{0,1},{1,0},{2,3},{3,2},{4,5},{5,4},{6,7},{7,6},{8,9},{9,8},{10,11... | collective-permute-start | bytes 172040 | tf_op jit(solution)/shard_map/ppermute | solution.py:594
  100.9 0.9 collective-permute-done.29
  101.9 0.5 slice_bitcast_fusion
  102.4 0.6 pad_maximum_fusion.1
  103.1 0.7 pad_maximum_fusion
  (111 shorter events, 5.0 us)
Async XLA Ops:
  2.6 4.8 %copy-start.24 = (f32[128,80]{0,1:T(8,128)S(1)}, f32[128,80]{0,1:T(8,128)}, u32[]{:S(2)}) copy-start(f32[128,80]{0,1:T(8,128)} %param.13) | copy-start | bytes 122884
  2.6 4.8 %copy-start.25 = (f32[80]{0:T(128)S(1)}, f32[80]{0:T(128)}, u32[]{:S(2)}) copy-start(f32[80]{0:T(128)} %param.14) | copy-start | bytes 964
  2.6 4.8 %copy-start.26 = (f32[80]{0:T(128)S(1)}, f32[80]{0:T(128)}, u32[]{:S(2)}) copy-start(f32[80]{0:T(128)} %param.15) | copy-start | bytes 964
  2.6 4.8 %copy-start.27 = (f32[80]{0:T(128)S(1)}, f32[80]{0:T(128)}, u32[]{:S(2)}) copy-start(f32[80]{0:T(128)} %param.16) | copy-start | bytes 964
  2.8 5.7 %collective-permute-start = (bf16[3,5376]{1,0:T(4,128)(2,1)S(1)}, bf16[3,5376]{1,0:T(4,128)(2,1)S(1)}, u32[]{:S(2)}, u32[]{:S(2)}) collective-permute-start(bf16[3,5376]{1,0:T(4,128)(2,1)S(1)} %shard_map.144), channel_id=1, source_target_pairs={{0,1},{1,2},{2,3},{3,4},{4,5},{5,6},{6,7},{8,9},{9,10},{10,11},{11... | collective-permute-start | bytes 96776 | tf_op jit(solution)/shard_map/ppermute | solution.py:667
  16.1 2.2 %collective-permute-start.6 = (f32[136,1280]{1,0:T(8,128)S(1)}, f32[136,1280]{1,0:T(8,128)S(1)}, u32[]{:S(2)}, u32[]{:S(2)}) collective-permute-start(f32[136,1280]{1,0:T(8,128)S(1)} %get-tuple-element.75), channel_id=1, source_target_pairs={{0,1},{1,0},{2,3},{3,2},{4,5},{5,4},{6,7},{7,6},{8,9},{9,8},{10,11... | collective-permute-start | bytes 2088968 | tf_op jit(solution)/shard_map/ppermute | solution.py:594
  16.2 5.2 %collective-permute-start.1 = (f32[136,1280]{1,0:T(8,128)S(1)}, f32[136,1280]{1,0:T(8,128)S(1)}, u32[]{:S(2)}, u32[]{:S(2)}) collective-permute-start(f32[136,1280]{1,0:T(8,128)S(1)} %get-tuple-element.71), channel_id=1, source_target_pairs={{0,1},{1,0},{2,3},{3,2},{4,5},{5,4},{6,7},{7,6},{8,9},{9,8},{10,11... | collective-permute-start | bytes 2088968 | tf_op jit(solution)/shard_map/ppermute | solution.py:594
  16.7 7.6 %collective-permute-start.8 = (f32[136,1280]{1,0:T(8,128)S(1)}, f32[136,1280]{1,0:T(8,128)S(1)}, u32[]{:S(2)}, u32[]{:S(2)}) collective-permute-start(f32[136,1280]{1,0:T(8,128)S(1)} %get-tuple-element.78), channel_id=1, source_target_pairs={{0,1},{1,0},{2,3},{3,2},{4,5},{5,4},{6,7},{7,6},{8,9},{9,8},{10,11... | collective-permute-start | bytes 2088968 | tf_op jit(solution)/shard_map/ppermute | solution.py:594
  16.8 9.0 %collective-permute-start.3 = (f32[136,1280]{1,0:T(8,128)S(1)}, f32[136,1280]{1,0:T(8,128)S(1)}, u32[]{:S(2)}, u32[]{:S(2)}) collective-permute-start(f32[136,1280]{1,0:T(8,128)S(1)} %get-tuple-element.74), channel_id=1, source_target_pairs={{0,1},{1,0},{2,3},{3,2},{4,5},{5,4},{6,7},{7,6},{8,9},{9,8},{10,11... | collective-permute-start | bytes 2088968 | tf_op jit(solution)/shard_map/ppermute | solution.py:594
  20.0 7.6 %copy-start.20 = (f32[136,1280]{1,0:T(8,128)}, f32[136,1280]{1,0:T(8,128)S(1)}, u32[]{:S(2)}) copy-start(f32[136,1280]{1,0:T(8,128)S(1)} %get-tuple-element.77.refs_0_) | copy-start | bytes 2088964
  20.0 7.6 %collective-permute-start.7 = (s16[144,1280]{1,0:T(8,128)(2,1)S(1)}, s16[144,1280]{1,0:T(8,128)(2,1)S(1)}, u32[]{:S(2)}, u32[]{:S(2)}) collective-permute-start(s16[144,1280]{1,0:T(8,128)(2,1)S(1)} %get-tuple-element.76), channel_id=1, source_target_pairs={{0,1},{1,3},{2,0},{3,5},{4,2},{5,7},{6,4},{7,6},{8,9},{9,11},{10,8... | collective-permute-start | bytes 1105928 | tf_op jit(solution)/shard_map/ppermute | solution.py:594
  23.0 7.0 %copy-start.22 = (f32[136,1280]{1,0:T(8,128)}, f32[136,1280]{1,0:T(8,128)S(1)}, u32[]{:S(2)}) copy-start(f32[136,1280]{1,0:T(8,128)S(1)} %get-tuple-element.73.refs_0_) | copy-start | bytes 2088964
  23.0 7.0 %collective-permute-start.2 = (s16[144,1280]{1,0:T(8,128)(2,1)S(1)}, s16[144,1280]{1,0:T(8,128)(2,1)S(1)}, u32[]{:S(2)}, u32[]{:S(2)}) collective-permute-start(s16[144,1280]{1,0:T(8,128)(2,1)S(1)} %get-tuple-element.72), channel_id=1, source_target_pairs={{0,1},{1,3},{2,0},{3,5},{4,2},{5,7},{6,4},{7,6},{8,9},{9,11},{10,8... | collective-permute-start | bytes 1105928 | tf_op jit(solution)/shard_map/ppermute | solution.py:594
  27.5 2.5 %copy-start.12 = (f32[136,1280]{1,0:T(8,128)}, f32[136,1280]{1,0:T(8,128)S(1)}, u32[]{:S(2)}) copy-start(f32[136,1280]{1,0:T(8,128)S(1)} %shard_map.148.refs_1_) | copy-start | bytes 2088964
  28.7 7.6 %collective-permute-start.9 = (s16[144,1280]{1,0:T(8,128)(2,1)}, s16[144,1280]{1,0:T(8,128)(2,1)}, u32[]{:S(2)}, u32[]{:S(2)}) collective-permute-start(s16[144,1280]{1,0:T(8,128)(2,1)} %shard_map.153), channel_id=1, source_target_pairs={{0,1},{1,3},{2,0},{3,5},{4,2},{5,7},{6,4},{7,6},{8,9},{9,11},{10,8... | collective-permute-start | bytes 1105928 | tf_op jit(solution)/shard_map/ppermute | solution.py:594
  31.1 7.9 %collective-permute-start.4 = (s16[144,1280]{1,0:T(8,128)(2,1)}, s16[144,1280]{1,0:T(8,128)(2,1)}, u32[]{:S(2)}, u32[]{:S(2)}) collective-permute-start(s16[144,1280]{1,0:T(8,128)(2,1)} %shard_map.149), channel_id=1, source_target_pairs={{0,1},{1,3},{2,0},{3,5},{4,2},{5,7},{6,4},{7,6},{8,9},{9,11},{10,8... | collective-permute-start | bytes 1105928 | tf_op jit(solution)/shard_map/ppermute | solution.py:594
  33.1 3.2 %copy-start.15 = (f32[136,1280]{1,0:T(8,128)S(1)}, f32[136,1280]{1,0:T(8,128)}, u32[]{:S(2)}) copy-start(f32[136,1280]{1,0:T(8,128)} %copy-done.14) | copy-start | bytes 2088964
  33.1 3.2 %copy-start.21 = (f32[136,1280]{1,0:T(8,128)S(1)}, f32[136,1280]{1,0:T(8,128)}, u32[]{:S(2)}) copy-start(f32[136,1280]{1,0:T(8,128)} %copy-done.20) | copy-start | bytes 2088964
  36.2 2.8 %copy-start.13 = (f32[136,1280]{1,0:T(8,128)S(1)}, f32[136,1280]{1,0:T(8,128)}, u32[]{:S(2)}) copy-start(f32[136,1280]{1,0:T(8,128)} %copy-done.12) | copy-start | bytes 2088964
  36.2 2.8 %copy-start.23 = (f32[136,1280]{1,0:T(8,128)S(1)}, f32[136,1280]{1,0:T(8,128)}, u32[]{:S(2)}) copy-start(f32[136,1280]{1,0:T(8,128)} %copy-done.22) | copy-start | bytes 2088964
  37.7 11.5 %collective-permute-start.10 = (s16[144,1280]{1,0:T(8,128)(2,1)S(1)}, s16[144,1280]{1,0:T(8,128)(2,1)S(1)}, u32[]{:S(2)}, u32[]{:S(2)}) collective-permute-start(s16[144,1280]{1,0:T(8,128)(2,1)S(1)} %shard_map.154), channel_id=1, source_target_pairs={{0,1},{1,3},{2,0},{3,5},{4,2},{5,7},{6,4},{7,6},{8,9},{9,11},{10,8... | collective-permute-start | bytes 1105928 | tf_op jit(solution)/shard_map/ppermute | solution.py:594
  40.4 9.6 %collective-permute-start.5 = (s16[144,1280]{1,0:T(8,128)(2,1)S(1)}, s16[144,1280]{1,0:T(8,128)(2,1)S(1)}, u32[]{:S(2)}, u32[]{:S(2)}) collective-permute-start(s16[144,1280]{1,0:T(8,128)(2,1)S(1)} %shard_map.150), channel_id=1, source_target_pairs={{0,1},{1,3},{2,0},{3,5},{4,2},{5,7},{6,4},{7,6},{8,9},{9,11},{10,8... | collective-permute-start | bytes 1105928 | tf_op jit(solution)/shard_map/ppermute | solution.py:594
  45.3 3.2 %copy-start.17 = (s16[144,1280]{1,0:T(8,128)(2,1)S(1)}, s16[144,1280]{1,0:T(8,128)(2,1)}, u32[]{:S(2)}) copy-start(s16[144,1280]{1,0:T(8,128)(2,1)} %copy-done.16) | copy-start | bytes 1105924
  45.3 3.3 %copy-start.19 = (s16[144,1280]{1,0:T(8,128)(2,1)S(1)}, s16[144,1280]{1,0:T(8,128)(2,1)}, u32[]{:S(2)}) copy-start(s16[144,1280]{1,0:T(8,128)(2,1)} %copy-done.18) | copy-start | bytes 1105924
  48.5 5.1 %collective-permute-start.16 = (s16[144,1280]{1,0:T(8,128)(2,1)S(1)}, s16[144,1280]{1,0:T(8,128)(2,1)S(1)}, u32[]{:S(2)}, u32[]{:S(2)}) collective-permute-start(s16[144,1280]{1,0:T(8,128)(2,1)S(1)} %copy-done.17), channel_id=1, source_target_pairs={{0,1},{1,0},{2,3},{3,2},{4,5},{5,4},{6,7},{7,6},{8,9},{9,8},{10,11... | collective-permute-start | bytes 1105928 | tf_op jit(solution)/shard_map/ppermute | solution.py:594
  48.6 14.0 %collective-permute-start.12 = (s16[144,1280]{1,0:T(8,128)(2,1)S(1)}, s16[144,1280]{1,0:T(8,128)(2,1)S(1)}, u32[]{:S(2)}, u32[]{:S(2)}) collective-permute-start(s16[144,1280]{1,0:T(8,128)(2,1)S(1)} %copy-done.19), channel_id=1, source_target_pairs={{0,1},{1,0},{2,3},{3,2},{4,5},{5,4},{6,7},{7,6},{8,9},{9,8},{10,11... | collective-permute-start | bytes 1105928 | tf_op jit(solution)/shard_map/ppermute | solution.py:594
  49.1 5.8 %collective-permute-start.17 = (s16[144,1280]{1,0:T(8,128)(2,1)}, s16[144,1280]{1,0:T(8,128)(2,1)S(1)}, u32[]{:S(2)}, u32[]{:S(2)}) collective-permute-start(s16[144,1280]{1,0:T(8,128)(2,1)} %collective-permute-done.9.previous_ref.refs_1_.refs_0_), channel_id=1, source_target_pairs={{0,1},{1,0},{2,3},{3,2},{4,5},{5,4},{6,7},{7,6},{8,9},{9,8},{10,11... | collective-permute-start | bytes 1105928 | tf_op jit(solution)/shard_map/ppermute | solution.py:594
  49.2 7.3 %collective-permute-start.18 = (s16[144,1280]{1,0:T(8,128)(2,1)S(1)}, s16[144,1280]{1,0:T(8,128)(2,1)S(1)}, u32[]{:S(2)}, u32[]{:S(2)}) collective-permute-start(s16[144,1280]{1,0:T(8,128)(2,1)S(1)} %collective-permute-done.10.previous_ref.refs_2_.refs_1_), channel_id=1, source_target_pairs={{0,1},{1,0},{2,3},{3,2},{4,5},{5,4},{6,7},{7,6},{8,9},{9,8},{10,11... | collective-permute-start | bytes 1105928 | tf_op jit(solution)/shard_map/ppermute | solution.py:594
  50.0 12.6 %collective-permute-start.13 = (s16[144,1280]{1,0:T(8,128)(2,1)}, s16[144,1280]{1,0:T(8,128)(2,1)S(1)}, u32[]{:S(2)}, u32[]{:S(2)}) collective-permute-start(s16[144,1280]{1,0:T(8,128)(2,1)} %collective-permute-done.4.previous_ref.refs_1_.refs_0_), channel_id=1, source_target_pairs={{0,1},{1,0},{2,3},{3,2},{4,5},{5,4},{6,7},{7,6},{8,9},{9,8},{10,11... | collective-permute-start | bytes 1105928 | tf_op jit(solution)/shard_map/ppermute | solution.py:594
  50.5 6.0 %copy-start.5 = (f32[136,1280]{1,0:T(8,128)S(1)}, f32[136,1280]{1,0:T(8,128)}, u32[]{:S(2)}) copy-start(f32[136,1280]{1,0:T(8,128)} %copy-done.4) | copy-start | bytes 2088964
  53.6 8.5 %collective-permute-start.15 = (s16[144,1280]{1,0:T(8,128)(2,1)S(1)}, s16[144,1280]{1,0:T(8,128)(2,1)S(1)}, u32[]{:S(2)}, u32[]{:S(2)}) collective-permute-start(s16[144,1280]{1,0:T(8,128)(2,1)S(1)} %shard_map.155), channel_id=1, source_target_pairs={{0,1},{1,3},{2,0},{3,5},{4,2},{5,7},{6,4},{7,6},{8,9},{9,11},{10,8... | collective-permute-start | bytes 1105928 | tf_op jit(solution)/shard_map/ppermute | solution.py:594
  54.9 13.2 %collective-permute-start.11 = (s16[144,1280]{1,0:T(8,128)(2,1)S(1)}, s16[144,1280]{1,0:T(8,128)(2,1)S(1)}, u32[]{:S(2)}, u32[]{:S(2)}) collective-permute-start(s16[144,1280]{1,0:T(8,128)(2,1)S(1)} %shard_map.156), channel_id=1, source_target_pairs={{0,1},{1,3},{2,0},{3,5},{4,2},{5,7},{6,4},{7,6},{8,9},{9,11},{10,8... | collective-permute-start | bytes 1105928 | tf_op jit(solution)/shard_map/ppermute | solution.py:594
  56.5 6.1 %collective-permute-start.14 = (s16[144,1280]{1,0:T(8,128)(2,1)S(1)}, s16[144,1280]{1,0:T(8,128)(2,1)S(1)}, u32[]{:S(2)}, u32[]{:S(2)}) collective-permute-start(s16[144,1280]{1,0:T(8,128)(2,1)S(1)} %collective-permute-done.5.previous_ref.refs_2_.refs_1_), channel_id=1, source_target_pairs={{0,1},{1,0},{2,3},{3,2},{4,5},{5,4},{6,7},{7,6},{8,9},{9,8},{10,11... | collective-permute-start | bytes 1105928 | tf_op jit(solution)/shard_map/ppermute | solution.py:594
  56.5 6.1 %copy-start.11 = (f32[136,1280]{1,0:T(8,128)S(1)}, f32[136,1280]{1,0:T(8,128)}, u32[]{:S(2)}) copy-start(f32[136,1280]{1,0:T(8,128)} %copy-done.10) | copy-start | bytes 2088964
  62.0 6.1 %collective-permute-start.20 = (s16[144,1280]{1,0:T(8,128)(2,1)S(1)}, s16[144,1280]{1,0:T(8,128)(2,1)S(1)}, u32[]{:S(2)}, u32[]{:S(2)}) collective-permute-start(s16[144,1280]{1,0:T(8,128)(2,1)S(1)} %collective-permute-done.15.refs_2_), channel_id=1, source_target_pairs={{0,1},{1,0},{2,3},{3,2},{4,5},{5,4},{6,7},{7,6},{8,9},{9,8},{10,11... | collective-permute-start | bytes 1105928 | tf_op jit(solution)/shard_map/ppermute | solution.py:594
  62.6 5.6 %copy-start.9 = (f32[136,1280]{1,0:T(8,128)S(1)}, f32[136,1280]{1,0:T(8,128)}, u32[]{:S(2)}) copy-start(f32[136,1280]{1,0:T(8,128)} %copy-done.8) | copy-start | bytes 2088964
  68.1 5.5 %collective-permute-start.19 = (s16[144,1280]{1,0:T(8,128)(2,1)S(1)}, s16[144,1280]{1,0:T(8,128)(2,1)S(1)}, u32[]{:S(2)}, u32[]{:S(2)}) collective-permute-start(s16[144,1280]{1,0:T(8,128)(2,1)S(1)} %collective-permute-done.11.refs_2_), channel_id=1, source_target_pairs={{0,1},{1,0},{2,3},{3,2},{4,5},{5,4},{6,7},{7,6},{8,9},{9,8},{10,11... | collective-permute-start | bytes 1105928 | tf_op jit(solution)/shard_map/ppermute | solution.py:594
  68.2 5.4 %copy-start.7 = (f32[136,1280]{1,0:T(8,128)S(1)}, f32[136,1280]{1,0:T(8,128)}, u32[]{:S(2)}) copy-start(f32[136,1280]{1,0:T(8,128)} %copy-done.6) | copy-start | bytes 2088964
  79.0 16.4 %copy-start.29 = (s32[128]{0:T(128)S(1)}, s32[128]{0:T(128)}, u32[]{:S(2)}) copy-start(s32[128]{0:T(128)} %param.10) | copy-start | bytes 1540
  81.3 1.4 %collective-permute-start.21 = (f32[8,1792]{1,0:T(8,128)S(1)}, f32[8,1792]{1,0:T(8,128)S(1)}, u32[]{:S(2)}, u32[]{:S(2)}) collective-permute-start(f32[8,1792]{1,0:T(8,128)S(1)} %slice_select_fusion), channel_id=1, source_target_pairs={{0,1},{1,0},{2,3},{3,2},{4,5},{5,4},{6,7},{7,6},{8,9},{9,8},{10,11... | collective-permute-start | bytes 172040 | tf_op jit(solution)/shard_map/ppermute | solution.py:594
  82.7 5.8 %collective-permute-start.22 = (f32[8,1792]{1,0:T(8,128)S(1)}, f32[8,1792]{1,0:T(8,128)S(1)}, u32[]{:S(2)}, u32[]{:S(2)}) collective-permute-start(f32[8,1792]{1,0:T(8,128)S(1)} %select_add_fusion), channel_id=1, source_target_pairs={{0,8},{8,0},{16,24},{24,16},{1,9},{9,1},{17,25},{25,17},{2,10},{10... | collective-permute-start | bytes 172040 | tf_op jit(solution)/shard_map/ppermute | solution.py:594
  84.0 4.6 %collective-permute-start.23 = (f32[8,1792]{1,0:T(8,128)S(1)}, f32[8,1792]{1,0:T(8,128)S(1)}, u32[]{:S(2)}, u32[]{:S(2)}) collective-permute-start(f32[8,1792]{1,0:T(8,128)S(1)} %select_add_fusion), channel_id=1, source_target_pairs={{0,16},{8,24},{16,0},{24,8},{1,17},{9,25},{17,1},{25,9},{2,18},{10... | collective-permute-start | bytes 172040 | tf_op jit(solution)/shard_map/ppermute | solution.py:594
  85.2 3.9 %collective-permute-start.24 = (f32[8,1792]{1,0:T(8,128)S(1)}, f32[8,1792]{1,0:T(8,128)S(1)}, u32[]{:S(2)}, u32[]{:S(2)}) collective-permute-start(f32[8,1792]{1,0:T(8,128)S(1)} %select_add_fusion), channel_id=1, source_target_pairs={{0,24},{8,16},{16,8},{24,0},{1,25},{9,17},{17,9},{25,1},{2,26},{10... | collective-permute-start | bytes 172040 | tf_op jit(solution)/shard_map/ppermute | solution.py:594
  85.4 6.4 %collective-permute-start.25 = (f32[3,5376]{1,0:T(4,128)S(1)}, f32[3,5376]{1,0:T(4,128)S(1)}, u32[]{:S(2)}, u32[]{:S(2)}) collective-permute-start(f32[3,5376]{1,0:T(4,128)S(1)} %slice.38), channel_id=1, source_target_pairs={{1,0},{2,1},{3,2},{4,3},{5,4},{6,5},{7,6},{9,8},{10,9},{11,10},{12... | collective-permute-start | bytes 193544 | tf_op jit(solution)/shard_map/ppermute | solution.py:791
  91.9 5.3 %collective-permute-start.26 = (f32[8,1792]{1,0:T(8,128)S(1)}, f32[8,1792]{1,0:T(8,128)S(1)}, u32[]{:S(2)}, u32[]{:S(2)}) collective-permute-start(f32[8,1792]{1,0:T(8,128)S(1)} %add_add_fusion.1), channel_id=1, source_target_pairs={{0,2},{1,3},{2,0},{3,1},{4,6},{5,7},{6,4},{7,5},{8,10},{9,11},{10,... | collective-permute-start | bytes 172040 | tf_op jit(solution)/shard_map/ppermute | solution.py:594
  92.5 4.7 %collective-permute-start.27 = (f32[8,1792]{1,0:T(8,128)S(1)}, f32[8,1792]{1,0:T(8,128)S(1)}, u32[]{:S(2)}, u32[]{:S(2)}) collective-permute-start(f32[8,1792]{1,0:T(8,128)S(1)} %add_add_fusion.1), channel_id=1, source_target_pairs={{0,4},{1,5},{2,6},{3,7},{4,0},{5,1},{6,2},{7,3},{8,12},{9,13},{10,... | collective-permute-start | bytes 172040 | tf_op jit(solution)/shard_map/ppermute | solution.py:594
  92.5 6.1 %collective-permute-start.28 = (f32[8,1792]{1,0:T(8,128)S(1)}, f32[8,1792]{1,0:T(8,128)S(1)}, u32[]{:S(2)}, u32[]{:S(2)}) collective-permute-start(f32[8,1792]{1,0:T(8,128)S(1)} %add_add_fusion.1), channel_id=1, source_target_pairs={{0,6},{1,7},{2,4},{3,5},{4,2},{5,3},{6,0},{7,1},{8,14},{9,15},{10,... | collective-permute-start | bytes 172040 | tf_op jit(solution)/shard_map/ppermute | solution.py:594
  98.7 3.1 %collective-permute-start.29 = (f32[8,1792]{1,0:T(8,128)S(1)}, f32[8,1792]{1,0:T(8,128)S(1)}, u32[]{:S(2)}, u32[]{:S(2)}) collective-permute-start(f32[8,1792]{1,0:T(8,128)S(1)} %broadcast_multiply_fusion), channel_id=1, source_target_pairs={{0,1},{1,0},{2,3},{3,2},{4,5},{5,4},{6,7},{7,6},{8,9},{9,8},{10,11... | collective-permute-start | bytes 172040 | tf_op jit(solution)/shard_map/ppermute | solution.py:594
  (13 other events, 17.9 us)
